TPU v7x, 32 devices: a whole 2x2x4 slice. The times are simulated.
32 devices in a mesh: kv: 2 (over y), blk: 16 (over z, x, core).
Axes of the slice: x: 2, y: 2, z: 4, core: 2. Of those that a mesh axis runs over, the one named last changes fastest.
Arguments:
- hidden_in: bfloat16 [8192, 1280], P('blk'), may hold values from -6 to 6
- w_query: bfloat16 [1280, 1280], P(None, 'kv'), may hold values from -0.15625 to 0.15625
- w_key: bfloat16 [1280, 1280], P(None, 'kv'), may hold values from -0.15625 to 0.15625
- w_value: bfloat16 [1280, 1280], P(None, 'kv'), may hold values from -0.15625 to 0.15625
- w_out: bfloat16 [1280, 1280], P('kv'), may hold values from -0.15625 to 0.15625
- head_gain: float32 [1280], P('kv'), may hold values from 1 to 2.5
- eigen_rate: float32 [1280], replicated, may hold values from 0.15 to 0.6
- pool_keys: bfloat16 [64, 256, 1280], P('blk', None, 'kv'), may hold values from -2 to 2
- pool_values: bfloat16 [64, 256, 1280], P('blk', None, 'kv'), may hold values from -6 to 6
- req_len: int32 [16], P('blk'), may hold values from 1 to 512, as said below
- prefix_len: int32 [16], P('blk'), may hold values from 0 to 4, as said below
- prefix_pages: int32 [16, 4], replicated, may hold values from 0 to 63, as said below
- placement: int32 [32], replicated, may hold values from 0 to 31, as said below
Outputs:
- layer_out: bfloat16 [8192, 1280], P('blk')
- new_keys: bfloat16 [32, 256, 1280], P('blk', None, 'kv')
- new_values: bfloat16 [32, 256, 1280], P('blk', None, 'kv')
Inputs may be any that keep to these rules, and one draw needn't show every extreme that they name: `req_len`: some request has all 512 tokens live. `prefix_len`: some request has 4 cached pages. Page prefix_pages[r, s] lies among pages h * 4 to (h + 1) * 4 - 1 with h = (r + 1 + s * 4) mod 16, for every slot s. Each page once; placement[b] lies among pages e * 2 to (e + 1) * 2 - 1 with e = (b // 2 + (2 * (b mod 2) + 1) * 4) mod 16.
All inputs are finite; a program needn't handle non-finite values.
Results may differ from a plain program's by a relative error of at most 0.0067.
Values may be sent and summed in bfloat16 or wider, within the bound.
No kernel may reach another device: no remote copies, remote signals or barrier semaphores. Data moves between devices by JAX's collectives and lax.ppermute only.
A program may use at most 128 MiB of HBM per device.

v0:
```python
import functools
import math

import jax
import jax.numpy as jnp
from jax import lax
from jax.experimental import pallas as pl
from jax.experimental.pallas import tpu as pltpu
from jax.sharding import PartitionSpec as P

HD = 64
PAGE = 256
PMAX = 4
LANES = 128
GROUPS = (256, 384)
UNITS = ((256,), (128, 128, 128))
WINDOW = 4
SLOT_ORDER = (2, 1, 3, 0)
VMEM_LIMIT = 16 * 1024 * 1024
FIRST_LIMIT = 58 * 1024 * 1024

epsilon = 1e-06

f32 = jnp.float32
bf16 = jnp.bfloat16


def from_behind(block, axis, distance):
    devices = range(lax.axis_size(axis))
    route = [((i - distance) % len(devices), i) for i in devices]
    return lax.ppermute(block, axis, route)


def over_blk(block, distances):
    devices = lax.axis_size("blk")
    route = []
    for kv in range(lax.axis_size("kv")):
        for i in range(devices):
            route.append((kv * devices + (i - distances[kv]) % devices, kv * devices + i))
    return lax.ppermute(block, ("kv", "blk"), route)


def after(block, *others):
    return lax.optimization_barrier((block, *others))[0]


def group_slices(width):
    slices, start = [], 0
    for size in GROUPS:
        slices.append((start, size))
        start += size
    assert start == width
    return slices


def unit_slices():
    units, base = [], 0
    for g, sizes in enumerate(UNITS):
        inner = 0
        for size in sizes:
            units.append((g, inner, base + inner, size))
            inner += size
        base += inner
    return units


def params(limit=VMEM_LIMIT):
    return pltpu.CompilerParams(vmem_limit_bytes=limit)


def cost():
    return pl.CostEstimate(flops=1, bytes_accessed=1, transcendentals=0)


def split_kernel(kv_ref, hidden, out, sem):
    rows = pl.ds(pl.multiple_of(kv_ref[0] * PAGE, PAGE), PAGE)
    copy = pltpu.make_async_copy(hidden.at[rows], out, sem)
    copy.start()
    copy.wait()


def split_rows(hidden_in, kv_index):
    return pl.pallas_call(
        split_kernel,
        in_specs=[pl.BlockSpec(memory_space=pltpu.SMEM), pl.BlockSpec(memory_space=pltpu.HBM)],
        out_specs=pl.BlockSpec(memory_space=pltpu.VMEM),
        out_shape=jax.ShapeDtypeStruct((PAGE, hidden_in.shape[1]), bf16),
        scratch_shapes=[pltpu.SemaphoreType.DMA],
        compiler_params=params(FIRST_LIMIT),
        cost_estimate=cost(),
        name="split_rows",
    )(kv_index, hidden_in)


def pack_kernel(slices, devices, offsets, here_ref, table, keys, values, _, *rest):
    outs, (buf, sem) = rest[:-2], rest[-2:]
    copies = []
    for slot in range(PMAX):
        asker = lax.rem(here_ref[0] + (devices - offsets[slot]), devices)
        local = lax.rem(table[slot, asker], keys.shape[0])
        for side, pool in enumerate((keys, values)):
            index = 2 * slot + side
            copies.append(pltpu.make_async_copy(pool.at[local], buf.at[index], sem.at[index]))
    for copy in copies:
        copy.start()
    for slot in range(PMAX):
        for side in range(2):
            index = 2 * slot + side
            copies[index].wait()
            for g, (start, size) in enumerate(slices):
                outs[g * PMAX + slot][side] = buf[index, :, start : start + size]


def pack(pool_keys, pool_values, table, here, devices, offsets, first):
    width = pool_keys.shape[2]
    slices = group_slices(width)
    outs = []
    for _, size in slices:
        outs += [jax.ShapeDtypeStruct((2, PAGE, size), bf16)] * PMAX
    smem = pl.BlockSpec(memory_space=pltpu.SMEM)
    hbm = pl.BlockSpec(memory_space=pltpu.HBM)
    result = pl.pallas_call(
        functools.partial(pack_kernel, slices, devices, offsets),
        in_specs=[smem, smem, hbm, hbm, pl.BlockSpec(memory_space=pl.ANY)],
        out_specs=[pl.BlockSpec(memory_space=pltpu.VMEM)] * len(outs),
        out_shape=outs,
        scratch_shapes=[
            pltpu.VMEM((2 * PMAX, PAGE, width), bf16),
            pltpu.SemaphoreType.DMA((2 * PMAX,)),
        ],
        compiler_params=params(FIRST_LIMIT),
        cost_estimate=cost(),
        name="pack",
    )(here, table, pool_keys, pool_values, first)
    return [result[PMAX * g : PMAX * (g + 1)] for g in range(len(slices))]


def head_sum_matrix():
    rows = (lax.broadcasted_iota(jnp.int32, (2 * LANES, LANES), 0) % LANES) // HD
    cols = lax.broadcasted_iota(jnp.int32, (2 * LANES, LANES), 1) // HD
    return jnp.where(rows == cols, 1.0 / HD, 0.0).astype(bf16)


def head_norm(projected, gain, matrix):
    parts = []
    for start in range(0, projected.shape[1], LANES):
        part = projected[:, start : start + LANES]
        squares = part * part
        high = squares.astype(bf16)
        low = (squares - high.astype(f32)).astype(bf16)
        both = jnp.concatenate([high, low], axis=1)
        mean = jnp.dot(both, matrix, preferred_element_type=f32)
        parts.append(part * lax.rsqrt(mean + epsilon) * gain[:, start : start + LANES])
    return jnp.concatenate(parts, axis=1) if len(parts) > 1 else parts[0]


def row_scale_of(hidden):
    hidden_f = hidden.astype(f32)
    return lax.rsqrt(jnp.mean(hidden_f * hidden_f, axis=-1, keepdims=True) + epsilon)


def project_kernel(slices, hidden, wq, wk, wv, gain, *outs):
    matrix = head_sum_matrix()
    rows_all = hidden.shape[0]
    for low in range(0, rows_all, PAGE):
        rows = slice(low, low + PAGE)
        x = hidden[rows, :]
        scale = row_scale_of(x)
        for g, (start, size) in enumerate(slices):
            cols = slice(start, start + size)
            q = jnp.dot(x, wq[:, cols], preferred_element_type=f32)
            q = head_norm(q, gain[:, cols], matrix).astype(bf16)
            outs[3 * g][rows, :] = q * jnp.asarray(1.0 / math.sqrt(HD), bf16)
            k = jnp.dot(x, wk[:, cols], preferred_element_type=f32)
            outs[3 * g + 1][rows, :] = head_norm(k, gain[:, cols], matrix).astype(bf16)
            v = jnp.dot(x, wv[:, cols], preferred_element_type=f32)
            outs[3 * g + 2][rows, :] = (v * scale).astype(bf16)


def project(hidden_in, wq, wk, wv, gain):
    tokens, depth = hidden_in.shape
    width = wq.shape[1]
    slices = [(start, size) for _, _, start, size in unit_slices()]
    outs = []
    for _, size in slices:
        outs += [jax.ShapeDtypeStruct((tokens, size), bf16)] * 3
    flat = pl.pallas_call(
        functools.partial(project_kernel, slices),
        out_shape=outs,
        compiler_params=params(),
        cost_estimate=cost(),
        name="project",
    )(hidden_in, wq, wk, wv, gain)
    return [flat[3 * g : 3 * g + 3] for g in range(len(slices))]


def relay_kernel(slices, blocks, devices, offsets, kv_ref, here_ref, placement, *refs):
    mine, theirs, wk, wv, gain, key_out, value_out = refs
    matrix = head_sum_matrix()
    for rows_ref, block in ((mine, kv_ref[0]), (theirs, 1 - kv_ref[0])):
        x = rows_ref[...]
        scale = row_scale_of(x)
        offset = jnp.where(block == 0, offsets[0], offsets[1])
        source = lax.rem(here_ref[0] + (devices - offset), devices)
        slot = lax.rem(placement[source * blocks + block], blocks)
        for start, size in slices:
            cols = slice(start, start + size)
            k = jnp.dot(x, wk[:, cols], preferred_element_type=f32)
            key_out[slot, :, cols] = head_norm(k, gain[:, cols], matrix).astype(bf16)
            v = jnp.dot(x, wv[:, cols], preferred_element_type=f32)
            value_out[slot, :, cols] = (v * scale).astype(bf16)


def relay_project(mine, theirs, wk, wv, gain, kv_index, here, placement, offsets):
    blocks = len(offsets)
    depth, width = wk.shape
    out = jax.ShapeDtypeStruct((blocks, PAGE, width), bf16)
    smem = pl.BlockSpec(memory_space=pltpu.SMEM)
    vmem = pl.BlockSpec(memory_space=pltpu.VMEM)
    return pl.pallas_call(
        functools.partial(
            relay_kernel, group_slices(width), blocks, lax.axis_size("blk"), offsets
        ),
        in_specs=[smem] * 3 + [vmem] * 5,
        out_specs=[vmem, vmem],
        out_shape=[out, out],
        compiler_params=params(),
        cost_estimate=cost(),
        name="relay_project",
    )(kv_index, here, placement, mine, theirs, wk, wv, gain)


def attend_kernel(inner, live_ref, depth_ref, q_ref, k_ref, v_ref, p0, p1, p2, p3, out):
    pages = (p0, p1, p2, p3)
    tokens, width = q_ref.shape
    live, depth = live_ref[0], depth_ref[0]
    lane = lax.broadcasted_iota(jnp.int32, (1, LANES), 1)
    row = lax.broadcasted_iota(jnp.int32, (PAGE, PAGE), 0)
    col = lax.broadcasted_iota(jnp.int32, (PAGE, PAGE), 1)
    causal = col <= row
    key_row = lax.broadcasted_iota(jnp.int32, (PAGE, LANES), 0)
    blocks = tokens // PAGE
    for start in range(0, width, LANES):
        cols = slice(start, start + LANES)
        page_cols = slice(inner + start, inner + start + LANES)
        keys, values = [], []
        for b in range(blocks):
            rows = slice(b * PAGE, (b + 1) * PAGE)
            keep = (key_row + b * PAGE) < live
            keys.append(k_ref[rows, cols])
            shown = jnp.where(keep, v_ref[rows, cols].astype(f32), 0.0).astype(bf16)
            ones = jnp.where(keep, 1.0, 0.0).astype(bf16)
            values.append(jnp.concatenate([shown, ones], axis=1))
        for p in range(PMAX):
            keep = jnp.where(p < depth, 1.0, 0.0).astype(bf16)
            keys.append(pages[p][0, :, page_cols])
            ones = jnp.full((PAGE, LANES), 1.0, bf16) * keep
            values.append(jnp.concatenate([pages[p][1, :, page_cols] * keep, ones], axis=1))
        for b in range(blocks):
            rows = slice(b * PAGE, (b + 1) * PAGE)
            q = q_ref[rows, cols]
            ratios = []
            for side in range(2):
                q_side = jnp.where((lane // HD) == side, q, jnp.zeros_like(q))
                acc = jnp.zeros((PAGE, 2 * LANES), f32)
                for j in list(range(b + 1)) + list(range(blocks, blocks + PMAX)):
                    scores = lax.dot_general(
                        q_side, keys[j], (((1,), (1,)), ((), ())), preferred_element_type=f32
                    )
                    weights = jnp.exp(scores)
                    if j == b:
                        weights = jnp.where(causal, weights, 0.0)
                    acc += jnp.dot(weights.astype(bf16), values[j], preferred_element_type=f32)
                ratios.append(acc[:, :LANES] / acc[:, LANES:])
            out[rows, cols] = jnp.where((lane // HD) == 0, ratios[0], ratios[1]).astype(bf16)


def attend(live, depth, q, k, v, pages, inner):
    tokens, width = q.shape
    heads = width // HD
    smem = pl.BlockSpec(memory_space=pltpu.SMEM)
    vmem = pl.BlockSpec(memory_space=pltpu.VMEM)
    keys = tokens + PMAX * PAGE
    return pl.pallas_call(
        functools.partial(attend_kernel, inner),
        in_specs=[smem, smem] + [vmem] * 7,
        out_specs=vmem,
        out_shape=jax.ShapeDtypeStruct((tokens, width), bf16),
        compiler_params=params(),
        cost_estimate=cost(),
        name="attend",
    )(live, depth, q, k, v, *pages)


def finish_kernel(slices, count, *refs):
    hidden, w_mine, w_theirs, rate = refs[:4]
    mine = refs[4 : 4 + count]
    theirs = refs[4 + count : 4 + 2 * count]
    out = refs[4 + 2 * count]

    def half(parts, weights):
        total = None
        for part, (start, size) in zip(parts, slices):
            term = jnp.dot(part[...], weights[start : start + size, :], preferred_element_type=f32)
            total = term if total is None else total + term
        return total

    branch = half(mine, w_mine) + half(theirs, w_theirs)
    hidden_f = hidden[...].astype(f32)
    anchor = hidden_f * lax.rsqrt(jnp.mean(hidden_f * hidden_f, axis=-1, keepdims=True) + epsilon)
    normed = branch * lax.rsqrt(jnp.mean(branch * branch, axis=-1, keepdims=True) + epsilon)
    updated = anchor + rate[...] * (normed - anchor)
    scale = lax.rsqrt(jnp.mean(updated * updated, axis=-1, keepdims=True) + epsilon)
    out[...] = (updated * scale).astype(bf16)


def finish(hidden_in, w_mine, w_theirs, rate, mine, theirs):
    tokens, depth = hidden_in.shape
    width = w_mine.shape[0]
    slices = [(start, size) for _, _, start, size in unit_slices()]
    step = 256
    by_rows = lambda size: pl.BlockSpec((step, size), lambda i: (i, 0))
    whole = lambda shape: pl.BlockSpec(shape, lambda i: (0, 0))
    return pl.pallas_call(
        functools.partial(finish_kernel, slices, len(slices)),
        grid=(tokens // step,),
        in_specs=[by_rows(depth), whole(w_mine.shape), whole(w_theirs.shape), whole(rate.shape)]
        + [by_rows(size) for _, size in slices] * 2,
        out_specs=by_rows(depth),
        out_shape=jax.ShapeDtypeStruct((tokens, depth), bf16),
        compiler_params=params(),
        cost_estimate=cost(),
        name="finish",
    )(hidden_in, w_mine, w_theirs, rate, *mine, *theirs)


def body(
    hidden_in,
    w_query,
    w_key,
    w_value,
    w_out,
    head_gain,
    eigen_rate,
    pool_keys,
    pool_values,
    req_len,
    prefix_len,
    prefix_pages,
    placement,
):
    devices = lax.axis_size("blk")
    here = lax.axis_index("blk").astype(jnp.int32).reshape(1)
    kv_index = lax.axis_index("kv").astype(jnp.int32).reshape(1)
    blocks = hidden_in.shape[0] // PAGE
    gain = head_gain.reshape(1, -1)
    rate = eigen_rate.reshape(1, -1)
    page_offsets = [slot * devices // PMAX + 1 for slot in range(PMAX)]
    block_offsets = [(2 * b + 1) * devices // (2 * blocks) for b in range(blocks)]

    assert blocks == lax.axis_size("kv") == 2
    relay_send = split_rows(hidden_in, kv_index)
    page_send = pack(
        pool_keys, pool_values, prefix_pages.T, here, devices, page_offsets, relay_send
    )

    projected = project(hidden_in, w_query, w_key, w_value, gain)

    sends = [(relay_send, block_offsets)]
    for sent in page_send:
        sends += [(sent[slot], [devices - page_offsets[slot]] * 2) for slot in SLOT_ORDER]
    arrived = []
    for index, (block, distance) in enumerate(sends):
        if index >= WINDOW:
            block = after(block, projected[0][0], *arrived[: index - WINDOW + 1])
        arrived.append(over_blk(block, distance))
    relay_mine = arrived[0]
    pages = []
    for g in range(len(page_send)):
        first = 1 + g * PMAX
        got = dict(zip(SLOT_ORDER, arrived[first : first + PMAX]))
        pages.append([got[slot] for slot in range(PMAX)])
    w_theirs = from_behind(after(w_out, page_send[0][2]), "kv", 1)
    first_pages = arrived[1 : 1 + PMAX]
    relay_theirs = from_behind(after(relay_mine, w_theirs, *first_pages), "kv", 1)
    new_keys, new_values = relay_project(
        relay_mine, relay_theirs, w_key, w_value, gain, kv_index, here, placement, block_offsets
    )

    mine, theirs = [], []
    for (g, inner, _, _), (q, k, v) in zip(unit_slices(), projected):
        q = after(q, new_keys, theirs[0]) if g else q
        attended = attend(req_len, prefix_len, q, k, v, pages[g], inner)
        mine.append(attended)
        theirs.append(from_behind(attended, "kv", 1))
    layer_out = finish(hidden_in, w_out, w_theirs, rate, mine, theirs)
    return (layer_out, new_keys, new_values)


def solution(mesh):
    in_specs = (
        P("blk", None),
        P(None, "kv"),
        P(None, "kv"),
        P(None, "kv"),
        P("kv", None),
        P("kv"),
        P(),
        P("blk", None, "kv"),
        P("blk", None, "kv"),
        P("blk"),
        P("blk"),
        P(),
        P(),
    )
    out_specs = (P("blk", None), P("blk", None, "kv"), P("blk", None, "kv"))
    return jax.shard_map(body, mesh=mesh, in_specs=in_specs, out_specs=out_specs, check_vma=False)
```

profile of v0, /device:TPU:0, one launch (start us, length us, event | category | flops | bytes accessed | tf_op | source)
XLA Modules:
  0.0 106.9 jit_solution(7334955522006045476)
XLA Ops:
  0.6 2.1 %split_rows.1._ = bf16[256,1280]{1,0:T(8,128)(2,1)} custom-call(s32[1]{0:T(128)} %bitcast.2.kv_ref, bf16[512,1280]{1,0:T(8,128)(2,1)} %refs_0_.1), custom_call_target="tpu_custom_call" | custom-call | flops 1 | bytes 1 | tf_op jit(solution)/shard_map/split_rows/pallas_call | solution.py:83
  2.7 4.2 %pack.1 = (bf16[2,256,256]{2,1,0:T(8,128)(2,1)}, bf16[2,256,256]{2,1,0:T(8,128)(2,1)}, bf16[2,256,256]{2,1,0:T(8,128)(2,1)}, bf16[2,256,256]{2,1,0:T(8,128)(2,1)...) custom-call(s32[1]{0:T(128)} %bitcast.here_ref, ...), custom_call_target="tpu_custom_call" | custom-call | flops 1 | bytes 1 | tf_op jit(solution)/shard_map/pack/pallas_call | solution.py:122
  6.9 3.0 %collective-permute-start = (bf16[640,1280]{1,0:T(8,128)(2,1)}, bf16[640,1280]{1,0:T(8,128)(2,1)S(1)}, u32[]{:S(2)}, u32[]{:S(2)}) collective-permute-start(bf16[640,1280]{1,0:T(8,128)(2,1)} %refs_1_.1), channel_id=1, source_target_pairs={{16,0},{0,16},{17,1},{1,17},{18,2},{2,18},{19,3},{3,19},{20,4},{4,... | collective-permute-start | bytes 4915208 | tf_op jit(solution)/shard_map/ppermute | solution.py:31
  9.9 1.6 %collective-permute-start.1 = (bf16[256,1280]{1,0:T(8,128)(2,1)}, bf16[256,1280]{1,0:T(8,128)(2,1)S(1)}, u32[]{:S(2)}, u32[]{:S(2)}) collective-permute-start(bf16[256,1280]{1,0:T(8,128)(2,1)} %split_rows.1._), channel_id=1, source_target_pairs={{12,0},{13,1},{14,2},{15,3},{0,4},{1,5},{2,6},{3,7},{4,8},{5,9},{6... | collective-permute-start | bytes 1966088 | tf_op jit(solution)/shard_map/ppermute | solution.py:40
  12.9 2.1 %collective-permute-start.3 = (bf16[2,256,256]{2,1,0:T(8,128)(2,1)}, bf16[2,256,256]{2,1,0:T(8,128)(2,1)S(1)}, u32[]{:S(2)}, u32[]{:S(2)}) collective-permute-start(bf16[2,256,256]{2,1,0:T(8,128)(2,1)} %get-tuple-element.42), channel_id=1, source_target_pairs={{5,0},{6,1},{7,2},{8,3},{9,4},{10,5},{11,6},{12,7},{13,8},{14,9},{... | collective-permute-start | bytes 786440 | tf_op jit(solution)/shard_map/ppermute | solution.py:40
  15.6 1.4 %copy-done.4 = bf16[1280,640]{1,0:T(8,128)(2,1)S(1)} copy-done((bf16[1280,640]{1,0:T(8,128)(2,1)S(1)}, bf16[1280,640]{1,0:T(8,128)(2,1)}, u32[]{:S(2)}) %copy-start.4) | copy-done | bytes 1638424
  17.0 6.9 %project.1 = (bf16[512,256]{1,0:T(8,128)(2,1)S(1)}, bf16[512,256]{1,0:T(8,128)(2,1)S(1)}, bf16[512,256]{1,0:T(8,128)(2,1)S(1)}, bf16[512,128]{1,0:T(8,128)(2,1)S...) custom-call(bf16[512,1280]{1,0:T(8,128)(2,1)S(1)} %copy-done, ...), custom_call_target="tpu_custom_call" | custom-call | flops 1 | bytes 1 | tf_op jit(solution)/shard_map/project/pallas_call | solution.py:187
  24.0 5.8 %collective-permute-done.1.refs_0_ = bf16[256,1280]{1,0:T(8,128)(2,1)S(1)} collective-permute-done((bf16[256,1280]{1,0:T(8,128)(2,1)}, bf16[256,1280]{1,0:T(8,128)(2,1)S(1)}, u32[]{:S(2)}, u32[]{:S(2)}) %collective-permute-start.1) | collective-permute-done | bytes 655392 | tf_op jit(solution)/shard_map/ppermute | solution.py:40
  29.8 8.6 %collective-permute-done.3.p1 = bf16[2,256,256]{2,1,0:T(8,128)(2,1)S(1)} collective-permute-done((bf16[2,256,256]{2,1,0:T(8,128)(2,1)}, bf16[2,256,256]{2,1,0:T(8,128)(2,1)S(1)}, u32[]{:S(2)}, u32[]{:S(2)}) %collective-permute-start.3) | collective-permute-done | bytes 262176 | tf_op jit(solution)/shard_map/ppermute | solution.py:40
  38.4 5.5 %collective-permute-done.5.p3 = bf16[2,256,256]{2,1,0:T(8,128)(2,1)S(1)} collective-permute-done((bf16[2,256,256]{2,1,0:T(8,128)(2,1)}, bf16[2,256,256]{2,1,0:T(8,128)(2,1)S(1)}, u32[]{:S(2)}, u32[]{:S(2)}) %collective-permute-start.5) | collective-permute-done | bytes 262176 | tf_op jit(solution)/shard_map/ppermute | solution.py:40
  45.9 1.7 %collective-permute-start.6 = (bf16[256,1280]{1,0:T(8,128)(2,1)S(1)}, bf16[256,1280]{1,0:T(8,128)(2,1)S(1)}, u32[]{:S(2)}, u32[]{:S(2)}) collective-permute-start(bf16[256,1280]{1,0:T(8,128)(2,1)S(1)} %collective-permute-done.1.refs_0_), channel_id=1, source_target_pairs={{16,0},{0,16},{17,1},{1,17},{18,2},{2,18},{19,3},{3,19},{20,4},{4,... | collective-permute-start | bytes 1966088 | tf_op jit(solution)/shard_map/ppermute | solution.py:31
  47.6 3.5 %collective-permute-start.9 = (bf16[2,256,384]{2,1,0:T(8,128)(2,1)S(1)}, bf16[2,256,384]{2,1,0:T(8,128)(2,1)S(1)}, u32[]{:S(2)}, u32[]{:S(2)}) collective-permute-start(bf16[2,256,384]{2,1,0:T(8,128)(2,1)S(1)} %copy-done.11), channel_id=1, source_target_pairs={{5,0},{6,1},{7,2},{8,3},{9,4},{10,5},{11,6},{12,7},{13,8},{14,9},{... | collective-permute-start | bytes 1179656 | tf_op jit(solution)/shard_map/ppermute | solution.py:40
  52.4 2.6 %collective-permute-start.11 = (bf16[2,256,384]{2,1,0:T(8,128)(2,1)S(1)}, bf16[2,256,384]{2,1,0:T(8,128)(2,1)S(1)}, u32[]{:S(2)}, u32[]{:S(2)}) collective-permute-start(bf16[2,256,384]{2,1,0:T(8,128)(2,1)S(1)} %copy-done.9), channel_id=1, source_target_pairs={{13,0},{14,1},{15,2},{0,3},{1,4},{2,5},{3,6},{4,7},{5,8},{6,9},{7,... | collective-permute-start | bytes 1179656 | tf_op jit(solution)/shard_map/ppermute | solution.py:40
  55.0 3.0 %collective-permute-start.8 = (bf16[2,256,384]{2,1,0:T(8,128)(2,1)S(1)}, bf16[2,256,384]{2,1,0:T(8,128)(2,1)S(1)}, u32[]{:S(2)}, u32[]{:S(2)}) collective-permute-start(bf16[2,256,384]{2,1,0:T(8,128)(2,1)S(1)} %copy-done.8), channel_id=1, source_target_pairs={{1,0},{2,1},{3,2},{4,3},{5,4},{6,5},{7,6},{8,7},{9,8},{10,9},{11,1... | collective-permute-start | bytes 1179656 | tf_op jit(solution)/shard_map/ppermute | solution.py:40
  59.3 3.4 %attend.4.refs_4_ = bf16[512,256]{1,0:T(8,128)(2,1)S(1)} custom-call(s32[1]{0:T(128)S(6)} %copy.16.live_ref, s32[1]{0:T(128)S(6)} %copy.17.depth_ref, bf16[512,256]{1,0:T(8,128)(2,1)S(1)} %get-tuple-element.37.q_ref, bf16[512,256]{1,0:T(8,128)(2,1)S(1)} %get-tuple-element.38.k_ref, bf16[512,256]{1,0:T(8,128)(2,1)S(1)} %get-tuple-element.39.v_ref, ...), custom_call_target="tpu_custom_call" | custom-call | flops 1 | bytes 1 | tf_op jit(solution)/shard_map/attend/pallas_call | solution.py:284
  63.7 4.4 %relay_project.1 = (bf16[2,256,640]{2,1,0:T(8,128)(2,1)}, bf16[2,256,640]{2,1,0:T(8,128)(2,1)}) custom-call(s32[1]{0:T(128)} %bitcast.2.kv_ref, s32[1]{0:T(128)} %bitcast.here_ref, s32[32]{0:T(128)S(1)} %copy-done.5, bf16[256,1280]{1,0:T(8,128)(2,1)S(1)} %collective-permute-done.1.refs_0_, bf16[256,1280]{1,0:T(8,128)(2,1)S(1)} %collective-permute-done.6.refs_1_, ...), custom_call_target="tpu_custom_call" | custom-call | flops 1 | bytes 1 | tf_op jit(solution)/shard_map/relay_project/pallas_call | solution.py:220
  68.1 2.2 %collective-permute-done.7.refs_8_ = bf16[512,256]{1,0:T(8,128)(2,1)S(1)} collective-permute-done((bf16[512,256]{1,0:T(8,128)(2,1)S(1)}, bf16[512,256]{1,0:T(8,128)(2,1)S(1)}, u32[]{:S(2)}, u32[]{:S(2)}) %collective-permute-start.7) | collective-permute-done | bytes 262176 | tf_op jit(solution)/shard_map/ppermute | solution.py:31
  70.3 17.9 %collective-permute-done.10.p2 = bf16[2,256,384]{2,1,0:T(8,128)(2,1)S(1)} collective-permute-done((bf16[2,256,384]{2,1,0:T(8,128)(2,1)S(1)}, bf16[2,256,384]{2,1,0:T(8,128)(2,1)S(1)}, u32[]{:S(2)}, u32[]{:S(2)}) %collective-permute-start.10) | collective-permute-done | bytes 393248 | tf_op jit(solution)/shard_map/ppermute | solution.py:40
  88.2 1.9 %attend.5.refs_5_ = bf16[512,128]{1,0:T(8,128)(2,1)S(1)} custom-call(s32[1]{0:T(128)S(6)} %copy.16.live_ref, s32[1]{0:T(128)S(6)} %copy.17.depth_ref, bf16[512,128]{1,0:T(8,128)(2,1)S(1)} %get-tuple-element.47.q_ref, bf16[512,128]{1,0:T(8,128)(2,1)S(1)} %get-tuple-element.48.k_ref, bf16[512,128]{1,0:T(8,128)(2,1)S(1)} %get-tuple-element.49.v_ref, ...), custom_call_target="tpu_custom_call" | custom-call | flops 1 | bytes 1 | tf_op jit(solution)/shard_map/attend/pallas_call | solution.py:284
  90.9 1.9 %attend.6.refs_6_ = bf16[512,128]{1,0:T(8,128)(2,1)S(1)} custom-call(s32[1]{0:T(128)S(6)} %copy.16.live_ref, s32[1]{0:T(128)S(6)} %copy.17.depth_ref, bf16[512,128]{1,0:T(8,128)(2,1)S(1)} %get-tuple-element.59.q_ref, bf16[512,128]{1,0:T(8,128)(2,1)S(1)} %get-tuple-element.60.k_ref, bf16[512,128]{1,0:T(8,128)(2,1)S(1)} %get-tuple-element.61.v_ref, ...), custom_call_target="tpu_custom_call" | custom-call | flops 1 | bytes 1 | tf_op jit(solution)/shard_map/attend/pallas_call | solution.py:284
  94.1 1.9 %attend.7.refs_7_ = bf16[512,128]{1,0:T(8,128)(2,1)S(1)} custom-call(s32[1]{0:T(128)S(6)} %copy.16.live_ref, s32[1]{0:T(128)S(6)} %copy.17.depth_ref, bf16[512,128]{1,0:T(8,128)(2,1)S(1)} %get-tuple-element.63.q_ref, bf16[512,128]{1,0:T(8,128)(2,1)S(1)} %get-tuple-element.64.k_ref, bf16[512,128]{1,0:T(8,128)(2,1)S(1)} %get-tuple-element.65.v_ref, ...), custom_call_target="tpu_custom_call" | custom-call | flops 1 | bytes 1 | tf_op jit(solution)/shard_map/attend/pallas_call | solution.py:284
  96.8 2.3 %collective-permute-done.13.refs_10_ = bf16[512,128]{1,0:T(8,128)(2,1)S(1)} collective-permute-done((bf16[512,128]{1,0:T(8,128)(2,1)S(1)}, bf16[512,128]{1,0:T(8,128)(2,1)S(1)}, u32[]{:S(2)}, u32[]{:S(2)}) %collective-permute-start.13) | collective-permute-done | bytes 131104 | tf_op jit(solution)/shard_map/ppermute | solution.py:31
  99.1 2.9 %collective-permute-done.14.refs_11_ = bf16[512,128]{1,0:T(8,128)(2,1)S(1)} collective-permute-done((bf16[512,128]{1,0:T(8,128)(2,1)S(1)}, bf16[512,128]{1,0:T(8,128)(2,1)S(1)}, u32[]{:S(2)}, u32[]{:S(2)}) %collective-permute-start.14) | collective-permute-done | bytes 131104 | tf_op jit(solution)/shard_map/ppermute | solution.py:31
  102.0 4.9 %finish.1 = bf16[512,1280]{1,0:T(8,128)(2,1)} custom-call(bf16[512,1280]{1,0:T(8,128)(2,1)S(1)} %copy-done, bf16[640,1280]{1,0:T(8,128)(2,1)S(1)} %copy-done.3, bf16[640,1280]{1,0:T(8,128)(2,1)S(1)} %collective-permute-done.refs_2_, f32[1,1280]{1,0:T(1,128)S(1)} %reshape.20.refs_3_, bf16[512,256]{1,0:T(8,128)(2,1)S(1)} %attend.4.refs_4_, ...), custom_call_target="tpu_custom_call" | custom-call | flops 1 | bytes 1 | tf_op jit(solution)/shard_map/finish/pallas_call | solution.py:324
  (43 shorter events, 9.2 us)
Async XLA Ops:
  0.6 14.9 %copy-start.2 = (bf16[1280,640]{1,0:T(8,128)(2,1)S(1)}, bf16[1280,640]{1,0:T(8,128)(2,1)}, u32[]{:S(2)}) copy-start(bf16[1280,640]{1,0:T(8,128)(2,1)} %refs_3_.1) | copy-start | bytes 4915204
  2.7 12.8 %copy-start.7 = (f32[640]{0:T(1024)S(1)}, f32[640]{0:T(1024)}, u32[]{:S(2)}) copy-start(f32[640]{0:T(1024)} %param.18) | copy-start | bytes 7684
  2.7 12.8 %copy-start = (bf16[512,1280]{1,0:T(8,128)(2,1)S(1)}, bf16[512,1280]{1,0:T(8,128)(2,1)}, u32[]{:S(2)}) copy-start(bf16[512,1280]{1,0:T(8,128)(2,1)} %refs_0_.1) | copy-start | bytes 3932164
  2.7 12.8 %copy-start.1 = (bf16[1280,640]{1,0:T(8,128)(2,1)S(1)}, bf16[1280,640]{1,0:T(8,128)(2,1)}, u32[]{:S(2)}) copy-start(bf16[1280,640]{1,0:T(8,128)(2,1)} %refs_2_.1) | copy-start | bytes 4915204
  6.9 39.0 %collective-permute-start = (bf16[640,1280]{1,0:T(8,128)(2,1)}, bf16[640,1280]{1,0:T(8,128)(2,1)S(1)}, u32[]{:S(2)}, u32[]{:S(2)}) collective-permute-start(bf16[640,1280]{1,0:T(8,128)(2,1)} %refs_1_.1), channel_id=1, source_target_pairs={{16,0},{0,16},{17,1},{1,17},{18,2},{2,18},{19,3},{3,19},{20,4},{4,... | collective-permute-start | bytes 4915208 | tf_op jit(solution)/shard_map/ppermute | solution.py:31
  9.9 19.8 %collective-permute-start.1 = (bf16[256,1280]{1,0:T(8,128)(2,1)}, bf16[256,1280]{1,0:T(8,128)(2,1)S(1)}, u32[]{:S(2)}, u32[]{:S(2)}) collective-permute-start(bf16[256,1280]{1,0:T(8,128)(2,1)} %split_rows.1._), channel_id=1, source_target_pairs={{12,0},{13,1},{14,2},{15,3},{0,4},{1,5},{2,6},{3,7},{4,8},{5,9},{6... | collective-permute-start | bytes 1966088 | tf_op jit(solution)/shard_map/ppermute | solution.py:40
  11.6 33.5 %collective-permute-start.4 = (bf16[2,256,256]{2,1,0:T(8,128)(2,1)}, bf16[2,256,256]{2,1,0:T(8,128)(2,1)S(1)}, u32[]{:S(2)}, u32[]{:S(2)}) collective-permute-start(bf16[2,256,256]{2,1,0:T(8,128)(2,1)} %get-tuple-element.35), channel_id=1, source_target_pairs={{9,0},{10,1},{11,2},{12,3},{13,4},{14,5},{15,6},{0,7},{1,8},{2,9},... | collective-permute-start | bytes 786440 | tf_op jit(solution)/shard_map/ppermute | solution.py:40
  12.9 25.4 %collective-permute-start.3 = (bf16[2,256,256]{2,1,0:T(8,128)(2,1)}, bf16[2,256,256]{2,1,0:T(8,128)(2,1)S(1)}, u32[]{:S(2)}, u32[]{:S(2)}) collective-permute-start(bf16[2,256,256]{2,1,0:T(8,128)(2,1)} %get-tuple-element.42), channel_id=1, source_target_pairs={{5,0},{6,1},{7,2},{8,3},{9,4},{10,5},{11,6},{12,7},{13,8},{14,9},{... | collective-permute-start | bytes 786440 | tf_op jit(solution)/shard_map/ppermute | solution.py:40
  15.0 28.8 %collective-permute-start.5 = (bf16[2,256,256]{2,1,0:T(8,128)(2,1)}, bf16[2,256,256]{2,1,0:T(8,128)(2,1)S(1)}, u32[]{:S(2)}, u32[]{:S(2)}) collective-permute-start(bf16[2,256,256]{2,1,0:T(8,128)(2,1)} %get-tuple-element.43), channel_id=1, source_target_pairs={{13,0},{14,1},{15,2},{0,3},{1,4},{2,5},{3,6},{4,7},{5,8},{6,9},{7,... | collective-permute-start | bytes 786440 | tf_op jit(solution)/shard_map/ppermute | solution.py:40
  17.0 30.7 %copy-start.11 = (bf16[2,256,384]{2,1,0:T(8,128)(2,1)S(1)}, bf16[2,256,384]{2,1,0:T(8,128)(2,1)}, u32[]{:S(2)}) copy-start(bf16[2,256,384]{2,1,0:T(8,128)(2,1)} %get-tuple-element.53) | copy-start | bytes 1179652
  17.0 34.2 %copy-start.10 = (bf16[2,256,384]{2,1,0:T(8,128)(2,1)S(1)}, bf16[2,256,384]{2,1,0:T(8,128)(2,1)}, u32[]{:S(2)}) copy-start(bf16[2,256,384]{2,1,0:T(8,128)(2,1)} %get-tuple-element.55) | copy-start | bytes 1179652
  17.0 35.4 %copy-start.9 = (bf16[2,256,384]{2,1,0:T(8,128)(2,1)S(1)}, bf16[2,256,384]{2,1,0:T(8,128)(2,1)}, u32[]{:S(2)}) copy-start(bf16[2,256,384]{2,1,0:T(8,128)(2,1)} %get-tuple-element.57) | copy-start | bytes 1179652
  17.0 38.0 %copy-start.8 = (bf16[2,256,384]{2,1,0:T(8,128)(2,1)S(1)}, bf16[2,256,384]{2,1,0:T(8,128)(2,1)}, u32[]{:S(2)}) copy-start(bf16[2,256,384]{2,1,0:T(8,128)(2,1)} %get-tuple-element.51) | copy-start | bytes 1179652
  24.0 39.8 %copy-start.5 = (s32[32]{0:T(128)S(1)}, s32[32]{0:T(128)}, u32[]{:S(2)}) copy-start(s32[32]{0:T(128)} %placement.1) | copy-start | bytes 388
  29.7 15.3 %collective-permute-start.2 = (bf16[2,256,256]{2,1,0:T(8,128)(2,1)S(1)}, bf16[2,256,256]{2,1,0:T(8,128)(2,1)S(1)}, u32[]{:S(2)}, u32[]{:S(2)}) collective-permute-start(bf16[2,256,256]{2,1,0:T(8,128)(2,1)S(1)} %copy-done.12), channel_id=1, source_target_pairs={{1,0},{2,1},{3,2},{4,3},{5,4},{6,5},{7,6},{8,7},{9,8},{10,9},{11,1... | collective-permute-start | bytes 786440 | tf_op jit(solution)/shard_map/ppermute | solution.py:40
  45.9 16.8 %collective-permute-start.6 = (bf16[256,1280]{1,0:T(8,128)(2,1)S(1)}, bf16[256,1280]{1,0:T(8,128)(2,1)S(1)}, u32[]{:S(2)}, u32[]{:S(2)}) collective-permute-start(bf16[256,1280]{1,0:T(8,128)(2,1)S(1)} %collective-permute-done.1.refs_0_), channel_id=1, source_target_pairs={{16,0},{0,16},{17,1},{1,17},{18,2},{2,18},{19,3},{3,19},{20,4},{4,... | collective-permute-start | bytes 1966088 | tf_op jit(solution)/shard_map/ppermute | solution.py:31
  47.6 22.7 %collective-permute-start.9 = (bf16[2,256,384]{2,1,0:T(8,128)(2,1)S(1)}, bf16[2,256,384]{2,1,0:T(8,128)(2,1)S(1)}, u32[]{:S(2)}, u32[]{:S(2)}) collective-permute-start(bf16[2,256,384]{2,1,0:T(8,128)(2,1)S(1)} %copy-done.11), channel_id=1, source_target_pairs={{5,0},{6,1},{7,2},{8,3},{9,4},{10,5},{11,6},{12,7},{13,8},{14,9},{... | collective-permute-start | bytes 1179656 | tf_op jit(solution)/shard_map/ppermute | solution.py:40
  51.2 37.0 %collective-permute-start.10 = (bf16[2,256,384]{2,1,0:T(8,128)(2,1)S(1)}, bf16[2,256,384]{2,1,0:T(8,128)(2,1)S(1)}, u32[]{:S(2)}, u32[]{:S(2)}) collective-permute-start(bf16[2,256,384]{2,1,0:T(8,128)(2,1)S(1)} %copy-done.10), channel_id=1, source_target_pairs={{9,0},{10,1},{11,2},{12,3},{13,4},{14,5},{15,6},{0,7},{1,8},{2,9},... | collective-permute-start | bytes 1179656 | tf_op jit(solution)/shard_map/ppermute | solution.py:40
  52.4 35.8 %collective-permute-start.11 = (bf16[2,256,384]{2,1,0:T(8,128)(2,1)S(1)}, bf16[2,256,384]{2,1,0:T(8,128)(2,1)S(1)}, u32[]{:S(2)}, u32[]{:S(2)}) collective-permute-start(bf16[2,256,384]{2,1,0:T(8,128)(2,1)S(1)} %copy-done.9), channel_id=1, source_target_pairs={{13,0},{14,1},{15,2},{0,3},{1,4},{2,5},{3,6},{4,7},{5,8},{6,9},{7,... | collective-permute-start | bytes 1179656 | tf_op jit(solution)/shard_map/ppermute | solution.py:40
  55.0 33.2 %collective-permute-start.8 = (bf16[2,256,384]{2,1,0:T(8,128)(2,1)S(1)}, bf16[2,256,384]{2,1,0:T(8,128)(2,1)S(1)}, u32[]{:S(2)}, u32[]{:S(2)}) collective-permute-start(bf16[2,256,384]{2,1,0:T(8,128)(2,1)S(1)} %copy-done.8), channel_id=1, source_target_pairs={{1,0},{2,1},{3,2},{4,3},{5,4},{6,5},{7,6},{8,7},{9,8},{10,9},{11,1... | collective-permute-start | bytes 1179656 | tf_op jit(solution)/shard_map/ppermute | solution.py:40
  62.7 7.5 %collective-permute-start.7 = (bf16[512,256]{1,0:T(8,128)(2,1)S(1)}, bf16[512,256]{1,0:T(8,128)(2,1)S(1)}, u32[]{:S(2)}, u32[]{:S(2)}) collective-permute-start(bf16[512,256]{1,0:T(8,128)(2,1)S(1)} %attend.4.refs_4_), channel_id=1, source_target_pairs={{16,0},{0,16},{17,1},{1,17},{18,2},{2,18},{19,3},{3,19},{20,4},{4,... | collective-permute-start | bytes 786440 | tf_op jit(solution)/shard_map/ppermute | solution.py:31
  90.1 6.7 %collective-permute-start.12 = (bf16[512,128]{1,0:T(8,128)(2,1)S(1)}, bf16[512,128]{1,0:T(8,128)(2,1)S(1)}, u32[]{:S(2)}, u32[]{:S(2)}) collective-permute-start(bf16[512,128]{1,0:T(8,128)(2,1)S(1)} %attend.5.refs_5_), channel_id=1, source_target_pairs={{16,0},{0,16},{17,1},{1,17},{18,2},{2,18},{19,3},{3,19},{20,4},{4,... | collective-permute-start | bytes 393224 | tf_op jit(solution)/shard_map/ppermute | solution.py:31
  92.7 6.3 %collective-permute-start.13 = (bf16[512,128]{1,0:T(8,128)(2,1)S(1)}, bf16[512,128]{1,0:T(8,128)(2,1)S(1)}, u32[]{:S(2)}, u32[]{:S(2)}) collective-permute-start(bf16[512,128]{1,0:T(8,128)(2,1)S(1)} %attend.6.refs_6_), channel_id=1, source_target_pairs={{16,0},{0,16},{17,1},{1,17},{18,2},{2,18},{19,3},{3,19},{20,4},{4,... | collective-permute-start | bytes 393224 | tf_op jit(solution)/shard_map/ppermute | solution.py:31
  96.0 6.0 %collective-permute-start.14 = (bf16[512,128]{1,0:T(8,128)(2,1)S(1)}, bf16[512,128]{1,0:T(8,128)(2,1)S(1)}, u32[]{:S(2)}, u32[]{:S(2)}) collective-permute-start(bf16[512,128]{1,0:T(8,128)(2,1)S(1)} %attend.7.refs_7_), channel_id=1, source_target_pairs={{16,0},{0,16},{17,1},{1,17},{18,2},{2,18},{19,3},{3,19},{20,4},{4,... | collective-permute-start | bytes 393224 | tf_op jit(solution)/shard_map/ppermute | solution.py:31
  (4 other events, 31.2 us)
where the time goes:
time: 107 us
  waiting for transfers between devices  47.3 us (44%)
  Pallas kernels  31.4 us (29%)
  starting transfers between devices  24.7 us (23%)
  between operations  2.09 us (2%)
  local copies, waits for them, and re-layouts  1.49 us (1%)
    ppermute x9, waiting for transfers between devices, over_blk(): return lax.ppermute(block, ('kv', 'blk'), route)  39 us
    ppermute x9, starting transfers between devices, over_blk(): return lax.ppermute(block, ('kv', 'blk'), route)  16 us
    pallas_call x4, Pallas kernels, attend(): pl.pallas_call(functools.partial(attend_kernel, inner), in_specs=[smem, s...  8.95 us
    ppermute x6, starting transfers between devices, from_behind(): return lax.ppermute(block, axis, route)  8.7 us
    ppermute x6, waiting for transfers between devices, from_behind(): return lax.ppermute(block, axis, route)  8.27 us
    pallas_call x1, Pallas kernels, project(): pl.pallas_call(functools.partial(project_kernel, slices), out_shape=outs,...  6.94 us
    pallas_call x1, Pallas kernels, finish(): pl.pallas_call(functools.partial(finish_kernel, slices, len(slices)), gri...  4.88 us
    pallas_call x1, Pallas kernels, relay_project(): pl.pallas_call(functools.partial(relay_kernel, group_slices(width), block...  4.37 us
  transfers between devices with their start and end apart: 15, of which 9 were waited for; matrix products, arithmetic and copies ran while one was open for 0% of the time, Pallas kernels for 17%

commit v1 on v0

--- a/solution.py
+++ b/solution.py
@@ -15,6 +15,7 @@
 GROUPS = (256, 384)
 UNITS = ((256,), (128, 128, 128))
 WINDOW = 4
+PARTS = 2
 SLOT_ORDER = (2, 1, 3, 0)
 VMEM_LIMIT = 16 * 1024 * 1024
 FIRST_LIMIT = 58 * 1024 * 1024
@@ -72,67 +73,94 @@
     return pl.CostEstimate(flops=1, bytes_accessed=1, transcendentals=0)
 
 
-def split_kernel(kv_ref, hidden, out, sem):
-    rows = pl.ds(pl.multiple_of(kv_ref[0] * PAGE, PAGE), PAGE)
-    copy = pltpu.make_async_copy(hidden.at[rows], out, sem)
-    copy.start()
-    copy.wait()
-
-
-def split_rows(hidden_in, kv_index):
-    return pl.pallas_call(
-        split_kernel,
-        in_specs=[pl.BlockSpec(memory_space=pltpu.SMEM), pl.BlockSpec(memory_space=pltpu.HBM)],
-        out_specs=pl.BlockSpec(memory_space=pltpu.VMEM),
-        out_shape=jax.ShapeDtypeStruct((PAGE, hidden_in.shape[1]), bf16),
-        scratch_shapes=[pltpu.SemaphoreType.DMA],
-        compiler_params=params(FIRST_LIMIT),
-        cost_estimate=cost(),
-        name="split_rows",
-    )(kv_index, hidden_in)
-
-
-def pack_kernel(slices, devices, offsets, here_ref, table, keys, values, _, *rest):
-    outs, (buf, sem) = rest[:-2], rest[-2:]
+def pack_kernel(slices, devices, offsets, kv_ref, here_ref, table, hidden, keys, values, *rest):
+    outs, (buf, row_sem, sem) = rest[:-3], rest[-3:]
+    part = PAGE // PARTS
+    row_copies = []
+    for i in range(PARTS):
+        rows = pl.ds(pl.multiple_of(kv_ref[0] * PAGE + i * part, part), part)
+        target = outs[0].at[pl.ds(i * part, part)]
+        row_copies.append(pltpu.make_async_copy(hidden.at[rows], target, row_sem.at[i]))
+    for copy in row_copies:
+        copy.start()
     copies = []
     for slot in range(PMAX):
         asker = lax.rem(here_ref[0] + (devices - offsets[slot]), devices)
         local = lax.rem(table[slot, asker], keys.shape[0])
         for side, pool in enumerate((keys, values)):
-            index = 2 * slot + side
-            copies.append(pltpu.make_async_copy(pool.at[local], buf.at[index], sem.at[index]))
+            for i in range(PARTS):
+                rows = pl.ds(i * part, part)
+                index = (2 * slot + side) * PARTS + i
+                target = buf.at[2 * slot + side, rows]
+                copies.append(pltpu.make_async_copy(pool.at[local, rows], target, sem.at[index]))
     for copy in copies:
         copy.start()
     for slot in range(PMAX):
         for side in range(2):
-            index = 2 * slot + side
-            copies[index].wait()
-            for g, (start, size) in enumerate(slices):
-                outs[g * PMAX + slot][side] = buf[index, :, start : start + size]
-
-
-def pack(pool_keys, pool_values, table, here, devices, offsets, first):
+            for i in range(PARTS):
+                copies[(2 * slot + side) * PARTS + i].wait()
+                rows = slice(i * part, (i + 1) * part)
+                for g, (start, size) in enumerate(slices):
+                    outs[1 + g * PMAX + slot][side, rows] = buf[
+                        2 * slot + side, rows, start : start + size
+                    ]
+    for copy in row_copies:
+        copy.wait()
+
+
+def pack(hidden_in, pool_keys, pool_values, table, kv_index, here, devices, offsets):
     width = pool_keys.shape[2]
     slices = group_slices(width)
-    outs = []
+    outs = [jax.ShapeDtypeStruct((PAGE, hidden_in.shape[1]), bf16)]
     for _, size in slices:
         outs += [jax.ShapeDtypeStruct((2, PAGE, size), bf16)] * PMAX
     smem = pl.BlockSpec(memory_space=pltpu.SMEM)
     hbm = pl.BlockSpec(memory_space=pltpu.HBM)
     result = pl.pallas_call(
         functools.partial(pack_kernel, slices, devices, offsets),
-        in_specs=[smem, smem, hbm, hbm, pl.BlockSpec(memory_space=pl.ANY)],
+        in_specs=[smem] * 3 + [hbm] * 3,
         out_specs=[pl.BlockSpec(memory_space=pltpu.VMEM)] * len(outs),
         out_shape=outs,
         scratch_shapes=[
             pltpu.VMEM((2 * PMAX, PAGE, width), bf16),
-            pltpu.SemaphoreType.DMA((2 * PMAX,)),
+            pltpu.SemaphoreType.DMA((PARTS,)),
+            pltpu.SemaphoreType.DMA((2 * PMAX * PARTS,)),
         ],
         compiler_params=params(FIRST_LIMIT),
         cost_estimate=cost(),
         name="pack",
-    )(here, table, pool_keys, pool_values, first)
-    return [result[PMAX * g : PMAX * (g + 1)] for g in range(len(slices))]
+    )(kv_index, here, table, hidden_in, pool_keys, pool_values)
+    return result[0], [result[1 + PMAX * g : 1 + PMAX * (g + 1)] for g in range(len(slices))]
+
+
+def join_kernel(w_out, rows, out, sem):
+    depth, count = w_out.shape[0], rows.shape[0]
+    copies = []
+    for i in range(PARTS):
+        part = pl.ds(i * (depth // PARTS), depth // PARTS)
+        copies.append(pltpu.make_async_copy(w_out.at[part], out.at[part], sem.at[i]))
+    for i in range(PARTS):
+        part = pl.ds(i * (count // PARTS), count // PARTS)
+        target = out.at[pl.ds(depth + i * (count // PARTS), count // PARTS)]
+        copies.append(pltpu.make_async_copy(rows.at[part], target, sem.at[PARTS + i]))
+    for copy in copies:
+        copy.start()
+    for copy in copies:
+        copy.wait()
+
+
+def join(w_out, rows):
+    out = jax.ShapeDtypeStruct((w_out.shape[0] + rows.shape[0], w_out.shape[1]), bf16)
+    return pl.pallas_call(
+        join_kernel,
+        in_specs=[pl.BlockSpec(memory_space=pl.ANY)] * 2,
+        out_specs=pl.BlockSpec(memory_space=pltpu.VMEM),
+        out_shape=out,
+        scratch_shapes=[pltpu.SemaphoreType.DMA((2 * PARTS,))],
+        compiler_params=params(),
+        cost_estimate=cost(),
+        name="join",
+    )(w_out, rows)
 
 
 def head_sum_matrix():
@@ -197,8 +225,9 @@
 def relay_kernel(slices, blocks, devices, offsets, kv_ref, here_ref, placement, *refs):
     mine, theirs, wk, wv, gain, key_out, value_out = refs
     matrix = head_sum_matrix()
-    for rows_ref, block in ((mine, kv_ref[0]), (theirs, 1 - kv_ref[0])):
-        x = rows_ref[...]
+    first = theirs.shape[0] - PAGE
+    for rows, block in ((mine[...], kv_ref[0]), (theirs[first:, :], 1 - kv_ref[0])):
+        x = rows
         scale = row_scale_of(x)
         offset = jnp.where(block == 0, offsets[0], offsets[1])
         source = lax.rem(here_ref[0] + (devices - offset), devices)
@@ -324,7 +353,7 @@
     return pl.pallas_call(
         functools.partial(finish_kernel, slices, len(slices)),
         grid=(tokens // step,),
-        in_specs=[by_rows(depth), whole(w_mine.shape), whole(w_theirs.shape), whole(rate.shape)]
+        in_specs=[by_rows(depth), whole(w_mine.shape), whole(w_mine.shape), whole(rate.shape)]
         + [by_rows(size) for _, size in slices] * 2,
         out_specs=by_rows(depth),
         out_shape=jax.ShapeDtypeStruct((tokens, depth), bf16),
@@ -359,11 +388,9 @@
     block_offsets = [(2 * b + 1) * devices // (2 * blocks) for b in range(blocks)]
 
     assert blocks == lax.axis_size("kv") == 2
-    relay_send = split_rows(hidden_in, kv_index)
-    page_send = pack(
-        pool_keys, pool_values, prefix_pages.T, here, devices, page_offsets, relay_send
+    relay_send, page_send = pack(
+        hidden_in, pool_keys, pool_values, prefix_pages.T, kv_index, here, devices, page_offsets
     )
-
     projected = project(hidden_in, w_query, w_key, w_value, gain)
 
     sends = [(relay_send, block_offsets)]
@@ -380,20 +407,18 @@
         first = 1 + g * PMAX
         got = dict(zip(SLOT_ORDER, arrived[first : first + PMAX]))
         pages.append([got[slot] for slot in range(PMAX)])
-    w_theirs = from_behind(after(w_out, page_send[0][2]), "kv", 1)
-    first_pages = arrived[1 : 1 + PMAX]
-    relay_theirs = from_behind(after(relay_mine, w_theirs, *first_pages), "kv", 1)
+    swapped = from_behind(join(w_out, relay_mine), "kv", 1)
     new_keys, new_values = relay_project(
-        relay_mine, relay_theirs, w_key, w_value, gain, kv_index, here, placement, block_offsets
+        relay_mine, swapped, w_key, w_value, gain, kv_index, here, placement, block_offsets
     )
 
     mine, theirs = [], []
     for (g, inner, _, _), (q, k, v) in zip(unit_slices(), projected):
-        q = after(q, new_keys, theirs[0]) if g else q
+        q = after(q, new_keys) if g else q
         attended = attend(req_len, prefix_len, q, k, v, pages[g], inner)
         mine.append(attended)
         theirs.append(from_behind(attended, "kv", 1))
-    layer_out = finish(hidden_in, w_out, w_theirs, rate, mine, theirs)
+    layer_out = finish(hidden_in, w_out, swapped, rate, mine, theirs)
     return (layer_out, new_keys, new_values)
 
 

time: 107 us -> 108 us (level)
  waiting for transfers between devices: 47.3 us -> 52.5 us
  starting transfers between devices: 24.7 us -> 22.5 us
  local copies, waits for them, and re-layouts: 1.49 us -> 0.08 us
    ppermute x6 -> x5, waiting for transfers between devices: 8.27 us -> 17.1 us  [from_behind(): return lax.ppermute(block, axis, route)]
    ppermute x6 -> x5, starting transfers between devices: 8.7 us -> 4.34 us  [from_behind(): return lax.ppermute(block, axis, route)]
    ppermute x9, waiting for transfers between devices: 39 us -> 35.4 us  [over_blk(): return lax.ppermute(block, ('kv', 'blk'), route)]
    ppermute x9, starting transfers between devices: 16 us -> 18.2 us  [over_blk(): return lax.ppermute(block, ('kv', 'blk'), route)]
    pallas_call x1, Pallas kernels: 2.06 us -> 0.43 us  [join(): pl.pallas_call(join_kernel, in_specs=[pl.BlockSpec(memory_space=pl.ANY)]...]
    unnamed x26, local copies, waits for them, and re-layouts: 1.48 us -> 0.07 us
  transfers between devices with their start and end apart: 15 -> 14, of which waited for: 9 -> 6; matrix products, arithmetic and copies ran while one was open for 0% -> 0% of each run, Pallas kernels for 17% -> 19%
where the time goes in v1:
time: 108 us
  waiting for transfers between devices  52.5 us (49%)
  Pallas kernels  30.5 us (28%)
  starting transfers between devices  22.5 us (21%)
  between operations  2.14 us (2%)
    ppermute x9, waiting for transfers between devices, over_blk(): return lax.ppermute(block, ('kv', 'blk'), route)  35.4 us
    ppermute x9, starting transfers between devices, over_blk(): return lax.ppermute(block, ('kv', 'blk'), route)  18.2 us
    ppermute x5, waiting for transfers between devices, from_behind(): return lax.ppermute(block, axis, route)  17.1 us
    pallas_call x4, Pallas kernels, attend(): pl.pallas_call(functools.partial(attend_kernel, inner), in_specs=[smem, s...  8.93 us
    pallas_call x1, Pallas kernels, project(): pl.pallas_call(functools.partial(project_kernel, slices), out_shape=outs,...  6.97 us
    pallas_call x1, Pallas kernels, finish(): pl.pallas_call(functools.partial(finish_kernel, slices, len(slices)), gri...  4.89 us
    pallas_call x1, Pallas kernels, pack(): pl.pallas_call(functools.partial(pack_kernel, slices, devices, offsets),...  4.8 us
    pallas_call x1, Pallas kernels, relay_project(): pl.pallas_call(functools.partial(relay_kernel, group_slices(width), block...  4.45 us
  transfers between devices with their start and end apart: 14, of which 6 were waited for; matrix products, arithmetic and copies ran while one was open for 0% of the time, Pallas kernels for 19%

profile of v1, /device:TPU:0, one launch (start us, length us, event | category | flops | bytes accessed | tf_op | source)
XLA Modules:
  0.0 107.7 jit_solution(1313448252450931407)
XLA Ops:
  0.7 4.8 %pack.1 = (bf16[256,1280]{1,0:T(8,128)(2,1)}, bf16[2,256,256]{2,1,0:T(8,128)(2,1)}, bf16[2,256,256]{2,1,0:T(8,128)(2,1)}, bf16[2,256,256]{2,1,0:T(8,128)(2,1)}, ...) custom-call(s32[1]{0:T(128)} %bitcast.kv_ref, ...), custom_call_target="tpu_custom_call" | custom-call | flops 1 | bytes 1 | tf_op jit(solution)/shard_map/pack/pallas_call | solution.py:119
  5.5 3.1 %collective-permute-start = (bf16[256,1280]{1,0:T(8,128)(2,1)}, bf16[256,1280]{1,0:T(8,128)(2,1)S(1)}, u32[]{:S(2)}, u32[]{:S(2)}) collective-permute-start(bf16[256,1280]{1,0:T(8,128)(2,1)} %get-tuple-element.34), channel_id=1, source_target_pairs={{12,0},{13,1},{14,2},{15,3},{0,4},{1,5},{2,6},{3,7},{4,8},{5,9},{6... | collective-permute-start | bytes 1966088 | tf_op jit(solution)/shard_map/ppermute | solution.py:41
  8.6 17.0 %collective-permute-done.rows.refs_0_ = bf16[256,1280]{1,0:T(8,128)(2,1)S(1)} collective-permute-done((bf16[256,1280]{1,0:T(8,128)(2,1)}, bf16[256,1280]{1,0:T(8,128)(2,1)S(1)}, u32[]{:S(2)}, u32[]{:S(2)}) %collective-permute-start) | collective-permute-done | bytes 655392 | tf_op jit(solution)/shard_map/ppermute | solution.py:41
  26.0 0.9 collective-permute-start.1
  27.5 2.1 %collective-permute-start.4 = (bf16[2,256,256]{2,1,0:T(8,128)(2,1)}, bf16[2,256,256]{2,1,0:T(8,128)(2,1)S(1)}, u32[]{:S(2)}, u32[]{:S(2)}) collective-permute-start(bf16[2,256,256]{2,1,0:T(8,128)(2,1)} %get-tuple-element.41), channel_id=1, source_target_pairs={{9,0},{10,1},{11,2},{12,3},{13,4},{14,5},{15,6},{0,7},{1,8},{2,9},... | collective-permute-start | bytes 786440 | tf_op jit(solution)/shard_map/ppermute | solution.py:41
  29.6 2.7 %collective-permute-start.5 = (bf16[2,256,256]{2,1,0:T(8,128)(2,1)}, bf16[2,256,256]{2,1,0:T(8,128)(2,1)S(1)}, u32[]{:S(2)}, u32[]{:S(2)}) collective-permute-start(bf16[2,256,256]{2,1,0:T(8,128)(2,1)} %get-tuple-element.42), channel_id=1, source_target_pairs={{13,0},{14,1},{15,2},{0,3},{1,4},{2,5},{3,6},{4,7},{5,8},{6,9},{7,... | collective-permute-start | bytes 786440 | tf_op jit(solution)/shard_map/ppermute | solution.py:41
  32.4 7.0 %project.1 = (bf16[512,256]{1,0:T(8,128)(2,1)S(1)}, bf16[512,256]{1,0:T(8,128)(2,1)S(1)}, bf16[512,256]{1,0:T(8,128)(2,1)S(1)}, bf16[512,128]{1,0:T(8,128)(2,1)S...) custom-call(bf16[512,1280]{1,0:T(8,128)(2,1)S(1)} %copy-done, ...), custom_call_target="tpu_custom_call" | custom-call | flops 1 | bytes 1 | tf_op jit(solution)/shard_map/project/pallas_call | solution.py:215
  39.4 1.6 %collective-permute-start.2 = (bf16[2,256,256]{2,1,0:T(8,128)(2,1)S(1)}, bf16[2,256,256]{2,1,0:T(8,128)(2,1)S(1)}, u32[]{:S(2)}, u32[]{:S(2)}) collective-permute-start(bf16[2,256,256]{2,1,0:T(8,128)(2,1)S(1)} %copy-done.12), channel_id=1, source_target_pairs={{1,0},{2,1},{3,2},{4,3},{5,4},{6,5},{7,6},{8,7},{9,8},{10,9},{11,1... | collective-permute-start | bytes 786440 | tf_op jit(solution)/shard_map/ppermute | solution.py:41
  41.0 10.5 %collective-permute-done.4.p2 = bf16[2,256,256]{2,1,0:T(8,128)(2,1)S(1)} collective-permute-done((bf16[2,256,256]{2,1,0:T(8,128)(2,1)}, bf16[2,256,256]{2,1,0:T(8,128)(2,1)S(1)}, u32[]{:S(2)}, u32[]{:S(2)}) %collective-permute-start.4) | collective-permute-done | bytes 262176 | tf_op jit(solution)/shard_map/ppermute | solution.py:41
  51.6 3.5 %collective-permute-start.7 = (bf16[2,256,384]{2,1,0:T(8,128)(2,1)S(1)}, bf16[2,256,384]{2,1,0:T(8,128)(2,1)S(1)}, u32[]{:S(2)}, u32[]{:S(2)}) collective-permute-start(bf16[2,256,384]{2,1,0:T(8,128)(2,1)S(1)} %copy-done.11), channel_id=1, source_target_pairs={{5,0},{6,1},{7,2},{8,3},{9,4},{10,5},{11,6},{12,7},{13,8},{14,9},{... | collective-permute-start | bytes 1179656 | tf_op jit(solution)/shard_map/ppermute | solution.py:41
  55.1 1.9 %collective-permute-start.9 = (bf16[2,256,384]{2,1,0:T(8,128)(2,1)S(1)}, bf16[2,256,384]{2,1,0:T(8,128)(2,1)S(1)}, u32[]{:S(2)}, u32[]{:S(2)}) collective-permute-start(bf16[2,256,384]{2,1,0:T(8,128)(2,1)S(1)} %copy-done.9), channel_id=1, source_target_pairs={{13,0},{14,1},{15,2},{0,3},{1,4},{2,5},{3,6},{4,7},{5,8},{6,9},{7,... | collective-permute-start | bytes 1179656 | tf_op jit(solution)/shard_map/ppermute | solution.py:41
  57.0 2.7 %collective-permute-start.6 = (bf16[2,256,384]{2,1,0:T(8,128)(2,1)S(1)}, bf16[2,256,384]{2,1,0:T(8,128)(2,1)S(1)}, u32[]{:S(2)}, u32[]{:S(2)}) collective-permute-start(bf16[2,256,384]{2,1,0:T(8,128)(2,1)S(1)} %copy-done.8), channel_id=1, source_target_pairs={{1,0},{2,1},{3,2},{4,3},{5,4},{6,5},{7,6},{8,7},{9,8},{10,9},{11,1... | collective-permute-start | bytes 1179656 | tf_op jit(solution)/shard_map/ppermute | solution.py:41
  61.0 3.4 %attend.4.refs_4_ = bf16[512,256]{1,0:T(8,128)(2,1)S(1)} custom-call(s32[1]{0:T(128)S(6)} %copy.16.live_ref, s32[1]{0:T(128)S(6)} %copy.17.depth_ref, bf16[512,256]{1,0:T(8,128)(2,1)S(1)} %get-tuple-element.35.q_ref, bf16[512,256]{1,0:T(8,128)(2,1)S(1)} %get-tuple-element.36.k_ref, bf16[512,256]{1,0:T(8,128)(2,1)S(1)} %get-tuple-element.37.v_ref, ...), custom_call_target="tpu_custom_call" | custom-call | flops 1 | bytes 1 | tf_op jit(solution)/shard_map/attend/pallas_call | solution.py:313
  64.4 12.7 %collective-permute-done.1.refs_1_.refs_2_ = bf16[896,1280]{1,0:T(8,128)(2,1)S(1)} collective-permute-done((bf16[896,1280]{1,0:T(8,128)(2,1)S(1)}, bf16[896,1280]{1,0:T(8,128)(2,1)S(1)}, u32[]{:S(2)}, u32[]{:S(2)}) %collective-permute-start.1) | collective-permute-done | bytes 2293792 | tf_op jit(solution)/shard_map/ppermute | solution.py:32
  77.7 4.5 %relay_project.1 = (bf16[2,256,640]{2,1,0:T(8,128)(2,1)}, bf16[2,256,640]{2,1,0:T(8,128)(2,1)}) custom-call(s32[1]{0:T(128)} %bitcast.kv_ref, s32[1]{0:T(128)} %bitcast.1.here_ref, s32[32]{0:T(128)S(1)} %copy-done.5, bf16[256,1280]{1,0:T(8,128)(2,1)S(1)} %collective-permute-done.rows.refs_0_, bf16[896,1280]{1,0:T(8,128)(2,1)S(1)} %collective-permute-done.1.refs_1_.refs_2_, ...), custom_call_target="tpu_custom_call" | custom-call | flops 1 | bytes 1 | tf_op jit(solution)/shard_map/relay_project/pallas_call | solution.py:249
  82.1 7.9 %collective-permute-done.8.p2 = bf16[2,256,384]{2,1,0:T(8,128)(2,1)S(1)} collective-permute-done((bf16[2,256,384]{2,1,0:T(8,128)(2,1)S(1)}, bf16[2,256,384]{2,1,0:T(8,128)(2,1)S(1)}, u32[]{:S(2)}, u32[]{:S(2)}) %collective-permute-start.8) | collective-permute-done | bytes 393248 | tf_op jit(solution)/shard_map/ppermute | solution.py:41
  90.0 1.9 %attend.5.refs_5_ = bf16[512,128]{1,0:T(8,128)(2,1)S(1)} custom-call(s32[1]{0:T(128)S(6)} %copy.16.live_ref, s32[1]{0:T(128)S(6)} %copy.17.depth_ref, bf16[512,128]{1,0:T(8,128)(2,1)S(1)} %get-tuple-element.45.q_ref, bf16[512,128]{1,0:T(8,128)(2,1)S(1)} %get-tuple-element.46.k_ref, bf16[512,128]{1,0:T(8,128)(2,1)S(1)} %get-tuple-element.47.v_ref, ...), custom_call_target="tpu_custom_call" | custom-call | flops 1 | bytes 1 | tf_op jit(solution)/shard_map/attend/pallas_call | solution.py:313
  91.9 0.7 collective-permute-start.11
  92.6 1.9 %attend.6.refs_6_ = bf16[512,128]{1,0:T(8,128)(2,1)S(1)} custom-call(s32[1]{0:T(128)S(6)} %copy.16.live_ref, s32[1]{0:T(128)S(6)} %copy.17.depth_ref, bf16[512,128]{1,0:T(8,128)(2,1)S(1)} %get-tuple-element.57.q_ref, bf16[512,128]{1,0:T(8,128)(2,1)S(1)} %get-tuple-element.58.k_ref, bf16[512,128]{1,0:T(8,128)(2,1)S(1)} %get-tuple-element.59.v_ref, ...), custom_call_target="tpu_custom_call" | custom-call | flops 1 | bytes 1 | tf_op jit(solution)/shard_map/attend/pallas_call | solution.py:313
  94.4 1.5 %collective-permute-start.12 = (bf16[512,128]{1,0:T(8,128)(2,1)S(1)}, bf16[512,128]{1,0:T(8,128)(2,1)S(1)}, u32[]{:S(2)}, u32[]{:S(2)}) collective-permute-start(bf16[512,128]{1,0:T(8,128)(2,1)S(1)} %attend.6.refs_6_), channel_id=1, source_target_pairs={{16,0},{0,16},{17,1},{1,17},{18,2},{2,18},{19,3},{3,19},{20,4},{4,... | collective-permute-start | bytes 393224 | tf_op jit(solution)/shard_map/ppermute | solution.py:32
  95.9 1.9 %attend.7.refs_7_ = bf16[512,128]{1,0:T(8,128)(2,1)S(1)} custom-call(s32[1]{0:T(128)S(6)} %copy.16.live_ref, s32[1]{0:T(128)S(6)} %copy.17.depth_ref, bf16[512,128]{1,0:T(8,128)(2,1)S(1)} %get-tuple-element.61.q_ref, bf16[512,128]{1,0:T(8,128)(2,1)S(1)} %get-tuple-element.62.k_ref, bf16[512,128]{1,0:T(8,128)(2,1)S(1)} %get-tuple-element.63.v_ref, ...), custom_call_target="tpu_custom_call" | custom-call | flops 1 | bytes 1 | tf_op jit(solution)/shard_map/attend/pallas_call | solution.py:313
  98.5 1.8 %collective-permute-done.12.refs_10_ = bf16[512,128]{1,0:T(8,128)(2,1)S(1)} collective-permute-done((bf16[512,128]{1,0:T(8,128)(2,1)S(1)}, bf16[512,128]{1,0:T(8,128)(2,1)S(1)}, u32[]{:S(2)}, u32[]{:S(2)}) %collective-permute-start.12) | collective-permute-done | bytes 131104 | tf_op jit(solution)/shard_map/ppermute | solution.py:32
  100.3 2.6 %collective-permute-done.13.refs_11_ = bf16[512,128]{1,0:T(8,128)(2,1)S(1)} collective-permute-done((bf16[512,128]{1,0:T(8,128)(2,1)S(1)}, bf16[512,128]{1,0:T(8,128)(2,1)S(1)}, u32[]{:S(2)}, u32[]{:S(2)}) %collective-permute-start.13) | collective-permute-done | bytes 131104 | tf_op jit(solution)/shard_map/ppermute | solution.py:32
  102.9 4.9 %finish.1 = bf16[512,1280]{1,0:T(8,128)(2,1)} custom-call(bf16[512,1280]{1,0:T(8,128)(2,1)S(1)} %copy-done, bf16[640,1280]{1,0:T(8,128)(2,1)S(1)} %copy-done.3, bf16[896,1280]{1,0:T(8,128)(2,1)S(1)} %collective-permute-done.1.refs_1_.refs_2_, f32[1,1280]{1,0:T(1,128)S(1)} %reshape.20.refs_3_, bf16[512,256]{1,0:T(8,128)(2,1)S(1)} %attend.4.refs_4_, ...), custom_call_target="tpu_custom_call" | custom-call | flops 1 | bytes 1 | tf_op jit(solution)/shard_map/finish/pallas_call | solution.py:353
  (41 shorter events, 2.3 us)
Async XLA Ops:
  0.6 24.9 %copy-start.3 = (bf16[640,1280]{1,0:T(8,128)(2,1)S(1)}, bf16[640,1280]{1,0:T(8,128)(2,1)}, u32[]{:S(2)}) copy-start(bf16[640,1280]{1,0:T(8,128)(2,1)} %refs_1_.1) | copy-start | bytes 4915204
  0.6 31.7 %copy-start.4 = (bf16[1280,640]{1,0:T(8,128)(2,1)S(1)}, bf16[1280,640]{1,0:T(8,128)(2,1)}, u32[]{:S(2)}) copy-start(bf16[1280,640]{1,0:T(8,128)(2,1)} %wq.1) | copy-start | bytes 4915204
  5.5 26.9 %copy-start.7 = (f32[640]{0:T(1024)S(1)}, f32[640]{0:T(1024)}, u32[]{:S(2)}) copy-start(f32[640]{0:T(1024)} %param.18) | copy-start | bytes 7684
  5.5 26.9 %copy-start = (bf16[512,1280]{1,0:T(8,128)(2,1)S(1)}, bf16[512,1280]{1,0:T(8,128)(2,1)}, u32[]{:S(2)}) copy-start(bf16[512,1280]{1,0:T(8,128)(2,1)} %refs_0_.1) | copy-start | bytes 3932164
  5.5 26.9 %copy-start.1 = (bf16[1280,640]{1,0:T(8,128)(2,1)S(1)}, bf16[1280,640]{1,0:T(8,128)(2,1)}, u32[]{:S(2)}) copy-start(bf16[1280,640]{1,0:T(8,128)(2,1)} %refs_2_.1) | copy-start | bytes 4915204
  5.5 26.9 %copy-start.2 = (bf16[1280,640]{1,0:T(8,128)(2,1)S(1)}, bf16[1280,640]{1,0:T(8,128)(2,1)}, u32[]{:S(2)}) copy-start(bf16[1280,640]{1,0:T(8,128)(2,1)} %refs_3_.1) | copy-start | bytes 4915204
  5.5 20.0 %collective-permute-start = (bf16[256,1280]{1,0:T(8,128)(2,1)}, bf16[256,1280]{1,0:T(8,128)(2,1)S(1)}, u32[]{:S(2)}, u32[]{:S(2)}) collective-permute-start(bf16[256,1280]{1,0:T(8,128)(2,1)} %get-tuple-element.34), channel_id=1, source_target_pairs={{12,0},{13,1},{14,2},{15,3},{0,4},{1,5},{2,6},{3,7},{4,8},{5,9},{6... | collective-permute-start | bytes 1966088 | tf_op jit(solution)/shard_map/ppermute | solution.py:41
  26.0 51.1 %collective-permute-start.1 = (bf16[896,1280]{1,0:T(8,128)(2,1)S(1)}, bf16[896,1280]{1,0:T(8,128)(2,1)S(1)}, u32[]{:S(2)}, u32[]{:S(2)}) collective-permute-start(bf16[896,1280]{1,0:T(8,128)(2,1)S(1)} %join.1), channel_id=1, source_target_pairs={{16,0},{0,16},{17,1},{1,17},{18,2},{2,18},{19,3},{3,19},{20,4},{4,... | collective-permute-start | bytes 6881288 | tf_op jit(solution)/shard_map/ppermute | solution.py:32
  27.0 14.1 %collective-permute-start.3 = (bf16[2,256,256]{2,1,0:T(8,128)(2,1)}, bf16[2,256,256]{2,1,0:T(8,128)(2,1)S(1)}, u32[]{:S(2)}, u32[]{:S(2)}) collective-permute-start(bf16[2,256,256]{2,1,0:T(8,128)(2,1)} %get-tuple-element.40), channel_id=1, source_target_pairs={{5,0},{6,1},{7,2},{8,3},{9,4},{10,5},{11,6},{12,7},{13,8},{14,9},{... | collective-permute-start | bytes 786440 | tf_op jit(solution)/shard_map/ppermute | solution.py:41
  27.5 24.0 %collective-permute-start.4 = (bf16[2,256,256]{2,1,0:T(8,128)(2,1)}, bf16[2,256,256]{2,1,0:T(8,128)(2,1)S(1)}, u32[]{:S(2)}, u32[]{:S(2)}) collective-permute-start(bf16[2,256,256]{2,1,0:T(8,128)(2,1)} %get-tuple-element.41), channel_id=1, source_target_pairs={{9,0},{10,1},{11,2},{12,3},{13,4},{14,5},{15,6},{0,7},{1,8},{2,9},... | collective-permute-start | bytes 786440 | tf_op jit(solution)/shard_map/ppermute | solution.py:41
  29.6 21.9 %collective-permute-start.5 = (bf16[2,256,256]{2,1,0:T(8,128)(2,1)}, bf16[2,256,256]{2,1,0:T(8,128)(2,1)S(1)}, u32[]{:S(2)}, u32[]{:S(2)}) collective-permute-start(bf16[2,256,256]{2,1,0:T(8,128)(2,1)} %get-tuple-element.42), channel_id=1, source_target_pairs={{13,0},{14,1},{15,2},{0,3},{1,4},{2,5},{3,6},{4,7},{5,8},{6,9},{7,... | collective-permute-start | bytes 786440 | tf_op jit(solution)/shard_map/ppermute | solution.py:41
  32.4 22.7 %copy-start.10 = (bf16[2,256,384]{2,1,0:T(8,128)(2,1)S(1)}, bf16[2,256,384]{2,1,0:T(8,128)(2,1)}, u32[]{:S(2)}) copy-start(bf16[2,256,384]{2,1,0:T(8,128)(2,1)} %get-tuple-element.53) | copy-start | bytes 1179652
  32.4 22.7 %copy-start.9 = (bf16[2,256,384]{2,1,0:T(8,128)(2,1)S(1)}, bf16[2,256,384]{2,1,0:T(8,128)(2,1)}, u32[]{:S(2)}) copy-start(bf16[2,256,384]{2,1,0:T(8,128)(2,1)} %get-tuple-element.55) | copy-start | bytes 1179652
  32.4 24.6 %copy-start.8 = (bf16[2,256,384]{2,1,0:T(8,128)(2,1)S(1)}, bf16[2,256,384]{2,1,0:T(8,128)(2,1)}, u32[]{:S(2)}) copy-start(bf16[2,256,384]{2,1,0:T(8,128)(2,1)} %get-tuple-element.49) | copy-start | bytes 1179652
  39.4 38.3 %copy-start.5 = (s32[32]{0:T(128)S(1)}, s32[32]{0:T(128)}, u32[]{:S(2)}) copy-start(s32[32]{0:T(128)} %placement.1) | copy-start | bytes 388
  39.4 17.6 %collective-permute-start.2 = (bf16[2,256,256]{2,1,0:T(8,128)(2,1)S(1)}, bf16[2,256,256]{2,1,0:T(8,128)(2,1)S(1)}, u32[]{:S(2)}, u32[]{:S(2)}) collective-permute-start(bf16[2,256,256]{2,1,0:T(8,128)(2,1)S(1)} %copy-done.12), channel_id=1, source_target_pairs={{1,0},{2,1},{3,2},{4,3},{5,4},{6,5},{7,6},{8,7},{9,8},{10,9},{11,1... | collective-permute-start | bytes 786440 | tf_op jit(solution)/shard_map/ppermute | solution.py:41
  51.6 30.6 %collective-permute-start.7 = (bf16[2,256,384]{2,1,0:T(8,128)(2,1)S(1)}, bf16[2,256,384]{2,1,0:T(8,128)(2,1)S(1)}, u32[]{:S(2)}, u32[]{:S(2)}) collective-permute-start(bf16[2,256,384]{2,1,0:T(8,128)(2,1)S(1)} %copy-done.11), channel_id=1, source_target_pairs={{5,0},{6,1},{7,2},{8,3},{9,4},{10,5},{11,6},{12,7},{13,8},{14,9},{... | collective-permute-start | bytes 1179656 | tf_op jit(solution)/shard_map/ppermute | solution.py:41
  55.1 34.9 %collective-permute-start.8 = (bf16[2,256,384]{2,1,0:T(8,128)(2,1)S(1)}, bf16[2,256,384]{2,1,0:T(8,128)(2,1)S(1)}, u32[]{:S(2)}, u32[]{:S(2)}) collective-permute-start(bf16[2,256,384]{2,1,0:T(8,128)(2,1)S(1)} %copy-done.10), channel_id=1, source_target_pairs={{9,0},{10,1},{11,2},{12,3},{13,4},{14,5},{15,6},{0,7},{1,8},{2,9},... | collective-permute-start | bytes 1179656 | tf_op jit(solution)/shard_map/ppermute | solution.py:41
  55.1 34.9 %collective-permute-start.9 = (bf16[2,256,384]{2,1,0:T(8,128)(2,1)S(1)}, bf16[2,256,384]{2,1,0:T(8,128)(2,1)S(1)}, u32[]{:S(2)}, u32[]{:S(2)}) collective-permute-start(bf16[2,256,384]{2,1,0:T(8,128)(2,1)S(1)} %copy-done.9), channel_id=1, source_target_pairs={{13,0},{14,1},{15,2},{0,3},{1,4},{2,5},{3,6},{4,7},{5,8},{6,9},{7,... | collective-permute-start | bytes 1179656 | tf_op jit(solution)/shard_map/ppermute | solution.py:41
  57.0 33.0 %collective-permute-start.6 = (bf16[2,256,384]{2,1,0:T(8,128)(2,1)S(1)}, bf16[2,256,384]{2,1,0:T(8,128)(2,1)S(1)}, u32[]{:S(2)}, u32[]{:S(2)}) collective-permute-start(bf16[2,256,384]{2,1,0:T(8,128)(2,1)S(1)} %copy-done.8), channel_id=1, source_target_pairs={{1,0},{2,1},{3,2},{4,3},{5,4},{6,5},{7,6},{8,7},{9,8},{10,9},{11,1... | collective-permute-start | bytes 1179656 | tf_op jit(solution)/shard_map/ppermute | solution.py:41
  77.1 21.4 %collective-permute-start.10 = (bf16[512,256]{1,0:T(8,128)(2,1)S(1)}, bf16[512,256]{1,0:T(8,128)(2,1)S(1)}, u32[]{:S(2)}, u32[]{:S(2)}) collective-permute-start(bf16[512,256]{1,0:T(8,128)(2,1)S(1)} %attend.4.refs_4_), channel_id=1, source_target_pairs={{16,0},{0,16},{17,1},{1,17},{18,2},{2,18},{19,3},{3,19},{20,4},{4,... | collective-permute-start | bytes 786440 | tf_op jit(solution)/shard_map/ppermute | solution.py:32
  91.9 6.6 %collective-permute-start.11 = (bf16[512,128]{1,0:T(8,128)(2,1)S(1)}, bf16[512,128]{1,0:T(8,128)(2,1)S(1)}, u32[]{:S(2)}, u32[]{:S(2)}) collective-permute-start(bf16[512,128]{1,0:T(8,128)(2,1)S(1)} %attend.5.refs_5_), channel_id=1, source_target_pairs={{16,0},{0,16},{17,1},{1,17},{18,2},{2,18},{19,3},{3,19},{20,4},{4,... | collective-permute-start | bytes 393224 | tf_op jit(solution)/shard_map/ppermute | solution.py:32
  94.4 5.9 %collective-permute-start.12 = (bf16[512,128]{1,0:T(8,128)(2,1)S(1)}, bf16[512,128]{1,0:T(8,128)(2,1)S(1)}, u32[]{:S(2)}, u32[]{:S(2)}) collective-permute-start(bf16[512,128]{1,0:T(8,128)(2,1)S(1)} %attend.6.refs_6_), channel_id=1, source_target_pairs={{16,0},{0,16},{17,1},{1,17},{18,2},{2,18},{19,3},{3,19},{20,4},{4,... | collective-permute-start | bytes 393224 | tf_op jit(solution)/shard_map/ppermute | solution.py:32
  97.8 5.1 %collective-permute-start.13 = (bf16[512,128]{1,0:T(8,128)(2,1)S(1)}, bf16[512,128]{1,0:T(8,128)(2,1)S(1)}, u32[]{:S(2)}, u32[]{:S(2)}) collective-permute-start(bf16[512,128]{1,0:T(8,128)(2,1)S(1)} %attend.7.refs_7_), channel_id=1, source_target_pairs={{16,0},{0,16},{17,1},{1,17},{18,2},{2,18},{19,3},{3,19},{20,4},{4,... | collective-permute-start | bytes 393224 | tf_op jit(solution)/shard_map/ppermute | solution.py:32
  (3 other events, 32.1 us)

commit v2 on v0

--- a/solution.py
+++ b/solution.py
@@ -14,8 +14,8 @@
 LANES = 128
 GROUPS = (256, 384)
 UNITS = ((256,), (128, 128, 128))
-WINDOW = 4
-SLOT_ORDER = (2, 1, 3, 0)
+PARTS = 4
+SLOT_ORDER = (2, 1, 3)
 VMEM_LIMIT = 16 * 1024 * 1024
 FIRST_LIMIT = 58 * 1024 * 1024
 
@@ -73,10 +73,16 @@
 
 
 def split_kernel(kv_ref, hidden, out, sem):
-    rows = pl.ds(pl.multiple_of(kv_ref[0] * PAGE, PAGE), PAGE)
-    copy = pltpu.make_async_copy(hidden.at[rows], out, sem)
-    copy.start()
-    copy.wait()
+    part = PAGE // PARTS
+    copies = []
+    for i in range(PARTS):
+        rows = pl.ds(pl.multiple_of(kv_ref[0] * PAGE + i * part, part), part)
+        target = out.at[pl.ds(i * part, part)]
+        copies.append(pltpu.make_async_copy(hidden.at[rows], target, sem.at[i]))
+    for copy in copies:
+        copy.start()
+    for copy in copies:
+        copy.wait()
 
 
 def split_rows(hidden_in, kv_index):
@@ -85,7 +91,7 @@
         in_specs=[pl.BlockSpec(memory_space=pltpu.SMEM), pl.BlockSpec(memory_space=pltpu.HBM)],
         out_specs=pl.BlockSpec(memory_space=pltpu.VMEM),
         out_shape=jax.ShapeDtypeStruct((PAGE, hidden_in.shape[1]), bf16),
-        scratch_shapes=[pltpu.SemaphoreType.DMA],
+        scratch_shapes=[pltpu.SemaphoreType.DMA((PARTS,))],
         compiler_params=params(FIRST_LIMIT),
         cost_estimate=cost(),
         name="split_rows",
@@ -107,16 +113,19 @@
         for side in range(2):
             index = 2 * slot + side
             copies[index].wait()
+            if slot == 0:
+                outs[0][side] = buf[index]
+                continue
             for g, (start, size) in enumerate(slices):
-                outs[g * PMAX + slot][side] = buf[index, :, start : start + size]
+                outs[g * (PMAX - 1) + slot][side] = buf[index, :, start : start + size]
 
 
 def pack(pool_keys, pool_values, table, here, devices, offsets, first):
     width = pool_keys.shape[2]
     slices = group_slices(width)
-    outs = []
+    outs = [jax.ShapeDtypeStruct((2, PAGE, width), bf16)]
     for _, size in slices:
-        outs += [jax.ShapeDtypeStruct((2, PAGE, size), bf16)] * PMAX
+        outs += [jax.ShapeDtypeStruct((2, PAGE, size), bf16)] * (PMAX - 1)
     smem = pl.BlockSpec(memory_space=pltpu.SMEM)
     hbm = pl.BlockSpec(memory_space=pltpu.HBM)
     result = pl.pallas_call(
@@ -132,7 +141,8 @@
         cost_estimate=cost(),
         name="pack",
     )(here, table, pool_keys, pool_values, first)
-    return [result[PMAX * g : PMAX * (g + 1)] for g in range(len(slices))]
+    each = PMAX - 1
+    return result[0], [result[1 + each * g : 1 + each * (g + 1)] for g in range(len(slices))]
 
 
 def head_sum_matrix():
@@ -230,7 +240,7 @@
     )(kv_index, here, placement, mine, theirs, wk, wv, gain)
 
 
-def attend_kernel(inner, live_ref, depth_ref, q_ref, k_ref, v_ref, p0, p1, p2, p3, out):
+def attend_kernel(inner, base, live_ref, depth_ref, q_ref, k_ref, v_ref, p0, p1, p2, p3, out):
     pages = (p0, p1, p2, p3)
     tokens, width = q_ref.shape
     live, depth = live_ref[0], depth_ref[0]
@@ -242,7 +252,8 @@
     blocks = tokens // PAGE
     for start in range(0, width, LANES):
         cols = slice(start, start + LANES)
-        page_cols = slice(inner + start, inner + start + LANES)
+        firsts = (base,) + (inner,) * (PMAX - 1)
+        page_cols = [slice(first + start, first + start + LANES) for first in firsts]
         keys, values = [], []
         for b in range(blocks):
             rows = slice(b * PAGE, (b + 1) * PAGE)
@@ -253,9 +264,9 @@
             values.append(jnp.concatenate([shown, ones], axis=1))
         for p in range(PMAX):
             keep = jnp.where(p < depth, 1.0, 0.0).astype(bf16)
-            keys.append(pages[p][0, :, page_cols])
+            keys.append(pages[p][0, :, page_cols[p]])
             ones = jnp.full((PAGE, LANES), 1.0, bf16) * keep
-            values.append(jnp.concatenate([pages[p][1, :, page_cols] * keep, ones], axis=1))
+            values.append(jnp.concatenate([pages[p][1, :, page_cols[p]] * keep, ones], axis=1))
         for b in range(blocks):
             rows = slice(b * PAGE, (b + 1) * PAGE)
             q = q_ref[rows, cols]
@@ -275,14 +286,14 @@
             out[rows, cols] = jnp.where((lane // HD) == 0, ratios[0], ratios[1]).astype(bf16)
 
 
-def attend(live, depth, q, k, v, pages, inner):
+def attend(live, depth, q, k, v, pages, inner, base):
     tokens, width = q.shape
     heads = width // HD
     smem = pl.BlockSpec(memory_space=pltpu.SMEM)
     vmem = pl.BlockSpec(memory_space=pltpu.VMEM)
     keys = tokens + PMAX * PAGE
     return pl.pallas_call(
-        functools.partial(attend_kernel, inner),
+        functools.partial(attend_kernel, inner, base),
         in_specs=[smem, smem] + [vmem] * 7,
         out_specs=vmem,
         out_shape=jax.ShapeDtypeStruct((tokens, width), bf16),
@@ -292,46 +303,81 @@
     )(live, depth, q, k, v, *pages)
 
 
-def finish_kernel(slices, count, *refs):
-    hidden, w_mine, w_theirs, rate = refs[:4]
-    mine = refs[4 : 4 + count]
-    theirs = refs[4 + count : 4 + 2 * count]
-    out = refs[4 + 2 * count]
-
+def projected_heads(slices, rows, mine, theirs, w_mine, w_theirs):
     def half(parts, weights):
         total = None
         for part, (start, size) in zip(parts, slices):
-            term = jnp.dot(part[...], weights[start : start + size, :], preferred_element_type=f32)
+            weight = weights[start : start + size, :]
+            term = jnp.dot(part[rows, :], weight, preferred_element_type=f32)
             total = term if total is None else total + term
         return total
 
-    branch = half(mine, w_mine) + half(theirs, w_theirs)
-    hidden_f = hidden[...].astype(f32)
-    anchor = hidden_f * lax.rsqrt(jnp.mean(hidden_f * hidden_f, axis=-1, keepdims=True) + epsilon)
-    normed = branch * lax.rsqrt(jnp.mean(branch * branch, axis=-1, keepdims=True) + epsilon)
-    updated = anchor + rate[...] * (normed - anchor)
-    scale = lax.rsqrt(jnp.mean(updated * updated, axis=-1, keepdims=True) + epsilon)
-    out[...] = (updated * scale).astype(bf16)
-
-
-def finish(hidden_in, w_mine, w_theirs, rate, mine, theirs):
+    return half(mine, w_mine) + half(theirs, w_theirs)
+
+
+def partial_kernel(slices, w_mine, w_theirs, *refs):
+    count = len(slices)
+    mine, theirs, out = refs[:count], refs[count : 2 * count], refs[2 * count]
+    for low in range(0, out.shape[0], PAGE):
+        rows = slice(low, low + PAGE)
+        out[rows, :] = projected_heads(slices, rows, mine, theirs, w_mine, w_theirs)
+
+
+def partial_branch(slices, w_mine, w_theirs, mine, theirs):
+    tokens, depth = mine[0].shape[0], w_mine.shape[1]
+    vmem = pl.BlockSpec(memory_space=pltpu.VMEM)
+    return pl.pallas_call(
+        functools.partial(partial_kernel, slices),
+        in_specs=[vmem] * (2 + 2 * len(slices)),
+        out_specs=vmem,
+        out_shape=jax.ShapeDtypeStruct((tokens, depth), f32),
+        compiler_params=params(),
+        cost_estimate=cost(),
+        name="partial_branch",
+    )(w_mine, w_theirs, *mine, *theirs)
+
+
+def finish_kernel(slices, hidden, w_mine, w_theirs, rate, begun, *refs):
+    count = len(slices)
+    mine, theirs = refs[:count], refs[count : 2 * count]
+    out, buf, sem = refs[2 * count :]
+    step = buf.shape[1]
+    copies = []
+    for i in range(buf.shape[0]):
+        rows = slice(i * step, (i + 1) * step)
+        branch = begun[rows, :] + projected_heads(slices, rows, mine, theirs, w_mine, w_theirs)
+        hidden_f = hidden[rows, :].astype(f32)
+        mean = jnp.mean(hidden_f * hidden_f, axis=-1, keepdims=True)
+        anchor = hidden_f * lax.rsqrt(mean + epsilon)
+        mean = jnp.mean(branch * branch, axis=-1, keepdims=True)
+        normed = branch * lax.rsqrt(mean + epsilon)
+        updated = anchor + rate[...] * (normed - anchor)
+        scale = lax.rsqrt(jnp.mean(updated * updated, axis=-1, keepdims=True) + epsilon)
+        buf[i] = (updated * scale).astype(bf16)
+        copy = pltpu.make_async_copy(buf.at[i], out.at[pl.ds(i * step, step)], sem.at[i])
+        copy.start()
+        copies.append(copy)
+    for copy in copies:
+        copy.wait()
+
+
+def finish(slices, hidden_in, w_mine, w_theirs, rate, begun, mine, theirs):
     tokens, depth = hidden_in.shape
-    width = w_mine.shape[0]
-    slices = [(start, size) for _, _, start, size in unit_slices()]
-    step = 256
-    by_rows = lambda size: pl.BlockSpec((step, size), lambda i: (i, 0))
-    whole = lambda shape: pl.BlockSpec(shape, lambda i: (0, 0))
+    steps = 4
+    vmem = pl.BlockSpec(memory_space=pltpu.VMEM)
     return pl.pallas_call(
-        functools.partial(finish_kernel, slices, len(slices)),
-        grid=(tokens // step,),
-        in_specs=[by_rows(depth), whole(w_mine.shape), whole(w_theirs.shape), whole(rate.shape)]
-        + [by_rows(size) for _, size in slices] * 2,
-        out_specs=by_rows(depth),
+        functools.partial(finish_kernel, slices),
+        in_specs=[vmem] * (5 + 2 * len(slices)),
+        out_specs=pl.BlockSpec(memory_space=pltpu.HBM),
         out_shape=jax.ShapeDtypeStruct((tokens, depth), bf16),
+        scratch_shapes=[
+            pltpu.VMEM((steps, tokens // steps, depth), bf16),
+            pltpu.SemaphoreType.DMA((steps,)),
+        ],
         compiler_params=params(),
         cost_estimate=cost(),
         name="finish",
-    )(hidden_in, w_mine, w_theirs, rate, *mine, *theirs)
+    )(hidden_in, w_mine, w_theirs, rate, begun, *mine, *theirs)
 
 
 def body(
@@ -360,40 +406,42 @@
 
     assert blocks == lax.axis_size("kv") == 2
     relay_send = split_rows(hidden_in, kv_index)
-    page_send = pack(
+    near_send, far_send = pack(
         pool_keys, pool_values, prefix_pages.T, here, devices, page_offsets, relay_send
     )
-
     projected = project(hidden_in, w_query, w_key, w_value, gain)
 
-    sends = [(relay_send, block_offsets)]
-    for sent in page_send:
-        sends += [(sent[slot], [devices - page_offsets[slot]] * 2) for slot in SLOT_ORDER]
-    arrived = []
-    for index, (block, distance) in enumerate(sends):
-        if index >= WINDOW:
-            block = after(block, projected[0][0], *arrived[: index - WINDOW + 1])
-        arrived.append(over_blk(block, distance))
-    relay_mine = arrived[0]
-    pages = []
-    for g in range(len(page_send)):
-        first = 1 + g * PMAX
-        got = dict(zip(SLOT_ORDER, arrived[first : first + PMAX]))
-        pages.append([got[slot] for slot in range(PMAX)])
-    w_theirs = from_behind(after(w_out, page_send[0][2]), "kv", 1)
-    first_pages = arrived[1 : 1 + PMAX]
-    relay_theirs = from_behind(after(relay_mine, w_theirs, *first_pages), "kv", 1)
+    def fetch(block, slot):
+        return over_blk(block, [devices - page_offsets[slot]] * 2)
+
+    relay_mine = over_blk(relay_send, block_offsets)
+    first = {slot: fetch(far_send[0][slot - 1], slot) for slot in SLOT_ORDER}
+    arrived = [first[slot] for slot in SLOT_ORDER]
+    near = fetch(after(near_send, projected[0][0], relay_mine, *arrived), 0)
+    second = {}
+    for i, slot in enumerate(SLOT_ORDER):
+        second[slot] = fetch(after(far_send[1][slot - 1], projected[0][0], relay_mine, *arrived[: i + 1]), slot)
+    pages = [[near] + [got[slot] for slot in range(1, PMAX)] for got in (first, second)]
+    w_theirs = from_behind(w_out, "kv", 1)
+    relay_theirs = from_behind(after(relay_mine, w_theirs, *arrived), "kv", 1)
     new_keys, new_values = relay_project(
         relay_mine, relay_theirs, w_key, w_value, gain, kv_index, here, placement, block_offsets
     )
 
-    mine, theirs = [], []
-    for (g, inner, _, _), (q, k, v) in zip(unit_slices(), projected):
-        q = after(q, new_keys, theirs[0]) if g else q
-        attended = attend(req_len, prefix_len, q, k, v, pages[g], inner)
-        mine.append(attended)
-        theirs.append(from_behind(attended, "kv", 1))
-    layer_out = finish(hidden_in, w_out, w_theirs, rate, mine, theirs)
+    mine, theirs, slices = [[], []], [[], []], [[], []]
+    begun = None
+    for (g, inner, start, size), (q, k, v) in zip(unit_slices(), projected):
+        if g and begun is None:
+            begun = partial_branch(slices[0], w_out, w_theirs, mine[0], theirs[0])
+        if g:
+            q = after(q, new_keys, begun)
+        attended = attend(req_len, prefix_len, q, k, v, pages[g], inner, start)
+        mine[g].append(attended)
+        theirs[g].append(from_behind(attended, "kv", 1))
+        slices[g].append((start, size))
+    layer_out = finish(
+        slices[1], hidden_in, w_out, w_theirs, rate, begun, mine[1], theirs[1]
+    )
     return (layer_out, new_keys, new_values)
 
 

time: 107 us -> 108 us (level)
  the two profiles are of different devices: /device:TPU:0 before, /device:TPU:16 now
where the time goes in v2:
time: 108 us
  starting transfers between devices  40.1 us (37%)
  Pallas kernels  32.2 us (30%)
  waiting for transfers between devices  30.8 us (29%)
  between operations  2.24 us (2%)
  local copies, waits for them, and re-layouts  2.16 us (2%)
    ppermute x6, starting transfers between devices, from_behind(): return lax.ppermute(block, axis, route)  28.6 us
    ppermute x8, waiting for transfers between devices, over_blk(): return lax.ppermute(block, ('kv', 'blk'), route)  23.5 us
    ppermute x8, starting transfers between devices, over_blk(): return lax.ppermute(block, ('kv', 'blk'), route)  11.6 us
    pallas_call x4, Pallas kernels, attend(): pl.pallas_call(functools.partial(attend_kernel, inner, base), in_specs=[s...  9.17 us
    ppermute x6, waiting for transfers between devices, from_behind(): return lax.ppermute(block, axis, route)  7.31 us
    pallas_call x1, Pallas kernels, project(): pl.pallas_call(functools.partial(project_kernel, slices), out_shape=outs,...  6.95 us
    pallas_call x1, Pallas kernels, relay_project(): pl.pallas_call(functools.partial(relay_kernel, group_slices(width), block...  4.93 us
    pallas_call x1, Pallas kernels, pack(): pl.pallas_call(functools.partial(pack_kernel, slices, devices, offsets),...  4.13 us
  transfers between devices with their start and end apart: 14, of which 7 were waited for; matrix products, arithmetic and copies ran while one was open for 1% of the time, Pallas kernels for 24%

profile of v2, /device:TPU:16, one launch (start us, length us, event | category | flops | bytes accessed | tf_op | source)
XLA Modules:
  0.0 107.6 jit_solution(10258233426603532078)
XLA Ops:
  0.6 1.6 %collective-permute-start = (bf16[640,1280]{1,0:T(8,128)(2,1)}, bf16[640,1280]{1,0:T(8,128)(2,1)S(1)}, u32[]{:S(2)}, u32[]{:S(2)}) collective-permute-start(bf16[640,1280]{1,0:T(8,128)(2,1)} %w_mine.3), channel_id=1, source_target_pairs={{16,0},{0,16},{17,1},{1,17},{18,2},{2,18},{19,3},{3,19},{20,4},{4,... | collective-permute-start | bytes 4915208 | tf_op jit(solution)/shard_map/ppermute | solution.py:31
  2.2 2.1 %split_rows.1._ = bf16[256,1280]{1,0:T(8,128)(2,1)} custom-call(s32[1]{0:T(128)} %bitcast.2.kv_ref, bf16[512,1280]{1,0:T(8,128)(2,1)} %hidden.5), custom_call_target="tpu_custom_call" | custom-call | flops 1 | bytes 1 | tf_op jit(solution)/shard_map/split_rows/pallas_call | solution.py:89
  4.4 1.6 %collective-permute-start.1 = (bf16[256,1280]{1,0:T(8,128)(2,1)}, bf16[256,1280]{1,0:T(8,128)(2,1)}, u32[]{:S(2)}, u32[]{:S(2)}) collective-permute-start(bf16[256,1280]{1,0:T(8,128)(2,1)} %split_rows.1._), channel_id=1, source_target_pairs={{12,0},{13,1},{14,2},{15,3},{0,4},{1,5},{2,6},{3,7},{4,8},{5,9},{6... | collective-permute-start | bytes 1966088 | tf_op jit(solution)/shard_map/ppermute | solution.py:40
  6.0 4.1 %pack.1 = (bf16[2,256,640]{2,1,0:T(8,128)(2,1)}, bf16[2,256,256]{2,1,0:T(8,128)(2,1)}, bf16[2,256,256]{2,1,0:T(8,128)(2,1)}, bf16[2,256,256]{2,1,0:T(8,128)(2,1)...) custom-call(s32[1]{0:T(128)} %bitcast.here_ref, s32[4,16]{1,0:T(4,128)} %bitcast.3, ...), custom_call_target="tpu_custom_call" | custom-call | flops 1 | bytes 1 | tf_op jit(solution)/shard_map/pack/pallas_call | solution.py:131
  10.3 3.4 %collective-permute-start.3 = (bf16[2,256,256]{2,1,0:T(8,128)(2,1)}, bf16[2,256,256]{2,1,0:T(8,128)(2,1)S(1)}, u32[]{:S(2)}, u32[]{:S(2)}) collective-permute-start(bf16[2,256,256]{2,1,0:T(8,128)(2,1)} %get-tuple-element.37), channel_id=1, source_target_pairs={{5,0},{6,1},{7,2},{8,3},{9,4},{10,5},{11,6},{12,7},{13,8},{14,9},{... | collective-permute-start | bytes 786440 | tf_op jit(solution)/shard_map/ppermute | solution.py:40
  15.9 7.0 %project.1 = (bf16[512,256]{1,0:T(8,128)(2,1)S(1)}, bf16[512,256]{1,0:T(8,128)(2,1)S(1)}, bf16[512,256]{1,0:T(8,128)(2,1)S(1)}, bf16[512,128]{1,0:T(8,128)(2,1)S...) custom-call(bf16[512,1280]{1,0:T(8,128)(2,1)S(1)} %copy-done, ...), custom_call_target="tpu_custom_call" | custom-call | flops 1 | bytes 1 | tf_op jit(solution)/shard_map/project/pallas_call | solution.py:197
  22.8 8.0 %collective-permute-done.2.p2 = bf16[2,256,256]{2,1,0:T(8,128)(2,1)S(1)} collective-permute-done((bf16[2,256,256]{2,1,0:T(8,128)(2,1)}, bf16[2,256,256]{2,1,0:T(8,128)(2,1)S(1)}, u32[]{:S(2)}, u32[]{:S(2)}) %collective-permute-start.2) | collective-permute-done | bytes 262176 | tf_op jit(solution)/shard_map/ppermute | solution.py:40
  30.8 5.9 %collective-permute-done.3.p1 = bf16[2,256,256]{2,1,0:T(8,128)(2,1)S(1)} collective-permute-done((bf16[2,256,256]{2,1,0:T(8,128)(2,1)}, bf16[2,256,256]{2,1,0:T(8,128)(2,1)S(1)}, u32[]{:S(2)}, u32[]{:S(2)}) %collective-permute-start.3) | collective-permute-done | bytes 262176 | tf_op jit(solution)/shard_map/ppermute | solution.py:40
  36.7 2.3 %collective-permute-done.4.p3 = bf16[2,256,256]{2,1,0:T(8,128)(2,1)S(1)} collective-permute-done((bf16[2,256,256]{2,1,0:T(8,128)(2,1)}, bf16[2,256,256]{2,1,0:T(8,128)(2,1)S(1)}, u32[]{:S(2)}, u32[]{:S(2)}) %collective-permute-start.4) | collective-permute-done | bytes 262176 | tf_op jit(solution)/shard_map/ppermute | solution.py:40
  39.0 3.1 %collective-permute-start.5 = (bf16[2,256,640]{2,1,0:T(8,128)(2,1)S(1)}, bf16[2,256,640]{2,1,0:T(8,128)(2,1)S(1)}, u32[]{:S(2)}, u32[]{:S(2)}) collective-permute-start(bf16[2,256,640]{2,1,0:T(8,128)(2,1)S(1)} %copy-done.7), channel_id=1, source_target_pairs={{1,0},{2,1},{3,2},{4,3},{5,4},{6,5},{7,6},{8,7},{9,8},{10,9},{11,1... | collective-permute-start | bytes 1966088 | tf_op jit(solution)/shard_map/ppermute | solution.py:40
  42.2 3.9 %collective-permute-start.7 = (bf16[256,1280]{1,0:T(8,128)(2,1)}, bf16[256,1280]{1,0:T(8,128)(2,1)S(1)}, u32[]{:S(2)}, u32[]{:S(2)}) collective-permute-start(bf16[256,1280]{1,0:T(8,128)(2,1)} %collective-permute-done.1.refs_0_), channel_id=1, source_target_pairs={{16,0},{0,16},{17,1},{1,17},{18,2},{2,18},{19,3},{3,19},{20,4},{4,... | collective-permute-start | bytes 1966088 | tf_op jit(solution)/shard_map/ppermute | solution.py:31
  47.8 1.6 %collective-permute-start.9 = (bf16[2,256,384]{2,1,0:T(8,128)(2,1)S(1)}, bf16[2,256,384]{2,1,0:T(8,128)(2,1)S(1)}, u32[]{:S(2)}, u32[]{:S(2)}) collective-permute-start(bf16[2,256,384]{2,1,0:T(8,128)(2,1)S(1)} %copy-done.8), channel_id=1, source_target_pairs={{9,0},{10,1},{11,2},{12,3},{13,4},{14,5},{15,6},{0,7},{1,8},{2,9},... | collective-permute-start | bytes 1179656 | tf_op jit(solution)/shard_map/ppermute | solution.py:40
  50.6 7.3 %collective-permute-done.5.p0 = bf16[2,256,640]{2,1,0:T(8,128)(2,1)S(1)} collective-permute-done((bf16[2,256,640]{2,1,0:T(8,128)(2,1)S(1)}, bf16[2,256,640]{2,1,0:T(8,128)(2,1)S(1)}, u32[]{:S(2)}, u32[]{:S(2)}) %collective-permute-start.5) | collective-permute-done | bytes 655392 | tf_op jit(solution)/shard_map/ppermute | solution.py:40
  58.0 3.4 %attend.4.refs_0_ = bf16[512,256]{1,0:T(8,128)(2,1)S(1)} custom-call(s32[1]{0:T(128)S(6)} %copy.16.live_ref, s32[1]{0:T(128)S(6)} %copy.17.depth_ref, bf16[512,256]{1,0:T(8,128)(2,1)S(1)} %get-tuple-element.32.q_ref, bf16[512,256]{1,0:T(8,128)(2,1)S(1)} %get-tuple-element.33.k_ref, bf16[512,256]{1,0:T(8,128)(2,1)S(1)} %get-tuple-element.34.v_ref, ...), custom_call_target="tpu_custom_call" | custom-call | flops 1 | bytes 1 | tf_op jit(solution)/shard_map/attend/pallas_call | solution.py:295
  61.3 18.8 %collective-permute-start.6 = (bf16[512,256]{1,0:T(8,128)(2,1)S(1)}, bf16[512,256]{1,0:T(8,128)(2,1)S(1)}, u32[]{:S(2)}, u32[]{:S(2)}) collective-permute-start(bf16[512,256]{1,0:T(8,128)(2,1)S(1)} %attend.4.refs_0_), channel_id=1, source_target_pairs={{16,0},{0,16},{17,1},{1,17},{18,2},{2,18},{19,3},{3,19},{20,4},{4,... | collective-permute-start | bytes 786440 | tf_op jit(solution)/shard_map/ppermute | solution.py:31
  80.1 4.4 %collective-permute-done.6.refs_1_ = bf16[512,256]{1,0:T(8,128)(2,1)S(1)} collective-permute-done((bf16[512,256]{1,0:T(8,128)(2,1)S(1)}, bf16[512,256]{1,0:T(8,128)(2,1)S(1)}, u32[]{:S(2)}, u32[]{:S(2)}) %collective-permute-start.6) | collective-permute-done | bytes 262176 | tf_op jit(solution)/shard_map/ppermute | solution.py:31
  85.3 4.9 %relay_project.1 = (bf16[2,256,640]{2,1,0:T(8,128)(2,1)}, bf16[2,256,640]{2,1,0:T(8,128)(2,1)}) custom-call(s32[1]{0:T(128)} %bitcast.2.kv_ref, s32[1]{0:T(128)} %bitcast.here_ref, s32[32]{0:T(128)S(1)} %copy-done.5, bf16[256,1280]{1,0:T(8,128)(2,1)} %collective-permute-done.1.refs_0_, bf16[256,1280]{1,0:T(8,128)(2,1)S(1)} %collective-permute-done.7.refs_1_, ...), custom_call_target="tpu_custom_call" | custom-call | flops 1 | bytes 1 | tf_op jit(solution)/shard_map/relay_project/pallas_call | solution.py:230
  90.3 1.9 %attend.5.refs_0_ = bf16[512,128]{1,0:T(8,128)(2,1)S(1)} custom-call(s32[1]{0:T(128)S(6)} %copy.16.live_ref, s32[1]{0:T(128)S(6)} %copy.17.depth_ref, bf16[512,128]{1,0:T(8,128)(2,1)S(1)} %get-tuple-element.43.q_ref, bf16[512,128]{1,0:T(8,128)(2,1)S(1)} %get-tuple-element.44.k_ref, bf16[512,128]{1,0:T(8,128)(2,1)S(1)} %get-tuple-element.45.v_ref, ...), custom_call_target="tpu_custom_call" | custom-call | flops 1 | bytes 1 | tf_op jit(solution)/shard_map/attend/pallas_call | solution.py:295
  92.2 2.1 %collective-permute-start.11 = (bf16[512,128]{1,0:T(8,128)(2,1)S(1)}, bf16[512,128]{1,0:T(8,128)(2,1)S(1)}, u32[]{:S(2)}, u32[]{:S(2)}) collective-permute-start(bf16[512,128]{1,0:T(8,128)(2,1)S(1)} %attend.5.refs_0_), channel_id=1, source_target_pairs={{16,0},{0,16},{17,1},{1,17},{18,2},{2,18},{19,3},{3,19},{20,4},{4,... | collective-permute-start | bytes 393224 | tf_op jit(solution)/shard_map/ppermute | solution.py:31
  94.3 1.9 %attend.6.refs_1_ = bf16[512,128]{1,0:T(8,128)(2,1)S(1)} custom-call(s32[1]{0:T(128)S(6)} %copy.16.live_ref, s32[1]{0:T(128)S(6)} %copy.17.depth_ref, bf16[512,128]{1,0:T(8,128)(2,1)S(1)} %get-tuple-element.53.q_ref, bf16[512,128]{1,0:T(8,128)(2,1)S(1)} %get-tuple-element.54.k_ref, bf16[512,128]{1,0:T(8,128)(2,1)S(1)} %get-tuple-element.55.v_ref, ...), custom_call_target="tpu_custom_call" | custom-call | flops 1 | bytes 1 | tf_op jit(solution)/shard_map/attend/pallas_call | solution.py:295
  96.2 2.1 %attend.7.refs_2_ = bf16[512,128]{1,0:T(8,128)(2,1)S(1)} custom-call(s32[1]{0:T(128)S(6)} %copy.16.live_ref, s32[1]{0:T(128)S(6)} %copy.17.depth_ref, bf16[512,128]{1,0:T(8,128)(2,1)S(1)} %get-tuple-element.57.q_ref, bf16[512,128]{1,0:T(8,128)(2,1)S(1)} %get-tuple-element.58.k_ref, bf16[512,128]{1,0:T(8,128)(2,1)S(1)} %get-tuple-element.59.v_ref, ...), custom_call_target="tpu_custom_call" | custom-call | flops 1 | bytes 1 | tf_op jit(solution)/shard_map/attend/pallas_call | solution.py:295
  98.3 2.1 %collective-permute-start.13 = (bf16[512,128]{1,0:T(8,128)(2,1)S(1)}, bf16[512,128]{1,0:T(8,128)(2,1)S(1)}, u32[]{:S(2)}, u32[]{:S(2)}) collective-permute-start(bf16[512,128]{1,0:T(8,128)(2,1)S(1)} %attend.7.refs_2_), channel_id=1, source_target_pairs={{16,0},{0,16},{17,1},{1,17},{18,2},{2,18},{19,3},{3,19},{20,4},{4,... | collective-permute-start | bytes 393224 | tf_op jit(solution)/shard_map/ppermute | solution.py:31
  101.2 2.2 %collective-permute-done.13.refs_5_ = bf16[512,128]{1,0:T(8,128)(2,1)S(1)} collective-permute-done((bf16[512,128]{1,0:T(8,128)(2,1)S(1)}, bf16[512,128]{1,0:T(8,128)(2,1)S(1)}, u32[]{:S(2)}, u32[]{:S(2)}) %collective-permute-start.13) | collective-permute-done | bytes 131104 | tf_op jit(solution)/shard_map/ppermute | solution.py:31
  103.3 4.0 %finish.1 = bf16[512,1280]{1,0:T(8,128)(2,1)} custom-call(bf16[512,1280]{1,0:T(8,128)(2,1)S(1)} %copy-done, bf16[640,1280]{1,0:T(8,128)(2,1)S(1)} %copy-done.3, bf16[640,1280]{1,0:T(8,128)(2,1)S(1)} %collective-permute-done.w_theirs, f32[1,1280]{1,0:T(1,128)S(1)} %reshape.18.rate, f32[512,1280]{1,0:T(8,128)S(1)} %partial_branch.1.begun, ...), custom_call_target="tpu_custom_call" | custom-call | flops 1 | bytes 1 | tf_op jit(solution)/shard_map/finish/pallas_call | solution.py:368
  (38 shorter events, 5.7 us)
Async XLA Ops:
  0.6 41.5 %collective-permute-start = (bf16[640,1280]{1,0:T(8,128)(2,1)}, bf16[640,1280]{1,0:T(8,128)(2,1)S(1)}, u32[]{:S(2)}, u32[]{:S(2)}) collective-permute-start(bf16[640,1280]{1,0:T(8,128)(2,1)} %w_mine.3), channel_id=1, source_target_pairs={{16,0},{0,16},{17,1},{1,17},{18,2},{2,18},{19,3},{3,19},{20,4},{4,... | collective-permute-start | bytes 4915208 | tf_op jit(solution)/shard_map/ppermute | solution.py:31
  2.2 12.2 %copy-start.2 = (bf16[1280,640]{1,0:T(8,128)(2,1)S(1)}, bf16[1280,640]{1,0:T(8,128)(2,1)}, u32[]{:S(2)}) copy-start(bf16[1280,640]{1,0:T(8,128)(2,1)} %refs_3_.1) | copy-start | bytes 4915204
  4.4 34.7 %collective-permute-start.1 = (bf16[256,1280]{1,0:T(8,128)(2,1)}, bf16[256,1280]{1,0:T(8,128)(2,1)}, u32[]{:S(2)}, u32[]{:S(2)}) collective-permute-start(bf16[256,1280]{1,0:T(8,128)(2,1)} %split_rows.1._), channel_id=1, source_target_pairs={{12,0},{13,1},{14,2},{15,3},{0,4},{1,5},{2,6},{3,7},{4,8},{5,9},{6... | collective-permute-start | bytes 1966088 | tf_op jit(solution)/shard_map/ppermute | solution.py:40
  6.0 8.4 %copy-start = (bf16[512,1280]{1,0:T(8,128)(2,1)S(1)}, bf16[512,1280]{1,0:T(8,128)(2,1)}, u32[]{:S(2)}) copy-start(bf16[512,1280]{1,0:T(8,128)(2,1)} %hidden.5) | copy-start | bytes 3932164
  6.0 8.4 %copy-start.1 = (bf16[1280,640]{1,0:T(8,128)(2,1)S(1)}, bf16[1280,640]{1,0:T(8,128)(2,1)}, u32[]{:S(2)}) copy-start(bf16[1280,640]{1,0:T(8,128)(2,1)} %refs_2_.1) | copy-start | bytes 4915204
  10.1 20.7 %collective-permute-start.2 = (bf16[2,256,256]{2,1,0:T(8,128)(2,1)}, bf16[2,256,256]{2,1,0:T(8,128)(2,1)S(1)}, u32[]{:S(2)}, u32[]{:S(2)}) collective-permute-start(bf16[2,256,256]{2,1,0:T(8,128)(2,1)} %get-tuple-element.36), channel_id=1, source_target_pairs={{9,0},{10,1},{11,2},{12,3},{13,4},{14,5},{15,6},{0,7},{1,8},{2,9},... | collective-permute-start | bytes 786440 | tf_op jit(solution)/shard_map/ppermute | solution.py:40
  10.3 26.4 %collective-permute-start.3 = (bf16[2,256,256]{2,1,0:T(8,128)(2,1)}, bf16[2,256,256]{2,1,0:T(8,128)(2,1)S(1)}, u32[]{:S(2)}, u32[]{:S(2)}) collective-permute-start(bf16[2,256,256]{2,1,0:T(8,128)(2,1)} %get-tuple-element.37), channel_id=1, source_target_pairs={{5,0},{6,1},{7,2},{8,3},{9,4},{10,5},{11,6},{12,7},{13,8},{14,9},{... | collective-permute-start | bytes 786440 | tf_op jit(solution)/shard_map/ppermute | solution.py:40
  13.7 25.3 %collective-permute-start.4 = (bf16[2,256,256]{2,1,0:T(8,128)(2,1)}, bf16[2,256,256]{2,1,0:T(8,128)(2,1)S(1)}, u32[]{:S(2)}, u32[]{:S(2)}) collective-permute-start(bf16[2,256,256]{2,1,0:T(8,128)(2,1)} %get-tuple-element.38), channel_id=1, source_target_pairs={{13,0},{14,1},{15,2},{0,3},{1,4},{2,5},{3,6},{4,7},{5,8},{6,9},{7,... | collective-permute-start | bytes 786440 | tf_op jit(solution)/shard_map/ppermute | solution.py:40
  15.9 23.2 %copy-start.7 = (bf16[2,256,640]{2,1,0:T(8,128)(2,1)S(1)}, bf16[2,256,640]{2,1,0:T(8,128)(2,1)}, u32[]{:S(2)}) copy-start(bf16[2,256,640]{2,1,0:T(8,128)(2,1)} %get-tuple-element.39) | copy-start | bytes 1966084
  15.9 30.3 %copy-start.10 = (bf16[2,256,384]{2,1,0:T(8,128)(2,1)S(1)}, bf16[2,256,384]{2,1,0:T(8,128)(2,1)}, u32[]{:S(2)}) copy-start(bf16[2,256,384]{2,1,0:T(8,128)(2,1)} %get-tuple-element.51) | copy-start | bytes 1179652
  15.9 31.2 %copy-start.9 = (bf16[2,256,384]{2,1,0:T(8,128)(2,1)S(1)}, bf16[2,256,384]{2,1,0:T(8,128)(2,1)}, u32[]{:S(2)}) copy-start(bf16[2,256,384]{2,1,0:T(8,128)(2,1)} %get-tuple-element.47) | copy-start | bytes 1179652
  15.9 31.9 %copy-start.8 = (bf16[2,256,384]{2,1,0:T(8,128)(2,1)S(1)}, bf16[2,256,384]{2,1,0:T(8,128)(2,1)}, u32[]{:S(2)}) copy-start(bf16[2,256,384]{2,1,0:T(8,128)(2,1)} %get-tuple-element.49) | copy-start | bytes 1179652
  22.8 61.6 %copy-start.3 = (bf16[640,1280]{1,0:T(8,128)(2,1)S(1)}, bf16[640,1280]{1,0:T(8,128)(2,1)}, u32[]{:S(2)}) copy-start(bf16[640,1280]{1,0:T(8,128)(2,1)} %w_mine.3) | copy-start | bytes 4915204
  39.0 18.9 %collective-permute-start.5 = (bf16[2,256,640]{2,1,0:T(8,128)(2,1)S(1)}, bf16[2,256,640]{2,1,0:T(8,128)(2,1)S(1)}, u32[]{:S(2)}, u32[]{:S(2)}) collective-permute-start(bf16[2,256,640]{2,1,0:T(8,128)(2,1)S(1)} %copy-done.7), channel_id=1, source_target_pairs={{1,0},{2,1},{3,2},{4,3},{5,4},{6,5},{7,6},{8,7},{9,8},{10,9},{11,1... | collective-permute-start | bytes 1966088 | tf_op jit(solution)/shard_map/ppermute | solution.py:40
  42.2 43.2 %collective-permute-start.7 = (bf16[256,1280]{1,0:T(8,128)(2,1)}, bf16[256,1280]{1,0:T(8,128)(2,1)S(1)}, u32[]{:S(2)}, u32[]{:S(2)}) collective-permute-start(bf16[256,1280]{1,0:T(8,128)(2,1)} %collective-permute-done.1.refs_0_), channel_id=1, source_target_pairs={{16,0},{0,16},{17,1},{1,17},{18,2},{2,18},{19,3},{3,19},{20,4},{4,... | collective-permute-start | bytes 1966088 | tf_op jit(solution)/shard_map/ppermute | solution.py:31
  46.1 44.2 %collective-permute-start.10 = (bf16[2,256,384]{2,1,0:T(8,128)(2,1)S(1)}, bf16[2,256,384]{2,1,0:T(8,128)(2,1)S(1)}, u32[]{:S(2)}, u32[]{:S(2)}) collective-permute-start(bf16[2,256,384]{2,1,0:T(8,128)(2,1)S(1)} %copy-done.10), channel_id=1, source_target_pairs={{13,0},{14,1},{15,2},{0,3},{1,4},{2,5},{3,6},{4,7},{5,8},{6,9},{7,... | collective-permute-start | bytes 1179656 | tf_op jit(solution)/shard_map/ppermute | solution.py:40
  47.1 43.2 %collective-permute-start.8 = (bf16[2,256,384]{2,1,0:T(8,128)(2,1)S(1)}, bf16[2,256,384]{2,1,0:T(8,128)(2,1)S(1)}, u32[]{:S(2)}, u32[]{:S(2)}) collective-permute-start(bf16[2,256,384]{2,1,0:T(8,128)(2,1)S(1)} %copy-done.9), channel_id=1, source_target_pairs={{5,0},{6,1},{7,2},{8,3},{9,4},{10,5},{11,6},{12,7},{13,8},{14,9},{... | collective-permute-start | bytes 1179656 | tf_op jit(solution)/shard_map/ppermute | solution.py:40
  47.8 42.5 %collective-permute-start.9 = (bf16[2,256,384]{2,1,0:T(8,128)(2,1)S(1)}, bf16[2,256,384]{2,1,0:T(8,128)(2,1)S(1)}, u32[]{:S(2)}, u32[]{:S(2)}) collective-permute-start(bf16[2,256,384]{2,1,0:T(8,128)(2,1)S(1)} %copy-done.8), channel_id=1, source_target_pairs={{9,0},{10,1},{11,2},{12,3},{13,4},{14,5},{15,6},{0,7},{1,8},{2,9},... | collective-permute-start | bytes 1179656 | tf_op jit(solution)/shard_map/ppermute | solution.py:40
  61.3 24.0 %copy-start.5 = (s32[32]{0:T(128)S(1)}, s32[32]{0:T(128)}, u32[]{:S(2)}) copy-start(s32[32]{0:T(128)} %placement.1) | copy-start | bytes 388
  61.3 23.1 %collective-permute-start.6 = (bf16[512,256]{1,0:T(8,128)(2,1)S(1)}, bf16[512,256]{1,0:T(8,128)(2,1)S(1)}, u32[]{:S(2)}, u32[]{:S(2)}) collective-permute-start(bf16[512,256]{1,0:T(8,128)(2,1)S(1)} %attend.4.refs_0_), channel_id=1, source_target_pairs={{16,0},{0,16},{17,1},{1,17},{18,2},{2,18},{19,3},{3,19},{20,4},{4,... | collective-permute-start | bytes 786440 | tf_op jit(solution)/shard_map/ppermute | solution.py:31
  92.2 8.2 %collective-permute-start.11 = (bf16[512,128]{1,0:T(8,128)(2,1)S(1)}, bf16[512,128]{1,0:T(8,128)(2,1)S(1)}, u32[]{:S(2)}, u32[]{:S(2)}) collective-permute-start(bf16[512,128]{1,0:T(8,128)(2,1)S(1)} %attend.5.refs_0_), channel_id=1, source_target_pairs={{16,0},{0,16},{17,1},{1,17},{18,2},{2,18},{19,3},{3,19},{20,4},{4,... | collective-permute-start | bytes 393224 | tf_op jit(solution)/shard_map/ppermute | solution.py:31
  96.1 4.3 %copy-start.6 = (f32[1280]{0:T(1024)S(1)}, f32[1280]{0:T(1024)}, u32[]{:S(2)}) copy-start(f32[1280]{0:T(1024)} %param.19) | copy-start | bytes 15364
  96.1 5.0 %collective-permute-start.12 = (bf16[512,128]{1,0:T(8,128)(2,1)S(1)}, bf16[512,128]{1,0:T(8,128)(2,1)S(1)}, u32[]{:S(2)}, u32[]{:S(2)}) collective-permute-start(bf16[512,128]{1,0:T(8,128)(2,1)S(1)} %attend.6.refs_1_), channel_id=1, source_target_pairs={{16,0},{0,16},{17,1},{1,17},{18,2},{2,18},{19,3},{3,19},{20,4},{4,... | collective-permute-start | bytes 393224 | tf_op jit(solution)/shard_map/ppermute | solution.py:31
  98.3 5.0 %collective-permute-start.13 = (bf16[512,128]{1,0:T(8,128)(2,1)S(1)}, bf16[512,128]{1,0:T(8,128)(2,1)S(1)}, u32[]{:S(2)}, u32[]{:S(2)}) collective-permute-start(bf16[512,128]{1,0:T(8,128)(2,1)S(1)} %attend.7.refs_2_), channel_id=1, source_target_pairs={{16,0},{0,16},{17,1},{1,17},{18,2},{2,18},{19,3},{3,19},{20,4},{4,... | collective-permute-start | bytes 393224 | tf_op jit(solution)/shard_map/ppermute | solution.py:31
  (1 other events, 1.4 us)

commit v3 on v2

--- a/solution.py
+++ b/solution.py
@@ -415,9 +415,14 @@
         return over_blk(block, [devices - page_offsets[slot]] * 2)
 
     relay_mine = over_blk(relay_send, block_offsets)
-    first = {slot: fetch(far_send[0][slot - 1], slot) for slot in SLOT_ORDER}
+    near = fetch(near_send, 0)
+    first = {}
+    for slot in SLOT_ORDER:
+        block = far_send[0][slot - 1]
+        if slot == SLOT_ORDER[-1]:
+            block = after(block, projected[0][0], near, relay_mine)
+        first[slot] = fetch(block, slot)
     arrived = [first[slot] for slot in SLOT_ORDER]
-    near = fetch(after(near_send, projected[0][0], relay_mine, *arrived), 0)
     second = {}
     for i, slot in enumerate(SLOT_ORDER):
         second[slot] = fetch(after(far_send[1][slot - 1], projected[0][0], relay_mine, *arrived[: i + 1]), slot)

time: 108 us -> 104 us (0.963)
  the two profiles are of different devices: /device:TPU:16 before, /device:TPU:1 now
where the time goes in v3:
time: 104 us
  starting transfers between devices  38.3 us (37%)
  Pallas kernels  32.2 us (31%)
  waiting for transfers between devices  29.1 us (28%)
  between operations  2.27 us (2%)
  local copies, waits for them, and re-layouts  2.16 us (2%)
    ppermute x8, starting transfers between devices, over_blk(): return lax.ppermute(block, ('kv', 'blk'), route)  32.5 us
    ppermute x8, waiting for transfers between devices, over_blk(): return lax.ppermute(block, ('kv', 'blk'), route)  21.7 us
    pallas_call x4, Pallas kernels, attend(): pl.pallas_call(functools.partial(attend_kernel, inner, base), in_specs=[s...  9.18 us
    ppermute x6, waiting for transfers between devices, from_behind(): return lax.ppermute(block, axis, route)  7.42 us
    pallas_call x1, Pallas kernels, project(): pl.pallas_call(functools.partial(project_kernel, slices), out_shape=outs,...  6.98 us
    ppermute x6, starting transfers between devices, from_behind(): return lax.ppermute(block, axis, route)  5.81 us
    pallas_call x1, Pallas kernels, relay_project(): pl.pallas_call(functools.partial(relay_kernel, group_slices(width), block...  4.93 us
    pallas_call x1, Pallas kernels, pack(): pl.pallas_call(functools.partial(pack_kernel, slices, devices, offsets),...  4.09 us
  transfers between devices with their start and end apart: 14, of which 5 were waited for; matrix products, arithmetic and copies ran while one was open for 1% of the time, Pallas kernels for 25%

profile of v3, /device:TPU:1, one launch (start us, length us, event | category | flops | bytes accessed | tf_op | source)
XLA Modules:
  0.0 104.0 jit_solution(16109105737874148793)
XLA Ops:
  0.6 2.1 %collective-permute-start = (bf16[640,1280]{1,0:T(8,128)(2,1)}, bf16[640,1280]{1,0:T(8,128)(2,1)S(1)}, u32[]{:S(2)}, u32[]{:S(2)}) collective-permute-start(bf16[640,1280]{1,0:T(8,128)(2,1)} %w_mine.3), channel_id=1, source_target_pairs={{16,0},{0,16},{17,1},{1,17},{18,2},{2,18},{19,3},{3,19},{20,4},{4,... | collective-permute-start | bytes 4915208 | tf_op jit(solution)/shard_map/ppermute | solution.py:31
  2.8 2.1 %split_rows.1._ = bf16[256,1280]{1,0:T(8,128)(2,1)} custom-call(s32[1]{0:T(128)} %bitcast.2.kv_ref, bf16[512,1280]{1,0:T(8,128)(2,1)} %hidden.5), custom_call_target="tpu_custom_call" | custom-call | flops 1 | bytes 1 | tf_op jit(solution)/shard_map/split_rows/pallas_call | solution.py:89
  4.9 1.3 %collective-permute-start.4 = (bf16[256,1280]{1,0:T(8,128)(2,1)}, bf16[256,1280]{1,0:T(8,128)(2,1)}, u32[]{:S(2)}, u32[]{:S(2)}) collective-permute-start(bf16[256,1280]{1,0:T(8,128)(2,1)} %split_rows.1._), channel_id=1, source_target_pairs={{12,0},{13,1},{14,2},{15,3},{0,4},{1,5},{2,6},{3,7},{4,8},{5,9},{6... | collective-permute-start | bytes 1966088 | tf_op jit(solution)/shard_map/ppermute | solution.py:40
  6.3 4.1 %pack.1 = (bf16[2,256,640]{2,1,0:T(8,128)(2,1)}, bf16[2,256,256]{2,1,0:T(8,128)(2,1)}, bf16[2,256,256]{2,1,0:T(8,128)(2,1)}, bf16[2,256,256]{2,1,0:T(8,128)(2,1)...) custom-call(s32[1]{0:T(128)} %bitcast.here_ref, s32[4,16]{1,0:T(4,128)} %bitcast.3, ...), custom_call_target="tpu_custom_call" | custom-call | flops 1 | bytes 1 | tf_op jit(solution)/shard_map/pack/pallas_call | solution.py:131
  10.4 1.3 %collective-permute-start.1 = (bf16[2,256,640]{2,1,0:T(8,128)(2,1)}, bf16[2,256,640]{2,1,0:T(8,128)(2,1)S(1)}, u32[]{:S(2)}, u32[]{:S(2)}) collective-permute-start(bf16[2,256,640]{2,1,0:T(8,128)(2,1)} %get-tuple-element.35), channel_id=1, source_target_pairs={{1,0},{2,1},{3,2},{4,3},{5,4},{6,5},{7,6},{8,7},{9,8},{10,9},{11,1... | collective-permute-start | bytes 1966088 | tf_op jit(solution)/shard_map/ppermute | solution.py:40
  11.7 3.5 %collective-permute-start.2 = (bf16[2,256,256]{2,1,0:T(8,128)(2,1)}, bf16[2,256,256]{2,1,0:T(8,128)(2,1)S(1)}, u32[]{:S(2)}, u32[]{:S(2)}) collective-permute-start(bf16[2,256,256]{2,1,0:T(8,128)(2,1)} %get-tuple-element.36), channel_id=1, source_target_pairs={{5,0},{6,1},{7,2},{8,3},{9,4},{10,5},{11,6},{12,7},{13,8},{14,9},{... | collective-permute-start | bytes 786440 | tf_op jit(solution)/shard_map/ppermute | solution.py:40
  16.0 1.4 %copy-done.4 = bf16[1280,640]{1,0:T(8,128)(2,1)S(1)} copy-done((bf16[1280,640]{1,0:T(8,128)(2,1)S(1)}, bf16[1280,640]{1,0:T(8,128)(2,1)}, u32[]{:S(2)}) %copy-start.4) | copy-done | bytes 1638424
  17.4 7.0 %project.1 = (bf16[512,256]{1,0:T(8,128)(2,1)S(1)}, bf16[512,256]{1,0:T(8,128)(2,1)S(1)}, bf16[512,256]{1,0:T(8,128)(2,1)S(1)}, bf16[512,128]{1,0:T(8,128)(2,1)S...) custom-call(bf16[512,1280]{1,0:T(8,128)(2,1)S(1)} %copy-done, ...), custom_call_target="tpu_custom_call" | custom-call | flops 1 | bytes 1 | tf_op jit(solution)/shard_map/project/pallas_call | solution.py:197
  24.5 15.2 %collective-permute-start.5 = (bf16[2,256,256]{2,1,0:T(8,128)(2,1)S(1)}, bf16[2,256,256]{2,1,0:T(8,128)(2,1)S(1)}, u32[]{:S(2)}, u32[]{:S(2)}) collective-permute-start(bf16[2,256,256]{2,1,0:T(8,128)(2,1)S(1)} %copy-done.10), channel_id=1, source_target_pairs={{13,0},{14,1},{15,2},{0,3},{1,4},{2,5},{3,6},{4,7},{5,8},{6,9},{7,... | collective-permute-start | bytes 786440 | tf_op jit(solution)/shard_map/ppermute | solution.py:40
  39.6 7.3 %collective-permute-done.3.p2 = bf16[2,256,256]{2,1,0:T(8,128)(2,1)S(1)} collective-permute-done((bf16[2,256,256]{2,1,0:T(8,128)(2,1)}, bf16[2,256,256]{2,1,0:T(8,128)(2,1)S(1)}, u32[]{:S(2)}, u32[]{:S(2)}) %collective-permute-start.3) | collective-permute-done | bytes 262176 | tf_op jit(solution)/shard_map/ppermute | solution.py:40
  46.9 2.0 %collective-permute-start.8 = (bf16[2,256,384]{2,1,0:T(8,128)(2,1)S(1)}, bf16[2,256,384]{2,1,0:T(8,128)(2,1)S(1)}, u32[]{:S(2)}, u32[]{:S(2)}) collective-permute-start(bf16[2,256,384]{2,1,0:T(8,128)(2,1)S(1)} %copy-done.9), channel_id=1, source_target_pairs={{5,0},{6,1},{7,2},{8,3},{9,4},{10,5},{11,6},{12,7},{13,8},{14,9},{... | collective-permute-start | bytes 1179656 | tf_op jit(solution)/shard_map/ppermute | solution.py:40
  48.9 9.0 %collective-permute-start.9 = (bf16[2,256,384]{2,1,0:T(8,128)(2,1)S(1)}, bf16[2,256,384]{2,1,0:T(8,128)(2,1)S(1)}, u32[]{:S(2)}, u32[]{:S(2)}) collective-permute-start(bf16[2,256,384]{2,1,0:T(8,128)(2,1)S(1)} %copy-done.8), channel_id=1, source_target_pairs={{9,0},{10,1},{11,2},{12,3},{13,4},{14,5},{15,6},{0,7},{1,8},{2,9},... | collective-permute-start | bytes 1179656 | tf_op jit(solution)/shard_map/ppermute | solution.py:40
  59.3 3.4 %attend.4.refs_0_ = bf16[512,256]{1,0:T(8,128)(2,1)S(1)} custom-call(s32[1]{0:T(128)S(6)} %copy.16.live_ref, s32[1]{0:T(128)S(6)} %copy.17.depth_ref, bf16[512,256]{1,0:T(8,128)(2,1)S(1)} %get-tuple-element.32.q_ref, bf16[512,256]{1,0:T(8,128)(2,1)S(1)} %get-tuple-element.33.k_ref, bf16[512,256]{1,0:T(8,128)(2,1)S(1)} %get-tuple-element.34.v_ref, ...), custom_call_target="tpu_custom_call" | custom-call | flops 1 | bytes 1 | tf_op jit(solution)/shard_map/attend/pallas_call | solution.py:295
  62.6 1.4 %collective-permute-start.6 = (bf16[512,256]{1,0:T(8,128)(2,1)S(1)}, bf16[512,256]{1,0:T(8,128)(2,1)S(1)}, u32[]{:S(2)}, u32[]{:S(2)}) collective-permute-start(bf16[512,256]{1,0:T(8,128)(2,1)S(1)} %attend.4.refs_0_), channel_id=1, source_target_pairs={{16,0},{0,16},{17,1},{1,17},{18,2},{2,18},{19,3},{3,19},{20,4},{4,... | collective-permute-start | bytes 786440 | tf_op jit(solution)/shard_map/ppermute | solution.py:31
  64.0 4.2 %collective-permute-done.6.refs_1_ = bf16[512,256]{1,0:T(8,128)(2,1)S(1)} collective-permute-done((bf16[512,256]{1,0:T(8,128)(2,1)S(1)}, bf16[512,256]{1,0:T(8,128)(2,1)S(1)}, u32[]{:S(2)}, u32[]{:S(2)}) %collective-permute-start.6) | collective-permute-done | bytes 262176 | tf_op jit(solution)/shard_map/ppermute | solution.py:31
  69.1 4.9 %relay_project.1 = (bf16[2,256,640]{2,1,0:T(8,128)(2,1)}, bf16[2,256,640]{2,1,0:T(8,128)(2,1)}) custom-call(s32[1]{0:T(128)} %bitcast.2.kv_ref, s32[1]{0:T(128)} %bitcast.here_ref, s32[32]{0:T(128)S(1)} %copy-done.5, bf16[256,1280]{1,0:T(8,128)(2,1)} %collective-permute-done.4.refs_0_, bf16[256,1280]{1,0:T(8,128)(2,1)S(1)} %collective-permute-done.7.refs_1_, ...), custom_call_target="tpu_custom_call" | custom-call | flops 1 | bytes 1 | tf_op jit(solution)/shard_map/relay_project/pallas_call | solution.py:230
  74.0 14.4 %collective-permute-done.9.p2 = bf16[2,256,384]{2,1,0:T(8,128)(2,1)S(1)} collective-permute-done((bf16[2,256,384]{2,1,0:T(8,128)(2,1)S(1)}, bf16[2,256,384]{2,1,0:T(8,128)(2,1)S(1)}, u32[]{:S(2)}, u32[]{:S(2)}) %collective-permute-start.9) | collective-permute-done | bytes 393248 | tf_op jit(solution)/shard_map/ppermute | solution.py:40
  88.4 1.9 %attend.5.refs_0_ = bf16[512,128]{1,0:T(8,128)(2,1)S(1)} custom-call(s32[1]{0:T(128)S(6)} %copy.16.live_ref, s32[1]{0:T(128)S(6)} %copy.17.depth_ref, bf16[512,128]{1,0:T(8,128)(2,1)S(1)} %get-tuple-element.43.q_ref, bf16[512,128]{1,0:T(8,128)(2,1)S(1)} %get-tuple-element.44.k_ref, bf16[512,128]{1,0:T(8,128)(2,1)S(1)} %get-tuple-element.45.v_ref, ...), custom_call_target="tpu_custom_call" | custom-call | flops 1 | bytes 1 | tf_op jit(solution)/shard_map/attend/pallas_call | solution.py:295
  91.0 1.9 %attend.6.refs_1_ = bf16[512,128]{1,0:T(8,128)(2,1)S(1)} custom-call(s32[1]{0:T(128)S(6)} %copy.16.live_ref, s32[1]{0:T(128)S(6)} %copy.17.depth_ref, bf16[512,128]{1,0:T(8,128)(2,1)S(1)} %get-tuple-element.53.q_ref, bf16[512,128]{1,0:T(8,128)(2,1)S(1)} %get-tuple-element.54.k_ref, bf16[512,128]{1,0:T(8,128)(2,1)S(1)} %get-tuple-element.55.v_ref, ...), custom_call_target="tpu_custom_call" | custom-call | flops 1 | bytes 1 | tf_op jit(solution)/shard_map/attend/pallas_call | solution.py:295
  92.9 0.9 collective-permute-start.12
  93.8 2.1 %attend.7.refs_2_ = bf16[512,128]{1,0:T(8,128)(2,1)S(1)} custom-call(s32[1]{0:T(128)S(6)} %copy.16.live_ref, s32[1]{0:T(128)S(6)} %copy.17.depth_ref, bf16[512,128]{1,0:T(8,128)(2,1)S(1)} %get-tuple-element.57.q_ref, bf16[512,128]{1,0:T(8,128)(2,1)S(1)} %get-tuple-element.58.k_ref, bf16[512,128]{1,0:T(8,128)(2,1)S(1)} %get-tuple-element.59.v_ref, ...), custom_call_target="tpu_custom_call" | custom-call | flops 1 | bytes 1 | tf_op jit(solution)/shard_map/attend/pallas_call | solution.py:295
  96.6 1.3 %collective-permute-done.12.refs_4_ = bf16[512,128]{1,0:T(8,128)(2,1)S(1)} collective-permute-done((bf16[512,128]{1,0:T(8,128)(2,1)S(1)}, bf16[512,128]{1,0:T(8,128)(2,1)S(1)}, u32[]{:S(2)}, u32[]{:S(2)}) %collective-permute-start.12) | collective-permute-done | bytes 131104 | tf_op jit(solution)/shard_map/ppermute | solution.py:31
  97.9 1.9 %collective-permute-done.13.refs_5_ = bf16[512,128]{1,0:T(8,128)(2,1)S(1)} collective-permute-done((bf16[512,128]{1,0:T(8,128)(2,1)S(1)}, bf16[512,128]{1,0:T(8,128)(2,1)S(1)}, u32[]{:S(2)}, u32[]{:S(2)}) %collective-permute-start.13) | collective-permute-done | bytes 131104 | tf_op jit(solution)/shard_map/ppermute | solution.py:31
  99.8 4.0 %finish.1 = bf16[512,1280]{1,0:T(8,128)(2,1)} custom-call(bf16[512,1280]{1,0:T(8,128)(2,1)S(1)} %copy-done, bf16[640,1280]{1,0:T(8,128)(2,1)S(1)} %copy-done.3, bf16[640,1280]{1,0:T(8,128)(2,1)S(1)} %collective-permute-done.w_theirs, f32[1,1280]{1,0:T(1,128)S(1)} %reshape.18.rate, f32[512,1280]{1,0:T(8,128)S(1)} %partial_branch.1.begun, ...), custom_call_target="tpu_custom_call" | custom-call | flops 1 | bytes 1 | tf_op jit(solution)/shard_map/finish/pallas_call | solution.py:368
  (38 shorter events, 3.2 us)
Async XLA Ops:
  0.6 46.3 %collective-permute-start = (bf16[640,1280]{1,0:T(8,128)(2,1)}, bf16[640,1280]{1,0:T(8,128)(2,1)S(1)}, u32[]{:S(2)}, u32[]{:S(2)}) collective-permute-start(bf16[640,1280]{1,0:T(8,128)(2,1)} %w_mine.3), channel_id=1, source_target_pairs={{16,0},{0,16},{17,1},{1,17},{18,2},{2,18},{19,3},{3,19},{20,4},{4,... | collective-permute-start | bytes 4915208 | tf_op jit(solution)/shard_map/ppermute | solution.py:31
  2.8 13.2 %copy-start.2 = (bf16[1280,640]{1,0:T(8,128)(2,1)S(1)}, bf16[1280,640]{1,0:T(8,128)(2,1)}, u32[]{:S(2)}) copy-start(bf16[1280,640]{1,0:T(8,128)(2,1)} %refs_3_.1) | copy-start | bytes 4915204
  4.9 19.5 %collective-permute-start.4 = (bf16[256,1280]{1,0:T(8,128)(2,1)}, bf16[256,1280]{1,0:T(8,128)(2,1)}, u32[]{:S(2)}, u32[]{:S(2)}) collective-permute-start(bf16[256,1280]{1,0:T(8,128)(2,1)} %split_rows.1._), channel_id=1, source_target_pairs={{12,0},{13,1},{14,2},{15,3},{0,4},{1,5},{2,6},{3,7},{4,8},{5,9},{6... | collective-permute-start | bytes 1966088 | tf_op jit(solution)/shard_map/ppermute | solution.py:40
  6.3 9.7 %copy-start = (bf16[512,1280]{1,0:T(8,128)(2,1)S(1)}, bf16[512,1280]{1,0:T(8,128)(2,1)}, u32[]{:S(2)}) copy-start(bf16[512,1280]{1,0:T(8,128)(2,1)} %hidden.5) | copy-start | bytes 3932164
  6.3 9.7 %copy-start.1 = (bf16[1280,640]{1,0:T(8,128)(2,1)S(1)}, bf16[1280,640]{1,0:T(8,128)(2,1)}, u32[]{:S(2)}) copy-start(bf16[1280,640]{1,0:T(8,128)(2,1)} %refs_2_.1) | copy-start | bytes 4915204
  10.4 14.1 %collective-permute-start.1 = (bf16[2,256,640]{2,1,0:T(8,128)(2,1)}, bf16[2,256,640]{2,1,0:T(8,128)(2,1)S(1)}, u32[]{:S(2)}, u32[]{:S(2)}) collective-permute-start(bf16[2,256,640]{2,1,0:T(8,128)(2,1)} %get-tuple-element.35), channel_id=1, source_target_pairs={{1,0},{2,1},{3,2},{4,3},{5,4},{6,5},{7,6},{8,7},{9,8},{10,9},{11,1... | collective-permute-start | bytes 1966088 | tf_op jit(solution)/shard_map/ppermute | solution.py:40
  11.7 28.0 %collective-permute-start.2 = (bf16[2,256,256]{2,1,0:T(8,128)(2,1)}, bf16[2,256,256]{2,1,0:T(8,128)(2,1)S(1)}, u32[]{:S(2)}, u32[]{:S(2)}) collective-permute-start(bf16[2,256,256]{2,1,0:T(8,128)(2,1)} %get-tuple-element.36), channel_id=1, source_target_pairs={{5,0},{6,1},{7,2},{8,3},{9,4},{10,5},{11,6},{12,7},{13,8},{14,9},{... | collective-permute-start | bytes 786440 | tf_op jit(solution)/shard_map/ppermute | solution.py:40
  15.1 31.8 %collective-permute-start.3 = (bf16[2,256,256]{2,1,0:T(8,128)(2,1)}, bf16[2,256,256]{2,1,0:T(8,128)(2,1)S(1)}, u32[]{:S(2)}, u32[]{:S(2)}) collective-permute-start(bf16[2,256,256]{2,1,0:T(8,128)(2,1)} %get-tuple-element.37), channel_id=1, source_target_pairs={{9,0},{10,1},{11,2},{12,3},{13,4},{14,5},{15,6},{0,7},{1,8},{2,9},... | collective-permute-start | bytes 786440 | tf_op jit(solution)/shard_map/ppermute | solution.py:40
  17.4 7.0 %copy-start.10 = (bf16[2,256,256]{2,1,0:T(8,128)(2,1)S(1)}, bf16[2,256,256]{2,1,0:T(8,128)(2,1)}, u32[]{:S(2)}) copy-start(bf16[2,256,256]{2,1,0:T(8,128)(2,1)} %get-tuple-element.39) | copy-start | bytes 786436
  17.4 29.5 %copy-start.9 = (bf16[2,256,384]{2,1,0:T(8,128)(2,1)S(1)}, bf16[2,256,384]{2,1,0:T(8,128)(2,1)}, u32[]{:S(2)}) copy-start(bf16[2,256,384]{2,1,0:T(8,128)(2,1)} %get-tuple-element.47) | copy-start | bytes 1179652
  17.4 31.5 %copy-start.8 = (bf16[2,256,384]{2,1,0:T(8,128)(2,1)S(1)}, bf16[2,256,384]{2,1,0:T(8,128)(2,1)}, u32[]{:S(2)}) copy-start(bf16[2,256,384]{2,1,0:T(8,128)(2,1)} %get-tuple-element.49) | copy-start | bytes 1179652
  17.4 40.5 %copy-start.7 = (bf16[2,256,384]{2,1,0:T(8,128)(2,1)S(1)}, bf16[2,256,384]{2,1,0:T(8,128)(2,1)}, u32[]{:S(2)}) copy-start(bf16[2,256,384]{2,1,0:T(8,128)(2,1)} %get-tuple-element.51) | copy-start | bytes 1179652
  24.4 43.8 %copy-start.3 = (bf16[640,1280]{1,0:T(8,128)(2,1)S(1)}, bf16[640,1280]{1,0:T(8,128)(2,1)}, u32[]{:S(2)}) copy-start(bf16[640,1280]{1,0:T(8,128)(2,1)} %w_mine.3) | copy-start | bytes 4915204
  24.5 22.4 %collective-permute-start.5 = (bf16[2,256,256]{2,1,0:T(8,128)(2,1)S(1)}, bf16[2,256,256]{2,1,0:T(8,128)(2,1)S(1)}, u32[]{:S(2)}, u32[]{:S(2)}) collective-permute-start(bf16[2,256,256]{2,1,0:T(8,128)(2,1)S(1)} %copy-done.10), channel_id=1, source_target_pairs={{13,0},{14,1},{15,2},{0,3},{1,4},{2,5},{3,6},{4,7},{5,8},{6,9},{7,... | collective-permute-start | bytes 786440 | tf_op jit(solution)/shard_map/ppermute | solution.py:40
  46.9 22.2 %collective-permute-start.7 = (bf16[256,1280]{1,0:T(8,128)(2,1)}, bf16[256,1280]{1,0:T(8,128)(2,1)S(1)}, u32[]{:S(2)}, u32[]{:S(2)}) collective-permute-start(bf16[256,1280]{1,0:T(8,128)(2,1)} %collective-permute-done.4.refs_0_), channel_id=1, source_target_pairs={{16,0},{0,16},{17,1},{1,17},{18,2},{2,18},{19,3},{3,19},{20,4},{4,... | collective-permute-start | bytes 1966088 | tf_op jit(solution)/shard_map/ppermute | solution.py:31
  46.9 27.1 %collective-permute-start.8 = (bf16[2,256,384]{2,1,0:T(8,128)(2,1)S(1)}, bf16[2,256,384]{2,1,0:T(8,128)(2,1)S(1)}, u32[]{:S(2)}, u32[]{:S(2)}) collective-permute-start(bf16[2,256,384]{2,1,0:T(8,128)(2,1)S(1)} %copy-done.9), channel_id=1, source_target_pairs={{5,0},{6,1},{7,2},{8,3},{9,4},{10,5},{11,6},{12,7},{13,8},{14,9},{... | collective-permute-start | bytes 1179656 | tf_op jit(solution)/shard_map/ppermute | solution.py:40
  48.9 39.5 %collective-permute-start.9 = (bf16[2,256,384]{2,1,0:T(8,128)(2,1)S(1)}, bf16[2,256,384]{2,1,0:T(8,128)(2,1)S(1)}, u32[]{:S(2)}, u32[]{:S(2)}) collective-permute-start(bf16[2,256,384]{2,1,0:T(8,128)(2,1)S(1)} %copy-done.8), channel_id=1, source_target_pairs={{9,0},{10,1},{11,2},{12,3},{13,4},{14,5},{15,6},{0,7},{1,8},{2,9},... | collective-permute-start | bytes 1179656 | tf_op jit(solution)/shard_map/ppermute | solution.py:40
  58.0 30.5 %collective-permute-start.10 = (bf16[2,256,384]{2,1,0:T(8,128)(2,1)S(1)}, bf16[2,256,384]{2,1,0:T(8,128)(2,1)S(1)}, u32[]{:S(2)}, u32[]{:S(2)}) collective-permute-start(bf16[2,256,384]{2,1,0:T(8,128)(2,1)S(1)} %copy-done.7), channel_id=1, source_target_pairs={{13,0},{14,1},{15,2},{0,3},{1,4},{2,5},{3,6},{4,7},{5,8},{6,9},{7,... | collective-permute-start | bytes 1179656 | tf_op jit(solution)/shard_map/ppermute | solution.py:40
  62.6 6.5 %copy-start.5 = (s32[32]{0:T(128)S(1)}, s32[32]{0:T(128)}, u32[]{:S(2)}) copy-start(s32[32]{0:T(128)} %placement.1) | copy-start | bytes 388
  62.6 5.6 %collective-permute-start.6 = (bf16[512,256]{1,0:T(8,128)(2,1)S(1)}, bf16[512,256]{1,0:T(8,128)(2,1)S(1)}, u32[]{:S(2)}, u32[]{:S(2)}) collective-permute-start(bf16[512,256]{1,0:T(8,128)(2,1)S(1)} %attend.4.refs_0_), channel_id=1, source_target_pairs={{16,0},{0,16},{17,1},{1,17},{18,2},{2,18},{19,3},{3,19},{20,4},{4,... | collective-permute-start | bytes 786440 | tf_op jit(solution)/shard_map/ppermute | solution.py:31
  90.3 6.3 %collective-permute-start.11 = (bf16[512,128]{1,0:T(8,128)(2,1)S(1)}, bf16[512,128]{1,0:T(8,128)(2,1)S(1)}, u32[]{:S(2)}, u32[]{:S(2)}) collective-permute-start(bf16[512,128]{1,0:T(8,128)(2,1)S(1)} %attend.5.refs_0_), channel_id=1, source_target_pairs={{16,0},{0,16},{17,1},{1,17},{18,2},{2,18},{19,3},{3,19},{20,4},{4,... | collective-permute-start | bytes 393224 | tf_op jit(solution)/shard_map/ppermute | solution.py:31
  92.8 3.7 %copy-start.6 = (f32[1280]{0:T(1024)S(1)}, f32[1280]{0:T(1024)}, u32[]{:S(2)}) copy-start(f32[1280]{0:T(1024)} %param.19) | copy-start | bytes 15364
  92.9 5.0 %collective-permute-start.12 = (bf16[512,128]{1,0:T(8,128)(2,1)S(1)}, bf16[512,128]{1,0:T(8,128)(2,1)S(1)}, u32[]{:S(2)}, u32[]{:S(2)}) collective-permute-start(bf16[512,128]{1,0:T(8,128)(2,1)S(1)} %attend.6.refs_1_), channel_id=1, source_target_pairs={{16,0},{0,16},{17,1},{1,17},{18,2},{2,18},{19,3},{3,19},{20,4},{4,... | collective-permute-start | bytes 393224 | tf_op jit(solution)/shard_map/ppermute | solution.py:31
  95.9 3.9 %collective-permute-start.13 = (bf16[512,128]{1,0:T(8,128)(2,1)S(1)}, bf16[512,128]{1,0:T(8,128)(2,1)S(1)}, u32[]{:S(2)}, u32[]{:S(2)}) collective-permute-start(bf16[512,128]{1,0:T(8,128)(2,1)S(1)} %attend.7.refs_2_), channel_id=1, source_target_pairs={{16,0},{0,16},{17,1},{1,17},{18,2},{2,18},{19,3},{3,19},{20,4},{4,... | collective-permute-start | bytes 393224 | tf_op jit(solution)/shard_map/ppermute | solution.py:31
  (1 other events, 1.4 us)

commit v4 on v2

--- a/solution.py
+++ b/solution.py
@@ -113,19 +113,16 @@
         for side in range(2):
             index = 2 * slot + side
             copies[index].wait()
-            if slot == 0:
-                outs[0][side] = buf[index]
-                continue
             for g, (start, size) in enumerate(slices):
-                outs[g * (PMAX - 1) + slot][side] = buf[index, :, start : start + size]
+                outs[g * PMAX + slot][side] = buf[index, :, start : start + size]
 
 
 def pack(pool_keys, pool_values, table, here, devices, offsets, first):
     width = pool_keys.shape[2]
     slices = group_slices(width)
-    outs = [jax.ShapeDtypeStruct((2, PAGE, width), bf16)]
+    outs = []
     for _, size in slices:
-        outs += [jax.ShapeDtypeStruct((2, PAGE, size), bf16)] * (PMAX - 1)
+        outs += [jax.ShapeDtypeStruct((2, PAGE, size), bf16)] * PMAX
     smem = pl.BlockSpec(memory_space=pltpu.SMEM)
     hbm = pl.BlockSpec(memory_space=pltpu.HBM)
     result = pl.pallas_call(
@@ -141,8 +138,7 @@
         cost_estimate=cost(),
         name="pack",
     )(here, table, pool_keys, pool_values, first)
-    each = PMAX - 1
-    return result[0], [result[1 + each * g : 1 + each * (g + 1)] for g in range(len(slices))]
+    return [result[PMAX * g : PMAX * (g + 1)] for g in range(len(slices))]
 
 
 def head_sum_matrix():
@@ -240,7 +236,7 @@
     )(kv_index, here, placement, mine, theirs, wk, wv, gain)
 
 
-def attend_kernel(inner, base, live_ref, depth_ref, q_ref, k_ref, v_ref, p0, p1, p2, p3, out):
+def attend_kernel(inner, live_ref, depth_ref, q_ref, k_ref, v_ref, p0, p1, p2, p3, out):
     pages = (p0, p1, p2, p3)
     tokens, width = q_ref.shape
     live, depth = live_ref[0], depth_ref[0]
@@ -252,8 +248,7 @@
     blocks = tokens // PAGE
     for start in range(0, width, LANES):
         cols = slice(start, start + LANES)
-        firsts = (base,) + (inner,) * (PMAX - 1)
-        page_cols = [slice(first + start, first + start + LANES) for first in firsts]
+        page_cols = slice(inner + start, inner + start + LANES)
         keys, values = [], []
         for b in range(blocks):
             rows = slice(b * PAGE, (b + 1) * PAGE)
@@ -264,9 +259,9 @@
             values.append(jnp.concatenate([shown, ones], axis=1))
         for p in range(PMAX):
             keep = jnp.where(p < depth, 1.0, 0.0).astype(bf16)
-            keys.append(pages[p][0, :, page_cols[p]])
+            keys.append(pages[p][0, :, page_cols])
             ones = jnp.full((PAGE, LANES), 1.0, bf16) * keep
-            values.append(jnp.concatenate([pages[p][1, :, page_cols[p]] * keep, ones], axis=1))
+            values.append(jnp.concatenate([pages[p][1, :, page_cols] * keep, ones], axis=1))
         for b in range(blocks):
             rows = slice(b * PAGE, (b + 1) * PAGE)
             q = q_ref[rows, cols]
@@ -286,14 +281,14 @@
             out[rows, cols] = jnp.where((lane // HD) == 0, ratios[0], ratios[1]).astype(bf16)
 
 
-def attend(live, depth, q, k, v, pages, inner, base):
+def attend(live, depth, q, k, v, pages, inner):
     tokens, width = q.shape
     heads = width // HD
     smem = pl.BlockSpec(memory_space=pltpu.SMEM)
     vmem = pl.BlockSpec(memory_space=pltpu.VMEM)
     keys = tokens + PMAX * PAGE
     return pl.pallas_call(
-        functools.partial(attend_kernel, inner, base),
+        functools.partial(attend_kernel, inner),
         in_specs=[smem, smem] + [vmem] * 7,
         out_specs=vmem,
         out_shape=jax.ShapeDtypeStruct((tokens, width), bf16),
@@ -406,7 +401,7 @@
 
     assert blocks == lax.axis_size("kv") == 2
     relay_send = split_rows(hidden_in, kv_index)
-    near_send, far_send = pack(
+    page_send = pack(
         pool_keys, pool_values, prefix_pages.T, here, devices, page_offsets, relay_send
     )
     projected = project(hidden_in, w_query, w_key, w_value, gain)
@@ -415,15 +410,17 @@
         return over_blk(block, [devices - page_offsets[slot]] * 2)
 
     relay_mine = over_blk(relay_send, block_offsets)
-    first = {slot: fetch(far_send[0][slot - 1], slot) for slot in SLOT_ORDER}
+    ready = projected[0][0]
+    first = {slot: fetch(page_send[0][slot], slot) for slot in SLOT_ORDER}
+    first[0] = fetch(after(page_send[0][0], ready, relay_mine), 0)
     arrived = [first[slot] for slot in SLOT_ORDER]
-    near = fetch(after(near_send, projected[0][0], relay_mine, *arrived), 0)
-    second = {}
+    second = {0: fetch(after(page_send[1][0], ready, first[0], relay_mine), 0)}
     for i, slot in enumerate(SLOT_ORDER):
-        second[slot] = fetch(after(far_send[1][slot - 1], projected[0][0], relay_mine, *arrived[: i + 1]), slot)
-    pages = [[near] + [got[slot] for slot in range(1, PMAX)] for got in (first, second)]
+        gate = arrived[: i + 1]
+        second[slot] = fetch(after(page_send[1][slot], ready, relay_mine, *gate), slot)
+    pages = [[got[slot] for slot in range(PMAX)] for got in (first, second)]
     w_theirs = from_behind(w_out, "kv", 1)
-    relay_theirs = from_behind(after(relay_mine, w_theirs, *arrived), "kv", 1)
+    relay_theirs = from_behind(after(relay_mine, w_theirs, *arrived, first[0]), "kv", 1)
     new_keys, new_values = relay_project(
         relay_mine, relay_theirs, w_key, w_value, gain, kv_index, here, placement, block_offsets
     )
@@ -432,10 +429,12 @@
     begun = None
     for (g, inner, start, size), (q, k, v) in zip(unit_slices(), projected):
         if g and begun is None:
-            begun = partial_branch(slices[0], w_out, w_theirs, mine[0], theirs[0])
+            begun = partial_branch(
+                slices[0], w_out, after(w_theirs, new_keys), mine[0], theirs[0]
+            )
         if g:
             q = after(q, new_keys, begun)
-        attended = attend(req_len, prefix_len, q, k, v, pages[g], inner, start)
+        attended = attend(req_len, prefix_len, q, k, v, pages[g], inner)
         mine[g].append(attended)
         theirs[g].append(from_behind(attended, "kv", 1))
         slices[g].append((start, size))

time: 108 us -> 100 us (0.926)
  the two profiles are of different devices: /device:TPU:16 before, /device:TPU:26 now
where the time goes in v4:
time: 100 us
  waiting for transfers between devices  40.6 us (41%)
  Pallas kernels  32.2 us (32%)
  starting transfers between devices  22.9 us (23%)
  between operations  2.24 us (2%)
  local copies, waits for them, and re-layouts  2.17 us (2%)
    ppermute x9, waiting for transfers between devices, over_blk(): return lax.ppermute(block, ('kv', 'blk'), route)  31.7 us
    ppermute x9, starting transfers between devices, over_blk(): return lax.ppermute(block, ('kv', 'blk'), route)  15.3 us
    pallas_call x4, Pallas kernels, attend(): pl.pallas_call(functools.partial(attend_kernel, inner), in_specs=[smem, s...  9.19 us
    ppermute x6, waiting for transfers between devices, from_behind(): return lax.ppermute(block, axis, route)  8.9 us
    ppermute x6, starting transfers between devices, from_behind(): return lax.ppermute(block, axis, route)  7.62 us
    pallas_call x1, Pallas kernels, project(): pl.pallas_call(functools.partial(project_kernel, slices), out_shape=outs,...  6.94 us
    pallas_call x1, Pallas kernels, relay_project(): pl.pallas_call(functools.partial(relay_kernel, group_slices(width), block...  4.93 us
    pallas_call x1, Pallas kernels, pack(): pl.pallas_call(functools.partial(pack_kernel, slices, devices, offsets),...  4.08 us
  transfers between devices with their start and end apart: 15, of which 7 were waited for; matrix products, arithmetic and copies ran while one was open for 1% of the time, Pallas kernels for 26%

profile of v4, /device:TPU:26, one launch (start us, length us, event | category | flops | bytes accessed | tf_op | source)
XLA Modules:
  0.0 100.2 jit_solution(12028878189242079276)
XLA Ops:
  0.6 1.6 %collective-permute-start = (bf16[640,1280]{1,0:T(8,128)(2,1)}, bf16[640,1280]{1,0:T(8,128)(2,1)S(1)}, u32[]{:S(2)}, u32[]{:S(2)}) collective-permute-start(bf16[640,1280]{1,0:T(8,128)(2,1)} %w_mine.3), channel_id=1, source_target_pairs={{16,0},{0,16},{17,1},{1,17},{18,2},{2,18},{19,3},{3,19},{20,4},{4,... | collective-permute-start | bytes 4915208 | tf_op jit(solution)/shard_map/ppermute | solution.py:31
  2.2 2.1 %split_rows.1._ = bf16[256,1280]{1,0:T(8,128)(2,1)} custom-call(s32[1]{0:T(128)} %bitcast.kv_ref, bf16[512,1280]{1,0:T(8,128)(2,1)} %hidden.5), custom_call_target="tpu_custom_call" | custom-call | flops 1 | bytes 1 | tf_op jit(solution)/shard_map/split_rows/pallas_call | solution.py:89
  4.6 4.1 %pack.1 = (bf16[2,256,256]{2,1,0:T(8,128)(2,1)}, bf16[2,256,256]{2,1,0:T(8,128)(2,1)}, bf16[2,256,256]{2,1,0:T(8,128)(2,1)}, bf16[2,256,256]{2,1,0:T(8,128)(2,1)...) custom-call(s32[1]{0:T(128)} %bitcast.1.here_ref, ...), custom_call_target="tpu_custom_call" | custom-call | flops 1 | bytes 1 | tf_op jit(solution)/shard_map/pack/pallas_call | solution.py:128
  9.4 1.2 %collective-permute-start.3 = (bf16[2,256,256]{2,1,0:T(8,128)(2,1)}, bf16[2,256,256]{2,1,0:T(8,128)(2,1)S(1)}, u32[]{:S(2)}, u32[]{:S(2)}) collective-permute-start(bf16[2,256,256]{2,1,0:T(8,128)(2,1)} %get-tuple-element.36), channel_id=1, source_target_pairs={{5,0},{6,1},{7,2},{8,3},{9,4},{10,5},{11,6},{12,7},{13,8},{14,9},{... | collective-permute-start | bytes 786440 | tf_op jit(solution)/shard_map/ppermute | solution.py:40
  10.6 3.1 %collective-permute-start.4 = (bf16[2,256,256]{2,1,0:T(8,128)(2,1)}, bf16[2,256,256]{2,1,0:T(8,128)(2,1)S(1)}, u32[]{:S(2)}, u32[]{:S(2)}) collective-permute-start(bf16[2,256,256]{2,1,0:T(8,128)(2,1)} %get-tuple-element.37), channel_id=1, source_target_pairs={{13,0},{14,1},{15,2},{0,3},{1,4},{2,5},{3,6},{4,7},{5,8},{6,9},{7,... | collective-permute-start | bytes 786440 | tf_op jit(solution)/shard_map/ppermute | solution.py:40
  14.4 1.4 %copy-done.4 = bf16[1280,640]{1,0:T(8,128)(2,1)S(1)} copy-done((bf16[1280,640]{1,0:T(8,128)(2,1)S(1)}, bf16[1280,640]{1,0:T(8,128)(2,1)}, u32[]{:S(2)}) %copy-start.4) | copy-done | bytes 1638424
  15.8 6.9 %project.1 = (bf16[512,256]{1,0:T(8,128)(2,1)S(1)}, bf16[512,256]{1,0:T(8,128)(2,1)S(1)}, bf16[512,256]{1,0:T(8,128)(2,1)S(1)}, bf16[512,128]{1,0:T(8,128)(2,1)S...) custom-call(bf16[512,1280]{1,0:T(8,128)(2,1)S(1)} %copy-done, ...), custom_call_target="tpu_custom_call" | custom-call | flops 1 | bytes 1 | tf_op jit(solution)/shard_map/project/pallas_call | solution.py:193
  23.4 12.8 %collective-permute-done.2.p2 = bf16[2,256,256]{2,1,0:T(8,128)(2,1)S(1)} collective-permute-done((bf16[2,256,256]{2,1,0:T(8,128)(2,1)}, bf16[2,256,256]{2,1,0:T(8,128)(2,1)S(1)}, u32[]{:S(2)}, u32[]{:S(2)}) %collective-permute-start.2) | collective-permute-done | bytes 262176 | tf_op jit(solution)/shard_map/ppermute | solution.py:40
  36.1 2.3 %collective-permute-done.w_theirs = bf16[640,1280]{1,0:T(8,128)(2,1)S(1)} collective-permute-done((bf16[640,1280]{1,0:T(8,128)(2,1)}, bf16[640,1280]{1,0:T(8,128)(2,1)S(1)}, u32[]{:S(2)}, u32[]{:S(2)}) %collective-permute-start) | collective-permute-done | bytes 1638432 | tf_op jit(solution)/shard_map/ppermute | solution.py:31
  38.4 1.7 %collective-permute-start.6 = (bf16[256,1280]{1,0:T(8,128)(2,1)}, bf16[256,1280]{1,0:T(8,128)(2,1)S(1)}, u32[]{:S(2)}, u32[]{:S(2)}) collective-permute-start(bf16[256,1280]{1,0:T(8,128)(2,1)} %collective-permute-done.1.refs_0_), channel_id=1, source_target_pairs={{16,0},{0,16},{17,1},{1,17},{18,2},{2,18},{19,3},{3,19},{20,4},{4,... | collective-permute-start | bytes 1966088 | tf_op jit(solution)/shard_map/ppermute | solution.py:31
  41.0 5.3 %collective-permute-start.9 = (bf16[2,256,384]{2,1,0:T(8,128)(2,1)S(1)}, bf16[2,256,384]{2,1,0:T(8,128)(2,1)S(1)}, u32[]{:S(2)}, u32[]{:S(2)}) collective-permute-start(bf16[2,256,384]{2,1,0:T(8,128)(2,1)S(1)} %copy-done.9), channel_id=1, source_target_pairs={{5,0},{6,1},{7,2},{8,3},{9,4},{10,5},{11,6},{12,7},{13,8},{14,9},{... | collective-permute-start | bytes 1179656 | tf_op jit(solution)/shard_map/ppermute | solution.py:40
  46.3 1.1 %collective-permute-start.10 = (bf16[2,256,384]{2,1,0:T(8,128)(2,1)S(1)}, bf16[2,256,384]{2,1,0:T(8,128)(2,1)S(1)}, u32[]{:S(2)}, u32[]{:S(2)}) collective-permute-start(bf16[2,256,384]{2,1,0:T(8,128)(2,1)S(1)} %copy-done.8), channel_id=1, source_target_pairs={{9,0},{10,1},{11,2},{12,3},{13,4},{14,5},{15,6},{0,7},{1,8},{2,9},... | collective-permute-start | bytes 1179656 | tf_op jit(solution)/shard_map/ppermute | solution.py:40
  47.4 2.6 %collective-permute-start.8 = (bf16[2,256,384]{2,1,0:T(8,128)(2,1)S(1)}, bf16[2,256,384]{2,1,0:T(8,128)(2,1)S(1)}, u32[]{:S(2)}, u32[]{:S(2)}) collective-permute-start(bf16[2,256,384]{2,1,0:T(8,128)(2,1)S(1)} %copy-done.7), channel_id=1, source_target_pairs={{1,0},{2,1},{3,2},{4,3},{5,4},{6,5},{7,6},{8,7},{9,8},{10,9},{11,1... | collective-permute-start | bytes 1179656 | tf_op jit(solution)/shard_map/ppermute | solution.py:40
  51.3 3.4 %attend.4.refs_0_ = bf16[512,256]{1,0:T(8,128)(2,1)S(1)} custom-call(s32[1]{0:T(128)S(6)} %copy.16.live_ref, s32[1]{0:T(128)S(6)} %copy.17.depth_ref, bf16[512,256]{1,0:T(8,128)(2,1)S(1)} %get-tuple-element.39.q_ref, bf16[512,256]{1,0:T(8,128)(2,1)S(1)} %get-tuple-element.44.k_ref, bf16[512,256]{1,0:T(8,128)(2,1)S(1)} %get-tuple-element.45.v_ref, ...), custom_call_target="tpu_custom_call" | custom-call | flops 1 | bytes 1 | tf_op jit(solution)/shard_map/attend/pallas_call | solution.py:290
  54.7 1.8 %collective-permute-start.7 = (bf16[512,256]{1,0:T(8,128)(2,1)S(1)}, bf16[512,256]{1,0:T(8,128)(2,1)S(1)}, u32[]{:S(2)}, u32[]{:S(2)}) collective-permute-start(bf16[512,256]{1,0:T(8,128)(2,1)S(1)} %attend.4.refs_0_), channel_id=1, source_target_pairs={{16,0},{0,16},{17,1},{1,17},{18,2},{2,18},{19,3},{3,19},{20,4},{4,... | collective-permute-start | bytes 786440 | tf_op jit(solution)/shard_map/ppermute | solution.py:31
  56.5 4.9 %relay_project.1 = (bf16[2,256,640]{2,1,0:T(8,128)(2,1)}, bf16[2,256,640]{2,1,0:T(8,128)(2,1)}) custom-call(s32[1]{0:T(128)} %bitcast.kv_ref, s32[1]{0:T(128)} %bitcast.1.here_ref, s32[32]{0:T(128)S(1)} %copy-done.5, bf16[256,1280]{1,0:T(8,128)(2,1)} %collective-permute-done.1.refs_0_, bf16[256,1280]{1,0:T(8,128)(2,1)S(1)} %collective-permute-done.6.refs_1_, ...), custom_call_target="tpu_custom_call" | custom-call | flops 1 | bytes 1 | tf_op jit(solution)/shard_map/relay_project/pallas_call | solution.py:226
  61.4 2.0 %collective-permute-done.7.refs_1_ = bf16[512,256]{1,0:T(8,128)(2,1)S(1)} collective-permute-done((bf16[512,256]{1,0:T(8,128)(2,1)S(1)}, bf16[512,256]{1,0:T(8,128)(2,1)S(1)}, u32[]{:S(2)}, u32[]{:S(2)}) %collective-permute-start.7) | collective-permute-done | bytes 262176 | tf_op jit(solution)/shard_map/ppermute | solution.py:31
  64.3 18.6 %collective-permute-done.10.p2 = bf16[2,256,384]{2,1,0:T(8,128)(2,1)S(1)} collective-permute-done((bf16[2,256,384]{2,1,0:T(8,128)(2,1)S(1)}, bf16[2,256,384]{2,1,0:T(8,128)(2,1)S(1)}, u32[]{:S(2)}, u32[]{:S(2)}) %collective-permute-start.10) | collective-permute-done | bytes 393248 | tf_op jit(solution)/shard_map/ppermute | solution.py:40
  82.9 1.9 %attend.5.refs_0_ = bf16[512,128]{1,0:T(8,128)(2,1)S(1)} custom-call(s32[1]{0:T(128)S(6)} %copy.16.live_ref, s32[1]{0:T(128)S(6)} %copy.17.depth_ref, bf16[512,128]{1,0:T(8,128)(2,1)S(1)} %get-tuple-element.47.q_ref, bf16[512,128]{1,0:T(8,128)(2,1)S(1)} %get-tuple-element.48.k_ref, bf16[512,128]{1,0:T(8,128)(2,1)S(1)} %get-tuple-element.49.v_ref, ...), custom_call_target="tpu_custom_call" | custom-call | flops 1 | bytes 1 | tf_op jit(solution)/shard_map/attend/pallas_call | solution.py:290
  85.2 1.9 %attend.6.refs_1_ = bf16[512,128]{1,0:T(8,128)(2,1)S(1)} custom-call(s32[1]{0:T(128)S(6)} %copy.16.live_ref, s32[1]{0:T(128)S(6)} %copy.17.depth_ref, bf16[512,128]{1,0:T(8,128)(2,1)S(1)} %get-tuple-element.59.q_ref, bf16[512,128]{1,0:T(8,128)(2,1)S(1)} %get-tuple-element.60.k_ref, bf16[512,128]{1,0:T(8,128)(2,1)S(1)} %get-tuple-element.61.v_ref, ...), custom_call_target="tpu_custom_call" | custom-call | flops 1 | bytes 1 | tf_op jit(solution)/shard_map/attend/pallas_call | solution.py:290
  87.1 1.7 %collective-permute-start.13 = (bf16[512,128]{1,0:T(8,128)(2,1)S(1)}, bf16[512,128]{1,0:T(8,128)(2,1)S(1)}, u32[]{:S(2)}, u32[]{:S(2)}) collective-permute-start(bf16[512,128]{1,0:T(8,128)(2,1)S(1)} %attend.6.refs_1_), channel_id=1, source_target_pairs={{16,0},{0,16},{17,1},{1,17},{18,2},{2,18},{19,3},{3,19},{20,4},{4,... | collective-permute-start | bytes 393224 | tf_op jit(solution)/shard_map/ppermute | solution.py:31
  88.8 2.1 %attend.7.refs_2_ = bf16[512,128]{1,0:T(8,128)(2,1)S(1)} custom-call(s32[1]{0:T(128)S(6)} %copy.16.live_ref, s32[1]{0:T(128)S(6)} %copy.17.depth_ref, bf16[512,128]{1,0:T(8,128)(2,1)S(1)} %get-tuple-element.63.q_ref, bf16[512,128]{1,0:T(8,128)(2,1)S(1)} %get-tuple-element.64.k_ref, bf16[512,128]{1,0:T(8,128)(2,1)S(1)} %get-tuple-element.65.v_ref, ...), custom_call_target="tpu_custom_call" | custom-call | flops 1 | bytes 1 | tf_op jit(solution)/shard_map/attend/pallas_call | solution.py:290
  92.1 3.8 %collective-permute-done.14.refs_5_ = bf16[512,128]{1,0:T(8,128)(2,1)S(1)} collective-permute-done((bf16[512,128]{1,0:T(8,128)(2,1)S(1)}, bf16[512,128]{1,0:T(8,128)(2,1)S(1)}, u32[]{:S(2)}, u32[]{:S(2)}) %collective-permute-start.14) | collective-permute-done | bytes 131104 | tf_op jit(solution)/shard_map/ppermute | solution.py:31
  95.9 4.0 %finish.1 = bf16[512,1280]{1,0:T(8,128)(2,1)} custom-call(bf16[512,1280]{1,0:T(8,128)(2,1)S(1)} %copy-done, bf16[640,1280]{1,0:T(8,128)(2,1)S(1)} %copy-done.3, bf16[640,1280]{1,0:T(8,128)(2,1)S(1)} %collective-permute-done.w_theirs, f32[1,1280]{1,0:T(1,128)S(1)} %reshape.18.rate, f32[512,1280]{1,0:T(8,128)S(1)} %partial_branch.1.begun, ...), custom_call_target="tpu_custom_call" | custom-call | flops 1 | bytes 1 | tf_op jit(solution)/shard_map/finish/pallas_call | solution.py:363
  (42 shorter events, 5.6 us)
Async XLA Ops:
  0.6 37.8 %collective-permute-start = (bf16[640,1280]{1,0:T(8,128)(2,1)}, bf16[640,1280]{1,0:T(8,128)(2,1)S(1)}, u32[]{:S(2)}, u32[]{:S(2)}) collective-permute-start(bf16[640,1280]{1,0:T(8,128)(2,1)} %w_mine.3), channel_id=1, source_target_pairs={{16,0},{0,16},{17,1},{1,17},{18,2},{2,18},{19,3},{3,19},{20,4},{4,... | collective-permute-start | bytes 4915208 | tf_op jit(solution)/shard_map/ppermute | solution.py:31
  2.2 12.2 %copy-start.2 = (bf16[1280,640]{1,0:T(8,128)(2,1)S(1)}, bf16[1280,640]{1,0:T(8,128)(2,1)}, u32[]{:S(2)}) copy-start(bf16[1280,640]{1,0:T(8,128)(2,1)} %refs_3_.1) | copy-start | bytes 4915204
  4.4 18.8 %collective-permute-start.1 = (bf16[256,1280]{1,0:T(8,128)(2,1)}, bf16[256,1280]{1,0:T(8,128)(2,1)}, u32[]{:S(2)}, u32[]{:S(2)}) collective-permute-start(bf16[256,1280]{1,0:T(8,128)(2,1)} %split_rows.1._), channel_id=1, source_target_pairs={{12,0},{13,1},{14,2},{15,3},{0,4},{1,5},{2,6},{3,7},{4,8},{5,9},{6... | collective-permute-start | bytes 1966088 | tf_op jit(solution)/shard_map/ppermute | solution.py:40
  4.6 9.7 %copy-start = (bf16[512,1280]{1,0:T(8,128)(2,1)S(1)}, bf16[512,1280]{1,0:T(8,128)(2,1)}, u32[]{:S(2)}) copy-start(bf16[512,1280]{1,0:T(8,128)(2,1)} %hidden.5) | copy-start | bytes 3932164
  4.6 9.7 %copy-start.1 = (bf16[1280,640]{1,0:T(8,128)(2,1)S(1)}, bf16[1280,640]{1,0:T(8,128)(2,1)}, u32[]{:S(2)}) copy-start(bf16[1280,640]{1,0:T(8,128)(2,1)} %refs_2_.1) | copy-start | bytes 4915204
  8.7 27.4 %collective-permute-start.2 = (bf16[2,256,256]{2,1,0:T(8,128)(2,1)}, bf16[2,256,256]{2,1,0:T(8,128)(2,1)S(1)}, u32[]{:S(2)}, u32[]{:S(2)}) collective-permute-start(bf16[2,256,256]{2,1,0:T(8,128)(2,1)} %get-tuple-element.35), channel_id=1, source_target_pairs={{9,0},{10,1},{11,2},{12,3},{13,4},{14,5},{15,6},{0,7},{1,8},{2,9},... | collective-permute-start | bytes 786440 | tf_op jit(solution)/shard_map/ppermute | solution.py:40
  9.4 26.7 %collective-permute-start.3 = (bf16[2,256,256]{2,1,0:T(8,128)(2,1)}, bf16[2,256,256]{2,1,0:T(8,128)(2,1)S(1)}, u32[]{:S(2)}, u32[]{:S(2)}) collective-permute-start(bf16[2,256,256]{2,1,0:T(8,128)(2,1)} %get-tuple-element.36), channel_id=1, source_target_pairs={{5,0},{6,1},{7,2},{8,3},{9,4},{10,5},{11,6},{12,7},{13,8},{14,9},{... | collective-permute-start | bytes 786440 | tf_op jit(solution)/shard_map/ppermute | solution.py:40
  10.6 25.5 %collective-permute-start.4 = (bf16[2,256,256]{2,1,0:T(8,128)(2,1)}, bf16[2,256,256]{2,1,0:T(8,128)(2,1)S(1)}, u32[]{:S(2)}, u32[]{:S(2)}) collective-permute-start(bf16[2,256,256]{2,1,0:T(8,128)(2,1)} %get-tuple-element.37), channel_id=1, source_target_pairs={{13,0},{14,1},{15,2},{0,3},{1,4},{2,5},{3,6},{4,7},{5,8},{6,9},{7,... | collective-permute-start | bytes 786440 | tf_op jit(solution)/shard_map/ppermute | solution.py:40
  15.8 24.3 %copy-start.10 = (bf16[2,256,384]{2,1,0:T(8,128)(2,1)S(1)}, bf16[2,256,384]{2,1,0:T(8,128)(2,1)}, u32[]{:S(2)}) copy-start(bf16[2,256,384]{2,1,0:T(8,128)(2,1)} %get-tuple-element.57) | copy-start | bytes 1179652
  15.8 25.2 %copy-start.9 = (bf16[2,256,384]{2,1,0:T(8,128)(2,1)S(1)}, bf16[2,256,384]{2,1,0:T(8,128)(2,1)}, u32[]{:S(2)}) copy-start(bf16[2,256,384]{2,1,0:T(8,128)(2,1)} %get-tuple-element.53) | copy-start | bytes 1179652
  15.8 30.4 %copy-start.8 = (bf16[2,256,384]{2,1,0:T(8,128)(2,1)S(1)}, bf16[2,256,384]{2,1,0:T(8,128)(2,1)}, u32[]{:S(2)}) copy-start(bf16[2,256,384]{2,1,0:T(8,128)(2,1)} %get-tuple-element.55) | copy-start | bytes 1179652
  15.8 31.6 %copy-start.7 = (bf16[2,256,384]{2,1,0:T(8,128)(2,1)S(1)}, bf16[2,256,384]{2,1,0:T(8,128)(2,1)}, u32[]{:S(2)}) copy-start(bf16[2,256,384]{2,1,0:T(8,128)(2,1)} %get-tuple-element.51) | copy-start | bytes 1179652
  22.8 33.7 %copy-start.5 = (s32[32]{0:T(128)S(1)}, s32[32]{0:T(128)}, u32[]{:S(2)}) copy-start(s32[32]{0:T(128)} %placement.1) | copy-start | bytes 388
  23.1 13.0 %collective-permute-start.5 = (bf16[2,256,256]{2,1,0:T(8,128)(2,1)S(1)}, bf16[2,256,256]{2,1,0:T(8,128)(2,1)S(1)}, u32[]{:S(2)}, u32[]{:S(2)}) collective-permute-start(bf16[2,256,256]{2,1,0:T(8,128)(2,1)S(1)} %copy-done.11), channel_id=1, source_target_pairs={{1,0},{2,1},{3,2},{4,3},{5,4},{6,5},{7,6},{8,7},{9,8},{10,9},{11,1... | collective-permute-start | bytes 786440 | tf_op jit(solution)/shard_map/ppermute | solution.py:40
  38.4 16.3 %collective-permute-start.6 = (bf16[256,1280]{1,0:T(8,128)(2,1)}, bf16[256,1280]{1,0:T(8,128)(2,1)S(1)}, u32[]{:S(2)}, u32[]{:S(2)}) collective-permute-start(bf16[256,1280]{1,0:T(8,128)(2,1)} %collective-permute-done.1.refs_0_), channel_id=1, source_target_pairs={{16,0},{0,16},{17,1},{1,17},{18,2},{2,18},{19,3},{3,19},{20,4},{4,... | collective-permute-start | bytes 1966088 | tf_op jit(solution)/shard_map/ppermute | solution.py:31
  40.2 24.1 %collective-permute-start.11 = (bf16[2,256,384]{2,1,0:T(8,128)(2,1)S(1)}, bf16[2,256,384]{2,1,0:T(8,128)(2,1)S(1)}, u32[]{:S(2)}, u32[]{:S(2)}) collective-permute-start(bf16[2,256,384]{2,1,0:T(8,128)(2,1)S(1)} %copy-done.10), channel_id=1, source_target_pairs={{13,0},{14,1},{15,2},{0,3},{1,4},{2,5},{3,6},{4,7},{5,8},{6,9},{7,... | collective-permute-start | bytes 1179656 | tf_op jit(solution)/shard_map/ppermute | solution.py:40
  41.0 23.3 %collective-permute-start.9 = (bf16[2,256,384]{2,1,0:T(8,128)(2,1)S(1)}, bf16[2,256,384]{2,1,0:T(8,128)(2,1)S(1)}, u32[]{:S(2)}, u32[]{:S(2)}) collective-permute-start(bf16[2,256,384]{2,1,0:T(8,128)(2,1)S(1)} %copy-done.9), channel_id=1, source_target_pairs={{5,0},{6,1},{7,2},{8,3},{9,4},{10,5},{11,6},{12,7},{13,8},{14,9},{... | collective-permute-start | bytes 1179656 | tf_op jit(solution)/shard_map/ppermute | solution.py:40
  46.3 36.6 %collective-permute-start.10 = (bf16[2,256,384]{2,1,0:T(8,128)(2,1)S(1)}, bf16[2,256,384]{2,1,0:T(8,128)(2,1)S(1)}, u32[]{:S(2)}, u32[]{:S(2)}) collective-permute-start(bf16[2,256,384]{2,1,0:T(8,128)(2,1)S(1)} %copy-done.8), channel_id=1, source_target_pairs={{9,0},{10,1},{11,2},{12,3},{13,4},{14,5},{15,6},{0,7},{1,8},{2,9},... | collective-permute-start | bytes 1179656 | tf_op jit(solution)/shard_map/ppermute | solution.py:40
  47.4 35.5 %collective-permute-start.8 = (bf16[2,256,384]{2,1,0:T(8,128)(2,1)S(1)}, bf16[2,256,384]{2,1,0:T(8,128)(2,1)S(1)}, u32[]{:S(2)}, u32[]{:S(2)}) collective-permute-start(bf16[2,256,384]{2,1,0:T(8,128)(2,1)S(1)} %copy-done.7), channel_id=1, source_target_pairs={{1,0},{2,1},{3,2},{4,3},{5,4},{6,5},{7,6},{8,7},{9,8},{10,9},{11,1... | collective-permute-start | bytes 1179656 | tf_op jit(solution)/shard_map/ppermute | solution.py:40
  54.7 8.7 %copy-start.3 = (bf16[640,1280]{1,0:T(8,128)(2,1)S(1)}, bf16[640,1280]{1,0:T(8,128)(2,1)}, u32[]{:S(2)}) copy-start(bf16[640,1280]{1,0:T(8,128)(2,1)} %w_mine.3) | copy-start | bytes 4915204
  54.7 8.7 %collective-permute-start.7 = (bf16[512,256]{1,0:T(8,128)(2,1)S(1)}, bf16[512,256]{1,0:T(8,128)(2,1)S(1)}, u32[]{:S(2)}, u32[]{:S(2)}) collective-permute-start(bf16[512,256]{1,0:T(8,128)(2,1)S(1)} %attend.4.refs_0_), channel_id=1, source_target_pairs={{16,0},{0,16},{17,1},{1,17},{18,2},{2,18},{19,3},{3,19},{20,4},{4,... | collective-permute-start | bytes 786440 | tf_op jit(solution)/shard_map/ppermute | solution.py:31
  84.8 6.5 %collective-permute-start.12 = (bf16[512,128]{1,0:T(8,128)(2,1)S(1)}, bf16[512,128]{1,0:T(8,128)(2,1)S(1)}, u32[]{:S(2)}, u32[]{:S(2)}) collective-permute-start(bf16[512,128]{1,0:T(8,128)(2,1)S(1)} %attend.5.refs_0_), channel_id=1, source_target_pairs={{16,0},{0,16},{17,1},{1,17},{18,2},{2,18},{19,3},{3,19},{20,4},{4,... | collective-permute-start | bytes 393224 | tf_op jit(solution)/shard_map/ppermute | solution.py:31
  87.1 5.0 %collective-permute-start.13 = (bf16[512,128]{1,0:T(8,128)(2,1)S(1)}, bf16[512,128]{1,0:T(8,128)(2,1)S(1)}, u32[]{:S(2)}, u32[]{:S(2)}) collective-permute-start(bf16[512,128]{1,0:T(8,128)(2,1)S(1)} %attend.6.refs_1_), channel_id=1, source_target_pairs={{16,0},{0,16},{17,1},{1,17},{18,2},{2,18},{19,3},{3,19},{20,4},{4,... | collective-permute-start | bytes 393224 | tf_op jit(solution)/shard_map/ppermute | solution.py:31
  90.9 5.0 %collective-permute-start.14 = (bf16[512,128]{1,0:T(8,128)(2,1)S(1)}, bf16[512,128]{1,0:T(8,128)(2,1)S(1)}, u32[]{:S(2)}, u32[]{:S(2)}) collective-permute-start(bf16[512,128]{1,0:T(8,128)(2,1)S(1)} %attend.7.refs_2_), channel_id=1, source_target_pairs={{16,0},{0,16},{17,1},{1,17},{18,2},{2,18},{19,3},{3,19},{20,4},{4,... | collective-permute-start | bytes 393224 | tf_op jit(solution)/shard_map/ppermute | solution.py:31
  (3 other events, 14.9 us)

commit v5 on v4

--- a/solution.py
+++ b/solution.py
@@ -16,6 +16,7 @@
 UNITS = ((256,), (128, 128, 128))
 PARTS = 4
 SLOT_ORDER = (2, 1, 3)
+PAGE_ORDER = (2, 1, 3, 0)
 VMEM_LIMIT = 16 * 1024 * 1024
 FIRST_LIMIT = 58 * 1024 * 1024
 
@@ -258,7 +259,7 @@
             ones = jnp.where(keep, 1.0, 0.0).astype(bf16)
             values.append(jnp.concatenate([shown, ones], axis=1))
         for p in range(PMAX):
-            keep = jnp.where(p < depth, 1.0, 0.0).astype(bf16)
+            keep = jnp.where(PAGE_ORDER[p] < depth, 1.0, 0.0).astype(bf16)
             keys.append(pages[p][0, :, page_cols])
             ones = jnp.full((PAGE, LANES), 1.0, bf16) * keep
             values.append(jnp.concatenate([pages[p][1, :, page_cols] * keep, ones], axis=1))
@@ -310,29 +311,54 @@
     return half(mine, w_mine) + half(theirs, w_theirs)
 
 
-def partial_kernel(slices, w_mine, w_theirs, *refs):
+def partial_kernel(slices, hidden, rate, w_mine, w_theirs, *refs):
+    count = len(slices)
+    mine, theirs = refs[:count], refs[count : 2 * count]
+    base, out = refs[2 * count :]
+    for low in range(0, out.shape[0], PAGE):
+        rows = slice(low, low + PAGE)
+        out[rows, :] = projected_heads(slices, rows, mine, theirs, w_mine, w_theirs)
+        anchor = hidden[rows, :].astype(f32) * row_scale_of(hidden[rows, :])
+        base[rows, :] = anchor - rate[...] * anchor
+
+
+def partial_branch(slices, hidden_in, rate, w_mine, w_theirs, mine, theirs):
+    out = jax.ShapeDtypeStruct(hidden_in.shape, f32)
+    vmem = pl.BlockSpec(memory_space=pltpu.VMEM)
+    return pl.pallas_call(
+        functools.partial(partial_kernel, slices),
+        in_specs=[vmem] * (4 + 2 * len(slices)),
+        out_specs=[vmem] * 2,
+        out_shape=[out, out],
+        compiler_params=params(),
+        cost_estimate=cost(),
+        name="partial_branch",
+    )(hidden_in, rate, w_mine, w_theirs, *mine, *theirs)
+
+
+def add_kernel(slices, begun, w_mine, w_theirs, *refs):
     count = len(slices)
     mine, theirs, out = refs[:count], refs[count : 2 * count], refs[2 * count]
     for low in range(0, out.shape[0], PAGE):
         rows = slice(low, low + PAGE)
-        out[rows, :] = projected_heads(slices, rows, mine, theirs, w_mine, w_theirs)
-
-
-def partial_branch(slices, w_mine, w_theirs, mine, theirs):
-    tokens, depth = mine[0].shape[0], w_mine.shape[1]
+        term = projected_heads(slices, rows, mine, theirs, w_mine, w_theirs)
+        out[rows, :] = begun[rows, :] + term
+
+
+def add_branch(slices, begun, w_mine, w_theirs, mine, theirs):
     vmem = pl.BlockSpec(memory_space=pltpu.VMEM)
     return pl.pallas_call(
-        functools.partial(partial_kernel, slices),
-        in_specs=[vmem] * (2 + 2 * len(slices)),
+        functools.partial(add_kernel, slices),
+        in_specs=[vmem] * (3 + 2 * len(slices)),
         out_specs=vmem,
-        out_shape=jax.ShapeDtypeStruct((tokens, depth), f32),
-        compiler_params=params(),
-        cost_estimate=cost(),
-        name="partial_branch",
-    )(w_mine, w_theirs, *mine, *theirs)
-
-
-def finish_kernel(slices, hidden, w_mine, w_theirs, rate, begun, *refs):
+        out_shape=jax.ShapeDtypeStruct(begun.shape, f32),
+        compiler_params=params(),
+        cost_estimate=cost(),
+        name="add_branch",
+    )(begun, w_mine, w_theirs, *mine, *theirs)
+
+
+def finish_kernel(slices, base, w_mine, w_theirs, rate, begun, *refs):
     count = len(slices)
     mine, theirs = refs[:count], refs[count : 2 * count]
     out, buf, sem = refs[2 * count :]
@@ -341,12 +367,8 @@
     for i in range(buf.shape[0]):
         rows = slice(i * step, (i + 1) * step)
         branch = begun[rows, :] + projected_heads(slices, rows, mine, theirs, w_mine, w_theirs)
-        hidden_f = hidden[rows, :].astype(f32)
-        mean = jnp.mean(hidden_f * hidden_f, axis=-1, keepdims=True)
-        anchor = hidden_f * lax.rsqrt(mean + epsilon)
         mean = jnp.mean(branch * branch, axis=-1, keepdims=True)
-        normed = branch * lax.rsqrt(mean + epsilon)
-        updated = anchor + rate[...] * (normed - anchor)
+        updated = base[rows, :] + rate[...] * (branch * lax.rsqrt(mean + epsilon))
         scale = lax.rsqrt(jnp.mean(updated * updated, axis=-1, keepdims=True) + epsilon)
         buf[i] = (updated * scale).astype(bf16)
         copy = pltpu.make_async_copy(buf.at[i], out.at[pl.ds(i * step, step)], sem.at[i])
@@ -356,8 +378,8 @@
         copy.wait()
 
 
-def finish(slices, hidden_in, w_mine, w_theirs, rate, begun, mine, theirs):
-    tokens, depth = hidden_in.shape
+def finish(slices, base, w_mine, w_theirs, rate, begun, mine, theirs):
+    tokens, depth = base.shape
     steps = 4
     vmem = pl.BlockSpec(memory_space=pltpu.VMEM)
     return pl.pallas_call(
@@ -372,7 +394,7 @@
         compiler_params=params(),
         cost_estimate=cost(),
         name="finish",
-    )(hidden_in, w_mine, w_theirs, rate, begun, *mine, *theirs)
+    )(base, w_mine, w_theirs, rate, begun, *mine, *theirs)
 
 
 def body(
@@ -414,11 +436,11 @@
     first = {slot: fetch(page_send[0][slot], slot) for slot in SLOT_ORDER}
     first[0] = fetch(after(page_send[0][0], ready, relay_mine), 0)
     arrived = [first[slot] for slot in SLOT_ORDER]
-    second = {0: fetch(after(page_send[1][0], ready, first[0], relay_mine), 0)}
-    for i, slot in enumerate(SLOT_ORDER):
-        gate = arrived[: i + 1]
-        second[slot] = fetch(after(page_send[1][slot], ready, relay_mine, *gate), slot)
-    pages = [[got[slot] for slot in range(PMAX)] for got in (first, second)]
+    second = {}
+    for slot in PAGE_ORDER:
+        gate = (ready, relay_mine, *arrived, first[0])
+        second[slot] = fetch(after(page_send[1][slot], *gate), slot)
+    pages = [[got[slot] for slot in PAGE_ORDER] for got in (first, second)]
     w_theirs = from_behind(w_out, "kv", 1)
     relay_theirs = from_behind(after(relay_mine, w_theirs, *arrived, first[0]), "kv", 1)
     new_keys, new_values = relay_project(
@@ -429,8 +451,8 @@
     begun = None
     for (g, inner, start, size), (q, k, v) in zip(unit_slices(), projected):
         if g and begun is None:
-            begun = partial_branch(
-                slices[0], w_out, after(w_theirs, new_keys), mine[0], theirs[0]
+            base, begun = partial_branch(
+                slices[0], hidden_in, rate, w_out, after(w_theirs, new_keys), mine[0], theirs[0]
             )
         if g:
             q = after(q, new_keys, begun)
@@ -438,8 +460,9 @@
         mine[g].append(attended)
         theirs[g].append(from_behind(attended, "kv", 1))
         slices[g].append((start, size))
+    begun = add_branch(slices[1][:-1], begun, w_out, w_theirs, mine[1][:-1], theirs[1][:-1])
     layer_out = finish(
-        slices[1], hidden_in, w_out, w_theirs, rate, begun, mine[1], theirs[1]
+        slices[1][-1:], base, w_out, w_theirs, rate, begun, mine[1][-1:], theirs[1][-1:]
     )
     return (layer_out, new_keys, new_values)
 

time: 100 us -> 96.2 us (0.962)
  the two profiles are of different devices: /device:TPU:26 before, /device:TPU:16 now
where the time goes in v5:
time: 96.2 us; the launch traced here: 95.9 us
  waiting for transfers between devices  37.4 us (39%)
  Pallas kernels  32.7 us (34%)
  starting transfers between devices  20.6 us (21%)
  local copies, waits for them, and re-layouts  2.92 us (3%)
  between operations  2.3 us (2%)
    ppermute x9, waiting for transfers between devices, over_blk(): return lax.ppermute(block, ('kv', 'blk'), route)  27 us
    ppermute x6, starting transfers between devices, from_behind(): return lax.ppermute(block, axis, route)  11.1 us
    ppermute x6, waiting for transfers between devices, from_behind(): return lax.ppermute(block, axis, route)  10.4 us
    ppermute x9, starting transfers between devices, over_blk(): return lax.ppermute(block, ('kv', 'blk'), route)  9.5 us
    pallas_call x4, Pallas kernels, attend(): pl.pallas_call(functools.partial(attend_kernel, inner), in_specs=[smem, s...  9.16 us
    pallas_call x1, Pallas kernels, project(): pl.pallas_call(functools.partial(project_kernel, slices), out_shape=outs,...  7 us
    pallas_call x1, Pallas kernels, relay_project(): pl.pallas_call(functools.partial(relay_kernel, group_slices(width), block...  5.11 us
    pallas_call x1, Pallas kernels, pack(): pl.pallas_call(functools.partial(pack_kernel, slices, devices, offsets),...  4.25 us
  transfers between devices with their start and end apart: 15, of which 10 were waited for; matrix products, arithmetic and copies ran while one was open for 0% of the time, Pallas kernels for 30%

profile of v5, /device:TPU:16, one launch (start us, length us, event | category | flops | bytes accessed | tf_op | source)
XLA Modules:
  0.0 95.9 jit_solution(12371720757554458882)
XLA Ops:
  0.6 1.6 %collective-permute-start = (bf16[640,1280]{1,0:T(8,128)(2,1)}, bf16[640,1280]{1,0:T(8,128)(2,1)S(1)}, u32[]{:S(2)}, u32[]{:S(2)}) collective-permute-start(bf16[640,1280]{1,0:T(8,128)(2,1)} %w_mine.5), channel_id=1, source_target_pairs={{16,0},{0,16},{17,1},{1,17},{18,2},{2,18},{19,3},{3,19},{20,4},{4,... | collective-permute-start | bytes 4915208 | tf_op jit(solution)/shard_map/ppermute | solution.py:32
  2.2 2.0 %split_rows.1._ = bf16[256,1280]{1,0:T(8,128)(2,1)} custom-call(s32[1]{0:T(128)} %bitcast.kv_ref, bf16[512,1280]{1,0:T(8,128)(2,1)} %hidden.5), custom_call_target="tpu_custom_call" | custom-call | flops 1 | bytes 1 | tf_op jit(solution)/shard_map/split_rows/pallas_call | solution.py:90
  4.2 1.6 %collective-permute-start.1 = (bf16[256,1280]{1,0:T(8,128)(2,1)}, bf16[256,1280]{1,0:T(8,128)(2,1)}, u32[]{:S(2)}, u32[]{:S(2)}) collective-permute-start(bf16[256,1280]{1,0:T(8,128)(2,1)} %split_rows.1._), channel_id=1, source_target_pairs={{12,0},{13,1},{14,2},{15,3},{0,4},{1,5},{2,6},{3,7},{4,8},{5,9},{6... | collective-permute-start | bytes 1966088 | tf_op jit(solution)/shard_map/ppermute | solution.py:41
  5.9 4.3 %pack.1 = (bf16[2,256,256]{2,1,0:T(8,128)(2,1)}, bf16[2,256,256]{2,1,0:T(8,128)(2,1)}, bf16[2,256,256]{2,1,0:T(8,128)(2,1)}, bf16[2,256,256]{2,1,0:T(8,128)(2,1)...) custom-call(s32[1]{0:T(128)} %bitcast.1.here_ref, ...), custom_call_target="tpu_custom_call" | custom-call | flops 1 | bytes 1 | tf_op jit(solution)/shard_map/pack/pallas_call | solution.py:129
  10.2 3.4 %collective-permute-start.3 = (bf16[2,256,256]{2,1,0:T(8,128)(2,1)}, bf16[2,256,256]{2,1,0:T(8,128)(2,1)S(1)}, u32[]{:S(2)}, u32[]{:S(2)}) collective-permute-start(bf16[2,256,256]{2,1,0:T(8,128)(2,1)} %get-tuple-element.38), channel_id=1, source_target_pairs={{5,0},{6,1},{7,2},{8,3},{9,4},{10,5},{11,6},{12,7},{13,8},{14,9},{... | collective-permute-start | bytes 786440 | tf_op jit(solution)/shard_map/ppermute | solution.py:41
  16.5 7.0 %project.1 = (bf16[512,256]{1,0:T(8,128)(2,1)S(1)}, bf16[512,256]{1,0:T(8,128)(2,1)S(1)}, bf16[512,256]{1,0:T(8,128)(2,1)S(1)}, bf16[512,128]{1,0:T(8,128)(2,1)S...) custom-call(bf16[512,1280]{1,0:T(8,128)(2,1)S(1)} %copy-done.1, ...), custom_call_target="tpu_custom_call" | custom-call | flops 1 | bytes 1 | tf_op jit(solution)/shard_map/project/pallas_call | solution.py:194
  23.6 1.7 %collective-permute-done.1.refs_0_ = bf16[256,1280]{1,0:T(8,128)(2,1)} collective-permute-done((bf16[256,1280]{1,0:T(8,128)(2,1)}, bf16[256,1280]{1,0:T(8,128)(2,1)}, u32[]{:S(2)}, u32[]{:S(2)}) %collective-permute-start.1) | collective-permute-done | bytes 655392 | tf_op jit(solution)/shard_map/ppermute | solution.py:41
  25.3 5.4 %collective-permute-done.2.p0 = bf16[2,256,256]{2,1,0:T(8,128)(2,1)S(1)} collective-permute-done((bf16[2,256,256]{2,1,0:T(8,128)(2,1)}, bf16[2,256,256]{2,1,0:T(8,128)(2,1)S(1)}, u32[]{:S(2)}, u32[]{:S(2)}) %collective-permute-start.2) | collective-permute-done | bytes 262176 | tf_op jit(solution)/shard_map/ppermute | solution.py:41
  30.7 5.9 %collective-permute-done.3.p1 = bf16[2,256,256]{2,1,0:T(8,128)(2,1)S(1)} collective-permute-done((bf16[2,256,256]{2,1,0:T(8,128)(2,1)}, bf16[2,256,256]{2,1,0:T(8,128)(2,1)S(1)}, u32[]{:S(2)}, u32[]{:S(2)}) %collective-permute-start.3) | collective-permute-done | bytes 262176 | tf_op jit(solution)/shard_map/ppermute | solution.py:41
  36.6 5.1 %collective-permute-done.4.p2 = bf16[2,256,256]{2,1,0:T(8,128)(2,1)S(1)} collective-permute-done((bf16[2,256,256]{2,1,0:T(8,128)(2,1)}, bf16[2,256,256]{2,1,0:T(8,128)(2,1)S(1)}, u32[]{:S(2)}, u32[]{:S(2)}) %collective-permute-start.4) | collective-permute-done | bytes 262176 | tf_op jit(solution)/shard_map/ppermute | solution.py:41
  42.0 3.6 %collective-permute-start.6 = (bf16[256,1280]{1,0:T(8,128)(2,1)}, bf16[256,1280]{1,0:T(8,128)(2,1)S(1)}, u32[]{:S(2)}, u32[]{:S(2)}) collective-permute-start(bf16[256,1280]{1,0:T(8,128)(2,1)} %collective-permute-done.1.refs_0_), channel_id=1, source_target_pairs={{16,0},{0,16},{17,1},{1,17},{18,2},{2,18},{19,3},{3,19},{20,4},{4,... | collective-permute-start | bytes 1966088 | tf_op jit(solution)/shard_map/ppermute | solution.py:32
  47.1 2.1 %collective-permute-start.9 = (bf16[2,256,384]{2,1,0:T(8,128)(2,1)S(1)}, bf16[2,256,384]{2,1,0:T(8,128)(2,1)S(1)}, u32[]{:S(2)}, u32[]{:S(2)}) collective-permute-start(bf16[2,256,384]{2,1,0:T(8,128)(2,1)S(1)} %copy-done.11), channel_id=1, source_target_pairs={{5,0},{6,1},{7,2},{8,3},{9,4},{10,5},{11,6},{12,7},{13,8},{14,9},{... | collective-permute-start | bytes 1179656 | tf_op jit(solution)/shard_map/ppermute | solution.py:41
  51.3 3.4 %attend.4.refs_0_ = bf16[512,256]{1,0:T(8,128)(2,1)S(1)} custom-call(s32[1]{0:T(128)S(6)} %copy.16.live_ref, s32[1]{0:T(128)S(6)} %copy.17.depth_ref, bf16[512,256]{1,0:T(8,128)(2,1)S(1)} %get-tuple-element.41.q_ref, bf16[512,256]{1,0:T(8,128)(2,1)S(1)} %get-tuple-element.46.k_ref, bf16[512,256]{1,0:T(8,128)(2,1)S(1)} %get-tuple-element.47.v_ref, ...), custom_call_target="tpu_custom_call" | custom-call | flops 1 | bytes 1 | tf_op jit(solution)/shard_map/attend/pallas_call | solution.py:291
  54.7 6.7 %collective-permute-done.6.refs_1_ = bf16[256,1280]{1,0:T(8,128)(2,1)S(1)} collective-permute-done((bf16[256,1280]{1,0:T(8,128)(2,1)}, bf16[256,1280]{1,0:T(8,128)(2,1)S(1)}, u32[]{:S(2)}, u32[]{:S(2)}) %collective-permute-start.6) | collective-permute-done | bytes 655392 | tf_op jit(solution)/shard_map/ppermute | solution.py:32
  61.3 1.8 %collective-permute-start.7 = (bf16[512,256]{1,0:T(8,128)(2,1)S(1)}, bf16[512,256]{1,0:T(8,128)(2,1)S(1)}, u32[]{:S(2)}, u32[]{:S(2)}) collective-permute-start(bf16[512,256]{1,0:T(8,128)(2,1)S(1)} %attend.4.refs_0_), channel_id=1, source_target_pairs={{16,0},{0,16},{17,1},{1,17},{18,2},{2,18},{19,3},{3,19},{20,4},{4,... | collective-permute-start | bytes 786440 | tf_op jit(solution)/shard_map/ppermute | solution.py:32
  63.2 5.1 %relay_project.1 = (bf16[2,256,640]{2,1,0:T(8,128)(2,1)}, bf16[2,256,640]{2,1,0:T(8,128)(2,1)}) custom-call(s32[1]{0:T(128)} %bitcast.kv_ref, s32[1]{0:T(128)} %bitcast.1.here_ref, s32[32]{0:T(128)S(1)} %copy-done.6, bf16[256,1280]{1,0:T(8,128)(2,1)} %collective-permute-done.1.refs_0_, bf16[256,1280]{1,0:T(8,128)(2,1)S(1)} %collective-permute-done.6.refs_1_, ...), custom_call_target="tpu_custom_call" | custom-call | flops 1 | bytes 1 | tf_op jit(solution)/shard_map/relay_project/pallas_call | solution.py:227
  71.0 8.6 %collective-permute-done.10.p2 = bf16[2,256,384]{2,1,0:T(8,128)(2,1)S(1)} collective-permute-done((bf16[2,256,384]{2,1,0:T(8,128)(2,1)S(1)}, bf16[2,256,384]{2,1,0:T(8,128)(2,1)S(1)}, u32[]{:S(2)}, u32[]{:S(2)}) %collective-permute-start.10) | collective-permute-done | bytes 393248 | tf_op jit(solution)/shard_map/ppermute | solution.py:41
  79.5 1.9 %attend.5.refs_0_ = bf16[512,128]{1,0:T(8,128)(2,1)S(1)} custom-call(s32[1]{0:T(128)S(6)} %copy.16.live_ref, s32[1]{0:T(128)S(6)} %copy.17.depth_ref, bf16[512,128]{1,0:T(8,128)(2,1)S(1)} %get-tuple-element.51.q_ref, bf16[512,128]{1,0:T(8,128)(2,1)S(1)} %get-tuple-element.52.k_ref, bf16[512,128]{1,0:T(8,128)(2,1)S(1)} %get-tuple-element.53.v_ref, ...), custom_call_target="tpu_custom_call" | custom-call | flops 1 | bytes 1 | tf_op jit(solution)/shard_map/attend/pallas_call | solution.py:291
  81.4 2.0 %collective-permute-start.12 = (bf16[512,128]{1,0:T(8,128)(2,1)S(1)}, bf16[512,128]{1,0:T(8,128)(2,1)S(1)}, u32[]{:S(2)}, u32[]{:S(2)}) collective-permute-start(bf16[512,128]{1,0:T(8,128)(2,1)S(1)} %attend.5.refs_0_), channel_id=1, source_target_pairs={{16,0},{0,16},{17,1},{1,17},{18,2},{2,18},{19,3},{3,19},{20,4},{4,... | collective-permute-start | bytes 393224 | tf_op jit(solution)/shard_map/ppermute | solution.py:32
  83.4 1.9 %attend.6.refs_1_ = bf16[512,128]{1,0:T(8,128)(2,1)S(1)} custom-call(s32[1]{0:T(128)S(6)} %copy.16.live_ref, s32[1]{0:T(128)S(6)} %copy.17.depth_ref, bf16[512,128]{1,0:T(8,128)(2,1)S(1)} %get-tuple-element.63.q_ref, bf16[512,128]{1,0:T(8,128)(2,1)S(1)} %get-tuple-element.64.k_ref, bf16[512,128]{1,0:T(8,128)(2,1)S(1)} %get-tuple-element.65.v_ref, ...), custom_call_target="tpu_custom_call" | custom-call | flops 1 | bytes 1 | tf_op jit(solution)/shard_map/attend/pallas_call | solution.py:291
  85.4 2.1 %attend.7.refs_0_ = bf16[512,128]{1,0:T(8,128)(2,1)S(1)} custom-call(s32[1]{0:T(128)S(6)} %copy.16.live_ref, s32[1]{0:T(128)S(6)} %copy.17.depth_ref, bf16[512,128]{1,0:T(8,128)(2,1)S(1)} %get-tuple-element.67.q_ref, bf16[512,128]{1,0:T(8,128)(2,1)S(1)} %get-tuple-element.68.k_ref, bf16[512,128]{1,0:T(8,128)(2,1)S(1)} %get-tuple-element.69.v_ref, ...), custom_call_target="tpu_custom_call" | custom-call | flops 1 | bytes 1 | tf_op jit(solution)/shard_map/attend/pallas_call | solution.py:291
  87.5 2.0 %collective-permute-start.14 = (bf16[512,128]{1,0:T(8,128)(2,1)S(1)}, bf16[512,128]{1,0:T(8,128)(2,1)S(1)}, u32[]{:S(2)}, u32[]{:S(2)}) collective-permute-start(bf16[512,128]{1,0:T(8,128)(2,1)S(1)} %attend.7.refs_0_), channel_id=1, source_target_pairs={{16,0},{0,16},{17,1},{1,17},{18,2},{2,18},{19,3},{3,19},{20,4},{4,... | collective-permute-start | bytes 393224 | tf_op jit(solution)/shard_map/ppermute | solution.py:32
  90.6 1.6 %add_branch.1.begun = f32[512,1280]{1,0:T(8,128)S(1)} custom-call(f32[512,1280]{1,0:T(8,128)S(1)} %get-tuple-element.49.begun, bf16[640,1280]{1,0:T(8,128)(2,1)S(1)} %copy-done, bf16[640,1280]{1,0:T(8,128)(2,1)S(1)} %collective-permute-done.w_theirs, bf16[512,128]{1,0:T(8,128)(2,1)S(1)} %attend.5.refs_0_, bf16[512,128]{1,0:T(8,128)(2,1)S(1)} %attend.6.refs_1_, ...), custom_call_target="tpu_custom_call" | custom-call | flops 1 | bytes 1 | tf_op jit(solution)/shard_map/add_branch/pallas_call | solution.py:350
  93.4 2.3 %finish.1 = bf16[512,1280]{1,0:T(8,128)(2,1)} custom-call(f32[512,1280]{1,0:T(8,128)S(1)} %get-tuple-element.48.base, bf16[640,1280]{1,0:T(8,128)(2,1)S(1)} %copy-done, bf16[640,1280]{1,0:T(8,128)(2,1)S(1)} %collective-permute-done.w_theirs, f32[1,1280]{1,0:T(1,128)S(1)} %reshape.18.rate, f32[512,1280]{1,0:T(8,128)S(1)} %add_branch.1.begun, ...), custom_call_target="tpu_custom_call" | custom-call | flops 1 | bytes 1 | tf_op jit(solution)/shard_map/finish/pallas_call | solution.py:385
  (47 shorter events, 10.8 us)
Async XLA Ops:
  0.6 41.4 %collective-permute-start = (bf16[640,1280]{1,0:T(8,128)(2,1)}, bf16[640,1280]{1,0:T(8,128)(2,1)S(1)}, u32[]{:S(2)}, u32[]{:S(2)}) collective-permute-start(bf16[640,1280]{1,0:T(8,128)(2,1)} %w_mine.5), channel_id=1, source_target_pairs={{16,0},{0,16},{17,1},{1,17},{18,2},{2,18},{19,3},{3,19},{20,4},{4,... | collective-permute-start | bytes 4915208 | tf_op jit(solution)/shard_map/ppermute | solution.py:32
  4.2 21.1 %collective-permute-start.1 = (bf16[256,1280]{1,0:T(8,128)(2,1)}, bf16[256,1280]{1,0:T(8,128)(2,1)}, u32[]{:S(2)}, u32[]{:S(2)}) collective-permute-start(bf16[256,1280]{1,0:T(8,128)(2,1)} %split_rows.1._), channel_id=1, source_target_pairs={{12,0},{13,1},{14,2},{15,3},{0,4},{1,5},{2,6},{3,7},{4,8},{5,9},{6... | collective-permute-start | bytes 1966088 | tf_op jit(solution)/shard_map/ppermute | solution.py:41
  5.9 7.8 %copy-start.2 = (bf16[1280,640]{1,0:T(8,128)(2,1)S(1)}, bf16[1280,640]{1,0:T(8,128)(2,1)}, u32[]{:S(2)}) copy-start(bf16[1280,640]{1,0:T(8,128)(2,1)} %refs_2_.1) | copy-start | bytes 4915204
  10.1 20.6 %collective-permute-start.2 = (bf16[2,256,256]{2,1,0:T(8,128)(2,1)}, bf16[2,256,256]{2,1,0:T(8,128)(2,1)S(1)}, u32[]{:S(2)}, u32[]{:S(2)}) collective-permute-start(bf16[2,256,256]{2,1,0:T(8,128)(2,1)} %get-tuple-element.37), channel_id=1, source_target_pairs={{9,0},{10,1},{11,2},{12,3},{13,4},{14,5},{15,6},{0,7},{1,8},{2,9},... | collective-permute-start | bytes 786440 | tf_op jit(solution)/shard_map/ppermute | solution.py:41
  10.2 26.4 %collective-permute-start.3 = (bf16[2,256,256]{2,1,0:T(8,128)(2,1)}, bf16[2,256,256]{2,1,0:T(8,128)(2,1)S(1)}, u32[]{:S(2)}, u32[]{:S(2)}) collective-permute-start(bf16[2,256,256]{2,1,0:T(8,128)(2,1)} %get-tuple-element.38), channel_id=1, source_target_pairs={{5,0},{6,1},{7,2},{8,3},{9,4},{10,5},{11,6},{12,7},{13,8},{14,9},{... | collective-permute-start | bytes 786440 | tf_op jit(solution)/shard_map/ppermute | solution.py:41
  13.6 28.1 %collective-permute-start.4 = (bf16[2,256,256]{2,1,0:T(8,128)(2,1)}, bf16[2,256,256]{2,1,0:T(8,128)(2,1)S(1)}, u32[]{:S(2)}, u32[]{:S(2)}) collective-permute-start(bf16[2,256,256]{2,1,0:T(8,128)(2,1)} %get-tuple-element.39), channel_id=1, source_target_pairs={{13,0},{14,1},{15,2},{0,3},{1,4},{2,5},{3,6},{4,7},{5,8},{6,9},{7,... | collective-permute-start | bytes 786440 | tf_op jit(solution)/shard_map/ppermute | solution.py:41
  16.5 8.8 %copy-start.13 = (bf16[2,256,256]{2,1,0:T(8,128)(2,1)S(1)}, bf16[2,256,256]{2,1,0:T(8,128)(2,1)}, u32[]{:S(2)}) copy-start(bf16[2,256,256]{2,1,0:T(8,128)(2,1)} %get-tuple-element.42) | copy-start | bytes 786436
  16.5 29.1 %copy-start.12 = (bf16[2,256,384]{2,1,0:T(8,128)(2,1)S(1)}, bf16[2,256,384]{2,1,0:T(8,128)(2,1)}, u32[]{:S(2)}) copy-start(bf16[2,256,384]{2,1,0:T(8,128)(2,1)} %get-tuple-element.55) | copy-start | bytes 1179652
  16.5 30.6 %copy-start.11 = (bf16[2,256,384]{2,1,0:T(8,128)(2,1)S(1)}, bf16[2,256,384]{2,1,0:T(8,128)(2,1)}, u32[]{:S(2)}) copy-start(bf16[2,256,384]{2,1,0:T(8,128)(2,1)} %get-tuple-element.57) | copy-start | bytes 1179652
  16.5 32.7 %copy-start.10 = (bf16[2,256,384]{2,1,0:T(8,128)(2,1)S(1)}, bf16[2,256,384]{2,1,0:T(8,128)(2,1)}, u32[]{:S(2)}) copy-start(bf16[2,256,384]{2,1,0:T(8,128)(2,1)} %get-tuple-element.59) | copy-start | bytes 1179652
  16.5 32.7 %copy-start.9 = (bf16[2,256,384]{2,1,0:T(8,128)(2,1)S(1)}, bf16[2,256,384]{2,1,0:T(8,128)(2,1)}, u32[]{:S(2)}) copy-start(bf16[2,256,384]{2,1,0:T(8,128)(2,1)} %get-tuple-element.61) | copy-start | bytes 1179652
  23.5 39.6 %copy-start.7 = (f32[1280]{0:T(1024)S(1)}, f32[1280]{0:T(1024)}, u32[]{:S(2)}) copy-start(f32[1280]{0:T(1024)} %param.19) | copy-start | bytes 15364
  23.5 39.6 %copy-start.4 = (bf16[1280,640]{1,0:T(8,128)(2,1)S(1)}, bf16[1280,640]{1,0:T(8,128)(2,1)}, u32[]{:S(2)}) copy-start(bf16[1280,640]{1,0:T(8,128)(2,1)} %refs_3_.1) | copy-start | bytes 4915204
  23.6 39.6 %copy-start.6 = (s32[32]{0:T(128)S(1)}, s32[32]{0:T(128)}, u32[]{:S(2)}) copy-start(s32[32]{0:T(128)} %placement.1) | copy-start | bytes 388
  25.3 16.7 %collective-permute-start.5 = (bf16[2,256,256]{2,1,0:T(8,128)(2,1)S(1)}, bf16[2,256,256]{2,1,0:T(8,128)(2,1)S(1)}, u32[]{:S(2)}, u32[]{:S(2)}) collective-permute-start(bf16[2,256,256]{2,1,0:T(8,128)(2,1)S(1)} %copy-done.13), channel_id=1, source_target_pairs={{1,0},{2,1},{3,2},{4,3},{5,4},{6,5},{7,6},{8,7},{9,8},{10,9},{11,1... | collective-permute-start | bytes 786440 | tf_op jit(solution)/shard_map/ppermute | solution.py:41
  42.0 19.3 %collective-permute-start.6 = (bf16[256,1280]{1,0:T(8,128)(2,1)}, bf16[256,1280]{1,0:T(8,128)(2,1)S(1)}, u32[]{:S(2)}, u32[]{:S(2)}) collective-permute-start(bf16[256,1280]{1,0:T(8,128)(2,1)} %collective-permute-done.1.refs_0_), channel_id=1, source_target_pairs={{16,0},{0,16},{17,1},{1,17},{18,2},{2,18},{19,3},{3,19},{20,4},{4,... | collective-permute-start | bytes 1966088 | tf_op jit(solution)/shard_map/ppermute | solution.py:32
  45.6 25.3 %collective-permute-start.8 = (bf16[2,256,384]{2,1,0:T(8,128)(2,1)S(1)}, bf16[2,256,384]{2,1,0:T(8,128)(2,1)S(1)}, u32[]{:S(2)}, u32[]{:S(2)}) collective-permute-start(bf16[2,256,384]{2,1,0:T(8,128)(2,1)S(1)} %copy-done.12), channel_id=1, source_target_pairs={{9,0},{10,1},{11,2},{12,3},{13,4},{14,5},{15,6},{0,7},{1,8},{2,9},... | collective-permute-start | bytes 1179656 | tf_op jit(solution)/shard_map/ppermute | solution.py:41
  47.1 23.8 %collective-permute-start.9 = (bf16[2,256,384]{2,1,0:T(8,128)(2,1)S(1)}, bf16[2,256,384]{2,1,0:T(8,128)(2,1)S(1)}, u32[]{:S(2)}, u32[]{:S(2)}) collective-permute-start(bf16[2,256,384]{2,1,0:T(8,128)(2,1)S(1)} %copy-done.11), channel_id=1, source_target_pairs={{5,0},{6,1},{7,2},{8,3},{9,4},{10,5},{11,6},{12,7},{13,8},{14,9},{... | collective-permute-start | bytes 1179656 | tf_op jit(solution)/shard_map/ppermute | solution.py:41
  49.2 30.3 %collective-permute-start.10 = (bf16[2,256,384]{2,1,0:T(8,128)(2,1)S(1)}, bf16[2,256,384]{2,1,0:T(8,128)(2,1)S(1)}, u32[]{:S(2)}, u32[]{:S(2)}) collective-permute-start(bf16[2,256,384]{2,1,0:T(8,128)(2,1)S(1)} %copy-done.10), channel_id=1, source_target_pairs={{13,0},{14,1},{15,2},{0,3},{1,4},{2,5},{3,6},{4,7},{5,8},{6,9},{7,... | collective-permute-start | bytes 1179656 | tf_op jit(solution)/shard_map/ppermute | solution.py:41
  49.2 30.3 %collective-permute-start.11 = (bf16[2,256,384]{2,1,0:T(8,128)(2,1)S(1)}, bf16[2,256,384]{2,1,0:T(8,128)(2,1)S(1)}, u32[]{:S(2)}, u32[]{:S(2)}) collective-permute-start(bf16[2,256,384]{2,1,0:T(8,128)(2,1)S(1)} %copy-done.9), channel_id=1, source_target_pairs={{1,0},{2,1},{3,2},{4,3},{5,4},{6,5},{7,6},{8,7},{9,8},{10,9},{11,1... | collective-permute-start | bytes 1179656 | tf_op jit(solution)/shard_map/ppermute | solution.py:41
  61.3 8.4 %collective-permute-start.7 = (bf16[512,256]{1,0:T(8,128)(2,1)S(1)}, bf16[512,256]{1,0:T(8,128)(2,1)S(1)}, u32[]{:S(2)}, u32[]{:S(2)}) collective-permute-start(bf16[512,256]{1,0:T(8,128)(2,1)S(1)} %attend.4.refs_0_), channel_id=1, source_target_pairs={{16,0},{0,16},{17,1},{1,17},{18,2},{2,18},{19,3},{3,19},{20,4},{4,... | collective-permute-start | bytes 786440 | tf_op jit(solution)/shard_map/ppermute | solution.py:32
  81.4 8.1 %collective-permute-start.12 = (bf16[512,128]{1,0:T(8,128)(2,1)S(1)}, bf16[512,128]{1,0:T(8,128)(2,1)S(1)}, u32[]{:S(2)}, u32[]{:S(2)}) collective-permute-start(bf16[512,128]{1,0:T(8,128)(2,1)S(1)} %attend.5.refs_0_), channel_id=1, source_target_pairs={{16,0},{0,16},{17,1},{1,17},{18,2},{2,18},{19,3},{3,19},{20,4},{4,... | collective-permute-start | bytes 393224 | tf_op jit(solution)/shard_map/ppermute | solution.py:32
  85.2 5.4 %collective-permute-start.13 = (bf16[512,128]{1,0:T(8,128)(2,1)S(1)}, bf16[512,128]{1,0:T(8,128)(2,1)S(1)}, u32[]{:S(2)}, u32[]{:S(2)}) collective-permute-start(bf16[512,128]{1,0:T(8,128)(2,1)S(1)} %attend.6.refs_1_), channel_id=1, source_target_pairs={{16,0},{0,16},{17,1},{1,17},{18,2},{2,18},{19,3},{3,19},{20,4},{4,... | collective-permute-start | bytes 393224 | tf_op jit(solution)/shard_map/ppermute | solution.py:32
  87.5 5.9 %collective-permute-start.14 = (bf16[512,128]{1,0:T(8,128)(2,1)S(1)}, bf16[512,128]{1,0:T(8,128)(2,1)S(1)}, u32[]{:S(2)}, u32[]{:S(2)}) collective-permute-start(bf16[512,128]{1,0:T(8,128)(2,1)S(1)} %attend.7.refs_0_), channel_id=1, source_target_pairs={{16,0},{0,16},{17,1},{1,17},{18,2},{2,18},{19,3},{3,19},{20,4},{4,... | collective-permute-start | bytes 393224 | tf_op jit(solution)/shard_map/ppermute | solution.py:32
  (5 other events, 24.9 us)

commit v6 on v5

--- a/solution.py
+++ b/solution.py
@@ -17,6 +17,7 @@
 PARTS = 4
 SLOT_ORDER = (2, 1, 3)
 PAGE_ORDER = (2, 1, 3, 0)
+EARLY = 2
 VMEM_LIMIT = 16 * 1024 * 1024
 FIRST_LIMIT = 58 * 1024 * 1024
 
@@ -237,66 +238,115 @@
     )(kv_index, here, placement, mine, theirs, wk, wv, gain)
 
 
-def attend_kernel(inner, live_ref, depth_ref, q_ref, k_ref, v_ref, p0, p1, p2, p3, out):
-    pages = (p0, p1, p2, p3)
-    tokens, width = q_ref.shape
-    live, depth = live_ref[0], depth_ref[0]
-    lane = lax.broadcasted_iota(jnp.int32, (1, LANES), 1)
+def weighted(q, blocks):
+    lane = lax.broadcasted_iota(jnp.int32, (1, LANES), 1) // HD
+    sums = []
+    for side in range(2):
+        q_side = jnp.where(lane == side, q, jnp.zeros_like(q))
+        acc = jnp.zeros((q.shape[0], 2 * LANES), f32)
+        for keys, values, visible in blocks:
+            scores = lax.dot_general(
+                q_side, keys, (((1,), (1,)), ((), ())), preferred_element_type=f32
+            )
+            weights = jnp.exp(scores)
+            if visible is not None:
+                weights = jnp.where(visible, weights, 0.0)
+            acc += jnp.dot(weights.astype(bf16), values, preferred_element_type=f32)
+        sums.append(acc)
+    mixed = jnp.where(lane == 0, sums[0][:, :LANES], sums[1][:, :LANES])
+    totals = jnp.where(lane == 0, sums[0][:, LANES:], sums[1][:, LANES:])
+    return mixed, totals
+
+
+def own_blocks(k_ref, v_ref, live, cols):
     row = lax.broadcasted_iota(jnp.int32, (PAGE, PAGE), 0)
     col = lax.broadcasted_iota(jnp.int32, (PAGE, PAGE), 1)
-    causal = col <= row
     key_row = lax.broadcasted_iota(jnp.int32, (PAGE, LANES), 0)
-    blocks = tokens // PAGE
+    blocks = []
+    for b in range(k_ref.shape[0] // PAGE):
+        rows = slice(b * PAGE, (b + 1) * PAGE)
+        keep = (key_row + b * PAGE) < live
+        shown = jnp.where(keep, v_ref[rows, cols].astype(f32), 0.0).astype(bf16)
+        ones = jnp.where(keep, 1.0, 0.0).astype(bf16)
+        blocks.append((k_ref[rows, cols], jnp.concatenate([shown, ones], axis=1)))
+    return blocks, col <= row
+
+
+def page_blocks(pages, slots, depth, cols):
+    blocks = []
+    for page, slot in zip(pages, slots):
+        keep = jnp.where(slot < depth, 1.0, 0.0).astype(bf16)
+        ones = jnp.full((PAGE, LANES), 1.0, bf16) * keep
+        values = jnp.concatenate([page[1, :, cols] * keep, ones], axis=1)
+        blocks.append((page[0, :, cols], values, None))
+    return blocks
+
+
+def attend_kernel(inner, slots, live_ref, depth_ref, q_ref, k_ref, v_ref, *refs):
+    pages, outs = refs[: len(slots)], refs[len(slots) :]
+    tokens, width = q_ref.shape
+    for start in range(0, width, LANES):
+        cols = slice(start, start + LANES)
+        own, causal = own_blocks(k_ref, v_ref, live_ref[0], cols)
+        page_cols = slice(inner + start, inner + start + LANES)
+        cached = page_blocks(pages, slots, depth_ref[0], page_cols)
+        for b in range(tokens // PAGE):
+            rows = slice(b * PAGE, (b + 1) * PAGE)
+            blocks = [own[j] + (causal if j == b else None,) for j in range(b + 1)]
+            mixed, totals = weighted(q_ref[rows, cols], blocks + cached)
+            if len(outs) == 1:
+                outs[0][rows, cols] = (mixed / totals).astype(bf16)
+            else:
+                outs[0][rows, cols] = mixed
+                outs[1][rows, cols] = totals
+
+
+def attend(live, depth, q, k, v, pages, slots, inner):
+    smem = pl.BlockSpec(memory_space=pltpu.SMEM)
+    vmem = pl.BlockSpec(memory_space=pltpu.VMEM)
+    if len(slots) == PMAX:
+        out = [jax.ShapeDtypeStruct(q.shape, bf16)]
+    else:
+        out = [jax.ShapeDtypeStruct(q.shape, f32)] * 2
+    result = pl.pallas_call(
+        functools.partial(attend_kernel, inner, slots),
+        in_specs=[smem, smem] + [vmem] * (3 + len(slots)),
+        out_specs=[vmem] * len(out),
+        out_shape=out,
+        compiler_params=params(),
+        cost_estimate=cost(),
+        name="attend",
+    )(live, depth, q, k, v, *pages)
+    return result[0] if len(out) == 1 else result
+
+
+def attend_rest_kernel(inner, slots, depth_ref, q_ref, mixed_ref, totals_ref, *refs):
+    pages, out = refs[: len(slots)], refs[len(slots)]
+    tokens, width = q_ref.shape
     for start in range(0, width, LANES):
         cols = slice(start, start + LANES)
         page_cols = slice(inner + start, inner + start + LANES)
-        keys, values = [], []
-        for b in range(blocks):
+        cached = page_blocks(pages, slots, depth_ref[0], page_cols)
+        for b in range(tokens // PAGE):
             rows = slice(b * PAGE, (b + 1) * PAGE)
-            keep = (key_row + b * PAGE) < live
-            keys.append(k_ref[rows, cols])
-            shown = jnp.where(keep, v_ref[rows, cols].astype(f32), 0.0).astype(bf16)
-            ones = jnp.where(keep, 1.0, 0.0).astype(bf16)
-            values.append(jnp.concatenate([shown, ones], axis=1))
-        for p in range(PMAX):
-            keep = jnp.where(PAGE_ORDER[p] < depth, 1.0, 0.0).astype(bf16)
-            keys.append(pages[p][0, :, page_cols])
-            ones = jnp.full((PAGE, LANES), 1.0, bf16) * keep
-            values.append(jnp.concatenate([pages[p][1, :, page_cols] * keep, ones], axis=1))
-        for b in range(blocks):
-            rows = slice(b * PAGE, (b + 1) * PAGE)
-            q = q_ref[rows, cols]
-            ratios = []
-            for side in range(2):
-                q_side = jnp.where((lane // HD) == side, q, jnp.zeros_like(q))
-                acc = jnp.zeros((PAGE, 2 * LANES), f32)
-                for j in list(range(b + 1)) + list(range(blocks, blocks + PMAX)):
-                    scores = lax.dot_general(
-                        q_side, keys[j], (((1,), (1,)), ((), ())), preferred_element_type=f32
-                    )
-                    weights = jnp.exp(scores)
-                    if j == b:
-                        weights = jnp.where(causal, weights, 0.0)
-                    acc += jnp.dot(weights.astype(bf16), values[j], preferred_element_type=f32)
-                ratios.append(acc[:, :LANES] / acc[:, LANES:])
-            out[rows, cols] = jnp.where((lane // HD) == 0, ratios[0], ratios[1]).astype(bf16)
-
-
-def attend(live, depth, q, k, v, pages, inner):
-    tokens, width = q.shape
-    heads = width // HD
+            mixed, totals = weighted(q_ref[rows, cols], cached)
+            mixed += mixed_ref[rows, cols]
+            totals += totals_ref[rows, cols]
+            out[rows, cols] = (mixed / totals).astype(bf16)
+
+
+def attend_rest(depth, q, mixed, totals, pages, slots, inner):
     smem = pl.BlockSpec(memory_space=pltpu.SMEM)
     vmem = pl.BlockSpec(memory_space=pltpu.VMEM)
-    keys = tokens + PMAX * PAGE
     return pl.pallas_call(
-        functools.partial(attend_kernel, inner),
-        in_specs=[smem, smem] + [vmem] * 7,
+        functools.partial(attend_rest_kernel, inner, slots),
+        in_specs=[smem] + [vmem] * (3 + len(slots)),
         out_specs=vmem,
-        out_shape=jax.ShapeDtypeStruct((tokens, width), bf16),
-        compiler_params=params(),
-        cost_estimate=cost(),
-        name="attend",
-    )(live, depth, q, k, v, *pages)
+        out_shape=jax.ShapeDtypeStruct(q.shape, bf16),
+        compiler_params=params(),
+        cost_estimate=cost(),
+        name="attend_rest",
+    )(depth, q, mixed, totals, *pages)
 
 
 def projected_heads(slices, rows, mine, theirs, w_mine, w_theirs):
@@ -448,18 +498,29 @@
     )
 
     mine, theirs, slices = [[], []], [[], []], [[], []]
-    begun = None
-    for (g, inner, start, size), (q, k, v) in zip(unit_slices(), projected):
-        if g and begun is None:
-            base, begun = partial_branch(
-                slices[0], hidden_in, rate, w_out, after(w_theirs, new_keys), mine[0], theirs[0]
-            )
-        if g:
-            q = after(q, new_keys, begun)
-        attended = attend(req_len, prefix_len, q, k, v, pages[g], inner)
+    units = list(zip(unit_slices(), projected))
+
+    def swap(g, start, size, attended):
         mine[g].append(attended)
         theirs[g].append(from_behind(attended, "kv", 1))
         slices[g].append((start, size))
+
+    for (g, inner, start, size), (q, k, v) in units:
+        if g == 0:
+            swap(g, start, size, attend(req_len, prefix_len, q, k, v, pages[0], PAGE_ORDER, inner))
+    base, begun = partial_branch(
+        slices[0], hidden_in, rate, w_out, after(w_theirs, new_keys), mine[0], theirs[0]
+    )
+    early, late = PAGE_ORDER[:EARLY], PAGE_ORDER[EARLY:]
+    sums = []
+    for (g, inner, _, _), (q, k, v) in units:
+        if g:
+            q = after(q, new_keys, begun)
+            sums.append(attend(req_len, prefix_len, q, k, v, pages[g][:EARLY], early, inner))
+    rest = [unit for unit in units if unit[0][0]]
+    for ((g, inner, start, size), (q, _, _)), (mixed, totals) in zip(rest, sums):
+        q = after(q, *[total for _, total in sums])
+        swap(g, start, size, attend_rest(prefix_len, q, mixed, totals, pages[g][EARLY:], late, inner))
     begun = add_branch(slices[1][:-1], begun, w_out, w_theirs, mine[1][:-1], theirs[1][:-1])
     layer_out = finish(
         slices[1][-1:], base, w_out, w_theirs, rate, begun, mine[1][-1:], theirs[1][-1:]

time: 96.2 us -> 98.5 us (1.024)
  the two profiles are of different devices: /device:TPU:16 before, /device:TPU:8 now
where the time goes in v6:
time: 98.5 us; the launch traced here: 98.2 us
  waiting for transfers between devices  40 us (41%)
  Pallas kernels  33.4 us (34%)
  starting transfers between devices  19.5 us (20%)
  local copies, waits for them, and re-layouts  2.92 us (3%)
  between operations  2.32 us (2%)
    ppermute x9, waiting for transfers between devices, over_blk(): return lax.ppermute(block, ('kv', 'blk'), route)  26.9 us
    ppermute x6, waiting for transfers between devices, from_behind(): return lax.ppermute(block, axis, route)  13.2 us
    ppermute x9, starting transfers between devices, over_blk(): return lax.ppermute(block, ('kv', 'blk'), route)  13 us
    pallas_call x4, Pallas kernels, attend(): pl.pallas_call(functools.partial(attend_kernel, inner, slots), in_specs=[...  7.25 us
    pallas_call x1, Pallas kernels, project(): pl.pallas_call(functools.partial(project_kernel, slices), out_shape=outs,...  6.95 us
    ppermute x6, starting transfers between devices, from_behind(): return lax.ppermute(block, axis, route)  6.59 us
    pallas_call x1, Pallas kernels, relay_project(): pl.pallas_call(functools.partial(relay_kernel, group_slices(width), block...  5.06 us
    pallas_call x1, Pallas kernels, pack(): pl.pallas_call(functools.partial(pack_kernel, slices, devices, offsets),...  4.11 us
  transfers between devices with their start and end apart: 15, of which 9 were waited for; matrix products, arithmetic and copies ran while one was open for 0% of the time, Pallas kernels for 31%

profile of v6, /device:TPU:8, one launch (start us, length us, event | category | flops | bytes accessed | tf_op | source)
XLA Modules:
  0.0 98.2 jit_solution(1799281135901146644)
XLA Ops:
  0.6 1.6 %collective-permute-start = (bf16[640,1280]{1,0:T(8,128)(2,1)}, bf16[640,1280]{1,0:T(8,128)(2,1)S(1)}, u32[]{:S(2)}, u32[]{:S(2)}) collective-permute-start(bf16[640,1280]{1,0:T(8,128)(2,1)} %w_mine.5), channel_id=1, source_target_pairs={{16,0},{0,16},{17,1},{1,17},{18,2},{2,18},{19,3},{3,19},{20,4},{4,... | collective-permute-start | bytes 4915208 | tf_op jit(solution)/shard_map/ppermute | solution.py:33
  2.2 2.0 %split_rows.1._ = bf16[256,1280]{1,0:T(8,128)(2,1)} custom-call(s32[1]{0:T(128)} %bitcast.kv_ref, bf16[512,1280]{1,0:T(8,128)(2,1)} %hidden.5), custom_call_target="tpu_custom_call" | custom-call | flops 1 | bytes 1 | tf_op jit(solution)/shard_map/split_rows/pallas_call | solution.py:91
  4.2 1.6 %collective-permute-start.1 = (bf16[256,1280]{1,0:T(8,128)(2,1)}, bf16[256,1280]{1,0:T(8,128)(2,1)}, u32[]{:S(2)}, u32[]{:S(2)}) collective-permute-start(bf16[256,1280]{1,0:T(8,128)(2,1)} %split_rows.1._), channel_id=1, source_target_pairs={{12,0},{13,1},{14,2},{15,3},{0,4},{1,5},{2,6},{3,7},{4,8},{5,9},{6... | collective-permute-start | bytes 1966088 | tf_op jit(solution)/shard_map/ppermute | solution.py:42
  5.9 4.1 %pack.1 = (bf16[2,256,256]{2,1,0:T(8,128)(2,1)}, bf16[2,256,256]{2,1,0:T(8,128)(2,1)}, bf16[2,256,256]{2,1,0:T(8,128)(2,1)}, bf16[2,256,256]{2,1,0:T(8,128)(2,1)...) custom-call(s32[1]{0:T(128)} %bitcast.1.here_ref, ...), custom_call_target="tpu_custom_call" | custom-call | flops 1 | bytes 1 | tf_op jit(solution)/shard_map/pack/pallas_call | solution.py:130
  10.0 1.4 %collective-permute-start.2 = (bf16[2,256,256]{2,1,0:T(8,128)(2,1)}, bf16[2,256,256]{2,1,0:T(8,128)(2,1)S(1)}, u32[]{:S(2)}, u32[]{:S(2)}) collective-permute-start(bf16[2,256,256]{2,1,0:T(8,128)(2,1)} %get-tuple-element.46), channel_id=1, source_target_pairs={{9,0},{10,1},{11,2},{12,3},{13,4},{14,5},{15,6},{0,7},{1,8},{2,9},... | collective-permute-start | bytes 786440 | tf_op jit(solution)/shard_map/ppermute | solution.py:42
  11.4 2.2 %collective-permute-start.3 = (bf16[2,256,256]{2,1,0:T(8,128)(2,1)}, bf16[2,256,256]{2,1,0:T(8,128)(2,1)S(1)}, u32[]{:S(2)}, u32[]{:S(2)}) collective-permute-start(bf16[2,256,256]{2,1,0:T(8,128)(2,1)} %get-tuple-element.47), channel_id=1, source_target_pairs={{5,0},{6,1},{7,2},{8,3},{9,4},{10,5},{11,6},{12,7},{13,8},{14,9},{... | collective-permute-start | bytes 786440 | tf_op jit(solution)/shard_map/ppermute | solution.py:42
  13.7 1.4 %copy-done.3 = bf16[1280,640]{1,0:T(8,128)(2,1)S(1)} copy-done((bf16[1280,640]{1,0:T(8,128)(2,1)S(1)}, bf16[1280,640]{1,0:T(8,128)(2,1)}, u32[]{:S(2)}) %copy-start.3) | copy-done | bytes 1638424
  15.1 1.4 %copy-done.5 = bf16[1280,640]{1,0:T(8,128)(2,1)S(1)} copy-done((bf16[1280,640]{1,0:T(8,128)(2,1)S(1)}, bf16[1280,640]{1,0:T(8,128)(2,1)}, u32[]{:S(2)}) %copy-start.5) | copy-done | bytes 1638424
  16.5 6.9 %project.1 = (bf16[512,256]{1,0:T(8,128)(2,1)S(1)}, bf16[512,256]{1,0:T(8,128)(2,1)S(1)}, bf16[512,256]{1,0:T(8,128)(2,1)S(1)}, bf16[512,128]{1,0:T(8,128)(2,1)S...) custom-call(bf16[512,1280]{1,0:T(8,128)(2,1)S(1)} %copy-done.1, ...), custom_call_target="tpu_custom_call" | custom-call | flops 1 | bytes 1 | tf_op jit(solution)/shard_map/project/pallas_call | solution.py:195
  23.9 1.5 %collective-permute-start.5 = (bf16[2,256,256]{2,1,0:T(8,128)(2,1)S(1)}, bf16[2,256,256]{2,1,0:T(8,128)(2,1)S(1)}, u32[]{:S(2)}, u32[]{:S(2)}) collective-permute-start(bf16[2,256,256]{2,1,0:T(8,128)(2,1)S(1)} %copy-done.13), channel_id=1, source_target_pairs={{1,0},{2,1},{3,2},{4,3},{5,4},{6,5},{7,6},{8,7},{9,8},{10,9},{11,1... | collective-permute-start | bytes 786440 | tf_op jit(solution)/shard_map/ppermute | solution.py:42
  25.4 12.8 %collective-permute-done.2.refs_0_ = bf16[2,256,256]{2,1,0:T(8,128)(2,1)S(1)} collective-permute-done((bf16[2,256,256]{2,1,0:T(8,128)(2,1)}, bf16[2,256,256]{2,1,0:T(8,128)(2,1)S(1)}, u32[]{:S(2)}, u32[]{:S(2)}) %collective-permute-start.2) | collective-permute-done | bytes 262176 | tf_op jit(solution)/shard_map/ppermute | solution.py:42
  38.2 5.7 %collective-permute-done.3.refs_1_ = bf16[2,256,256]{2,1,0:T(8,128)(2,1)S(1)} collective-permute-done((bf16[2,256,256]{2,1,0:T(8,128)(2,1)}, bf16[2,256,256]{2,1,0:T(8,128)(2,1)S(1)}, u32[]{:S(2)}, u32[]{:S(2)}) %collective-permute-start.3) | collective-permute-done | bytes 262176 | tf_op jit(solution)/shard_map/ppermute | solution.py:42
  44.8 3.6 %collective-permute-start.9 = (bf16[2,256,384]{2,1,0:T(8,128)(2,1)S(1)}, bf16[2,256,384]{2,1,0:T(8,128)(2,1)S(1)}, u32[]{:S(2)}, u32[]{:S(2)}) collective-permute-start(bf16[2,256,384]{2,1,0:T(8,128)(2,1)S(1)} %copy-done.11), channel_id=1, source_target_pairs={{5,0},{6,1},{7,2},{8,3},{9,4},{10,5},{11,6},{12,7},{13,8},{14,9},{... | collective-permute-start | bytes 1179656 | tf_op jit(solution)/shard_map/ppermute | solution.py:42
  48.4 1.5 %collective-permute-start.10 = (bf16[2,256,384]{2,1,0:T(8,128)(2,1)S(1)}, bf16[2,256,384]{2,1,0:T(8,128)(2,1)S(1)}, u32[]{:S(2)}, u32[]{:S(2)}) collective-permute-start(bf16[2,256,384]{2,1,0:T(8,128)(2,1)S(1)} %copy-done.10), channel_id=1, source_target_pairs={{13,0},{14,1},{15,2},{0,3},{1,4},{2,5},{3,6},{4,7},{5,8},{6,9},{7,... | collective-permute-start | bytes 1179656 | tf_op jit(solution)/shard_map/ppermute | solution.py:42
  52.3 3.4 %attend.4.refs_0_ = bf16[512,256]{1,0:T(8,128)(2,1)S(1)} custom-call(s32[1]{0:T(128)S(6)} %copy.16.live_ref, s32[1]{0:T(128)S(6)} %copy.17.depth_ref, bf16[512,256]{1,0:T(8,128)(2,1)S(1)} %get-tuple-element.50.q_ref, bf16[512,256]{1,0:T(8,128)(2,1)S(1)} %get-tuple-element.55.k_ref, bf16[512,256]{1,0:T(8,128)(2,1)S(1)} %get-tuple-element.56.v_ref, ...), custom_call_target="tpu_custom_call" | custom-call | flops 1 | bytes 1 | tf_op jit(solution)/shard_map/attend/pallas_call | solution.py:311
  55.7 6.1 %collective-permute-done.6.refs_1_ = bf16[256,1280]{1,0:T(8,128)(2,1)S(1)} collective-permute-done((bf16[256,1280]{1,0:T(8,128)(2,1)}, bf16[256,1280]{1,0:T(8,128)(2,1)S(1)}, u32[]{:S(2)}, u32[]{:S(2)}) %collective-permute-start.6) | collective-permute-done | bytes 655392 | tf_op jit(solution)/shard_map/ppermute | solution.py:33
  62.1 5.1 %relay_project.1 = (bf16[2,256,640]{2,1,0:T(8,128)(2,1)}, bf16[2,256,640]{2,1,0:T(8,128)(2,1)}) custom-call(s32[1]{0:T(128)} %bitcast.kv_ref, s32[1]{0:T(128)} %bitcast.1.here_ref, s32[32]{0:T(128)S(1)} %copy-done.6, bf16[256,1280]{1,0:T(8,128)(2,1)} %collective-permute-done.1.refs_0_, bf16[256,1280]{1,0:T(8,128)(2,1)S(1)} %collective-permute-done.6.refs_1_, ...), custom_call_target="tpu_custom_call" | custom-call | flops 1 | bytes 1 | tf_op jit(solution)/shard_map/relay_project/pallas_call | solution.py:228
  67.1 2.8 %collective-permute-done.7.refs_1_ = bf16[512,256]{1,0:T(8,128)(2,1)S(1)} collective-permute-done((bf16[512,256]{1,0:T(8,128)(2,1)S(1)}, bf16[512,256]{1,0:T(8,128)(2,1)S(1)}, u32[]{:S(2)}, u32[]{:S(2)}) %collective-permute-start.7) | collective-permute-done | bytes 262176 | tf_op jit(solution)/shard_map/ppermute | solution.py:33
  71.1 7.9 %collective-permute-done.9.refs_1_ = bf16[2,256,384]{2,1,0:T(8,128)(2,1)S(1)} collective-permute-done((bf16[2,256,384]{2,1,0:T(8,128)(2,1)S(1)}, bf16[2,256,384]{2,1,0:T(8,128)(2,1)S(1)}, u32[]{:S(2)}, u32[]{:S(2)}) %collective-permute-start.9) | collective-permute-done | bytes 393248 | tf_op jit(solution)/shard_map/ppermute | solution.py:42
  83.9 1.7 %collective-permute-start.12 = (bf16[512,128]{1,0:T(8,128)(2,1)S(1)}, bf16[512,128]{1,0:T(8,128)(2,1)S(1)}, u32[]{:S(2)}, u32[]{:S(2)}) collective-permute-start(bf16[512,128]{1,0:T(8,128)(2,1)S(1)} %attend_rest.3.refs_0_), channel_id=1, source_target_pairs={{16,0},{0,16},{17,1},{1,17},{18,2},{2,18},{19,3},{3,19},{20,4},{4,... | collective-permute-start | bytes 393224 | tf_op jit(solution)/shard_map/ppermute | solution.py:33
  88.1 1.7 %collective-permute-start.14 = (bf16[512,128]{1,0:T(8,128)(2,1)S(1)}, bf16[512,128]{1,0:T(8,128)(2,1)S(1)}, u32[]{:S(2)}, u32[]{:S(2)}) collective-permute-start(bf16[512,128]{1,0:T(8,128)(2,1)S(1)} %attend_rest.5.refs_0_), channel_id=1, source_target_pairs={{16,0},{0,16},{17,1},{1,17},{18,2},{2,18},{19,3},{3,19},{20,4},{4,... | collective-permute-start | bytes 393224 | tf_op jit(solution)/shard_map/ppermute | solution.py:33
  90.3 2.9 %collective-permute-done.13.refs_3_ = bf16[512,128]{1,0:T(8,128)(2,1)S(1)} collective-permute-done((bf16[512,128]{1,0:T(8,128)(2,1)S(1)}, bf16[512,128]{1,0:T(8,128)(2,1)S(1)}, u32[]{:S(2)}, u32[]{:S(2)}) %collective-permute-start.13) | collective-permute-done | bytes 131104 | tf_op jit(solution)/shard_map/ppermute | solution.py:33
  93.3 1.5 %add_branch.1.begun = f32[512,1280]{1,0:T(8,128)S(1)} custom-call(f32[512,1280]{1,0:T(8,128)S(1)} %get-tuple-element.58.begun, bf16[640,1280]{1,0:T(8,128)(2,1)S(1)} %copy-done, bf16[640,1280]{1,0:T(8,128)(2,1)S(1)} %collective-permute-done.w_theirs, bf16[512,128]{1,0:T(8,128)(2,1)S(1)} %attend_rest.3.refs_0_, bf16[512,128]{1,0:T(8,128)(2,1)S(1)} %attend_rest.4.refs_1_, ...), custom_call_target="tpu_custom_call" | custom-call | flops 1 | bytes 1 | tf_op jit(solution)/shard_map/add_branch/pallas_call | solution.py:400
  95.7 2.3 %finish.1 = bf16[512,1280]{1,0:T(8,128)(2,1)} custom-call(f32[512,1280]{1,0:T(8,128)S(1)} %get-tuple-element.57.base, bf16[640,1280]{1,0:T(8,128)(2,1)S(1)} %copy-done, bf16[640,1280]{1,0:T(8,128)(2,1)S(1)} %collective-permute-done.w_theirs, f32[1,1280]{1,0:T(1,128)S(1)} %reshape.18.rate, f32[512,1280]{1,0:T(8,128)S(1)} %add_branch.1.begun, ...), custom_call_target="tpu_custom_call" | custom-call | flops 1 | bytes 1 | tf_op jit(solution)/shard_map/finish/pallas_call | solution.py:435
  (50 shorter events, 12.5 us)
Async XLA Ops:
  0.6 43.3 %collective-permute-start = (bf16[640,1280]{1,0:T(8,128)(2,1)}, bf16[640,1280]{1,0:T(8,128)(2,1)S(1)}, u32[]{:S(2)}, u32[]{:S(2)}) collective-permute-start(bf16[640,1280]{1,0:T(8,128)(2,1)} %w_mine.5), channel_id=1, source_target_pairs={{16,0},{0,16},{17,1},{1,17},{18,2},{2,18},{19,3},{3,19},{20,4},{4,... | collective-permute-start | bytes 4915208 | tf_op jit(solution)/shard_map/ppermute | solution.py:33
  4.2 19.7 %collective-permute-start.1 = (bf16[256,1280]{1,0:T(8,128)(2,1)}, bf16[256,1280]{1,0:T(8,128)(2,1)}, u32[]{:S(2)}, u32[]{:S(2)}) collective-permute-start(bf16[256,1280]{1,0:T(8,128)(2,1)} %split_rows.1._), channel_id=1, source_target_pairs={{12,0},{13,1},{14,2},{15,3},{0,4},{1,5},{2,6},{3,7},{4,8},{5,9},{6... | collective-permute-start | bytes 1966088 | tf_op jit(solution)/shard_map/ppermute | solution.py:42
  5.9 7.8 %copy-start.2 = (bf16[1280,640]{1,0:T(8,128)(2,1)S(1)}, bf16[1280,640]{1,0:T(8,128)(2,1)}, u32[]{:S(2)}) copy-start(bf16[1280,640]{1,0:T(8,128)(2,1)} %refs_2_.1) | copy-start | bytes 4915204
  10.0 28.2 %collective-permute-start.2 = (bf16[2,256,256]{2,1,0:T(8,128)(2,1)}, bf16[2,256,256]{2,1,0:T(8,128)(2,1)S(1)}, u32[]{:S(2)}, u32[]{:S(2)}) collective-permute-start(bf16[2,256,256]{2,1,0:T(8,128)(2,1)} %get-tuple-element.46), channel_id=1, source_target_pairs={{9,0},{10,1},{11,2},{12,3},{13,4},{14,5},{15,6},{0,7},{1,8},{2,9},... | collective-permute-start | bytes 786440 | tf_op jit(solution)/shard_map/ppermute | solution.py:42
  11.4 32.5 %collective-permute-start.3 = (bf16[2,256,256]{2,1,0:T(8,128)(2,1)}, bf16[2,256,256]{2,1,0:T(8,128)(2,1)S(1)}, u32[]{:S(2)}, u32[]{:S(2)}) collective-permute-start(bf16[2,256,256]{2,1,0:T(8,128)(2,1)} %get-tuple-element.47), channel_id=1, source_target_pairs={{5,0},{6,1},{7,2},{8,3},{9,4},{10,5},{11,6},{12,7},{13,8},{14,9},{... | collective-permute-start | bytes 786440 | tf_op jit(solution)/shard_map/ppermute | solution.py:42
  13.6 30.3 %collective-permute-start.4 = (bf16[2,256,256]{2,1,0:T(8,128)(2,1)}, bf16[2,256,256]{2,1,0:T(8,128)(2,1)S(1)}, u32[]{:S(2)}, u32[]{:S(2)}) collective-permute-start(bf16[2,256,256]{2,1,0:T(8,128)(2,1)} %get-tuple-element.48), channel_id=1, source_target_pairs={{13,0},{14,1},{15,2},{0,3},{1,4},{2,5},{3,6},{4,7},{5,8},{6,9},{7,... | collective-permute-start | bytes 786440 | tf_op jit(solution)/shard_map/ppermute | solution.py:42
  16.5 28.3 %copy-start.12 = (bf16[2,256,384]{2,1,0:T(8,128)(2,1)S(1)}, bf16[2,256,384]{2,1,0:T(8,128)(2,1)}, u32[]{:S(2)}) copy-start(bf16[2,256,384]{2,1,0:T(8,128)(2,1)} %get-tuple-element.64) | copy-start | bytes 1179652
  16.5 28.3 %copy-start.11 = (bf16[2,256,384]{2,1,0:T(8,128)(2,1)S(1)}, bf16[2,256,384]{2,1,0:T(8,128)(2,1)}, u32[]{:S(2)}) copy-start(bf16[2,256,384]{2,1,0:T(8,128)(2,1)} %get-tuple-element.66) | copy-start | bytes 1179652
  16.5 31.8 %copy-start.10 = (bf16[2,256,384]{2,1,0:T(8,128)(2,1)S(1)}, bf16[2,256,384]{2,1,0:T(8,128)(2,1)}, u32[]{:S(2)}) copy-start(bf16[2,256,384]{2,1,0:T(8,128)(2,1)} %get-tuple-element.81) | copy-start | bytes 1179652
  16.5 33.4 %copy-start.9 = (bf16[2,256,384]{2,1,0:T(8,128)(2,1)S(1)}, bf16[2,256,384]{2,1,0:T(8,128)(2,1)}, u32[]{:S(2)}) copy-start(bf16[2,256,384]{2,1,0:T(8,128)(2,1)} %get-tuple-element.83) | copy-start | bytes 1179652
  23.5 38.5 %copy-start.7 = (f32[1280]{0:T(1024)S(1)}, f32[1280]{0:T(1024)}, u32[]{:S(2)}) copy-start(f32[1280]{0:T(1024)} %param.19) | copy-start | bytes 15364
  23.5 38.5 %copy-start.4 = (bf16[1280,640]{1,0:T(8,128)(2,1)S(1)}, bf16[1280,640]{1,0:T(8,128)(2,1)}, u32[]{:S(2)}) copy-start(bf16[1280,640]{1,0:T(8,128)(2,1)} %refs_3_.1) | copy-start | bytes 4915204
  23.5 38.5 %copy-start.6 = (s32[32]{0:T(128)S(1)}, s32[32]{0:T(128)}, u32[]{:S(2)}) copy-start(s32[32]{0:T(128)} %placement.1) | copy-start | bytes 388
  23.9 20.1 %collective-permute-start.5 = (bf16[2,256,256]{2,1,0:T(8,128)(2,1)S(1)}, bf16[2,256,256]{2,1,0:T(8,128)(2,1)S(1)}, u32[]{:S(2)}, u32[]{:S(2)}) collective-permute-start(bf16[2,256,256]{2,1,0:T(8,128)(2,1)S(1)} %copy-done.13), channel_id=1, source_target_pairs={{1,0},{2,1},{3,2},{4,3},{5,4},{6,5},{7,6},{8,7},{9,8},{10,9},{11,1... | collective-permute-start | bytes 786440 | tf_op jit(solution)/shard_map/ppermute | solution.py:42
  44.0 17.8 %collective-permute-start.6 = (bf16[256,1280]{1,0:T(8,128)(2,1)}, bf16[256,1280]{1,0:T(8,128)(2,1)S(1)}, u32[]{:S(2)}, u32[]{:S(2)}) collective-permute-start(bf16[256,1280]{1,0:T(8,128)(2,1)} %collective-permute-done.1.refs_0_), channel_id=1, source_target_pairs={{16,0},{0,16},{17,1},{1,17},{18,2},{2,18},{19,3},{3,19},{20,4},{4,... | collective-permute-start | bytes 1966088 | tf_op jit(solution)/shard_map/ppermute | solution.py:33
  44.8 26.3 %collective-permute-start.8 = (bf16[2,256,384]{2,1,0:T(8,128)(2,1)S(1)}, bf16[2,256,384]{2,1,0:T(8,128)(2,1)S(1)}, u32[]{:S(2)}, u32[]{:S(2)}) collective-permute-start(bf16[2,256,384]{2,1,0:T(8,128)(2,1)S(1)} %copy-done.12), channel_id=1, source_target_pairs={{9,0},{10,1},{11,2},{12,3},{13,4},{14,5},{15,6},{0,7},{1,8},{2,9},... | collective-permute-start | bytes 1179656 | tf_op jit(solution)/shard_map/ppermute | solution.py:42
  44.8 34.3 %collective-permute-start.9 = (bf16[2,256,384]{2,1,0:T(8,128)(2,1)S(1)}, bf16[2,256,384]{2,1,0:T(8,128)(2,1)S(1)}, u32[]{:S(2)}, u32[]{:S(2)}) collective-permute-start(bf16[2,256,384]{2,1,0:T(8,128)(2,1)S(1)} %copy-done.11), channel_id=1, source_target_pairs={{5,0},{6,1},{7,2},{8,3},{9,4},{10,5},{11,6},{12,7},{13,8},{14,9},{... | collective-permute-start | bytes 1179656 | tf_op jit(solution)/shard_map/ppermute | solution.py:42
  48.4 34.6 %collective-permute-start.10 = (bf16[2,256,384]{2,1,0:T(8,128)(2,1)S(1)}, bf16[2,256,384]{2,1,0:T(8,128)(2,1)S(1)}, u32[]{:S(2)}, u32[]{:S(2)}) collective-permute-start(bf16[2,256,384]{2,1,0:T(8,128)(2,1)S(1)} %copy-done.10), channel_id=1, source_target_pairs={{13,0},{14,1},{15,2},{0,3},{1,4},{2,5},{3,6},{4,7},{5,8},{6,9},{7,... | collective-permute-start | bytes 1179656 | tf_op jit(solution)/shard_map/ppermute | solution.py:42
  49.9 33.1 %collective-permute-start.11 = (bf16[2,256,384]{2,1,0:T(8,128)(2,1)S(1)}, bf16[2,256,384]{2,1,0:T(8,128)(2,1)S(1)}, u32[]{:S(2)}, u32[]{:S(2)}) collective-permute-start(bf16[2,256,384]{2,1,0:T(8,128)(2,1)S(1)} %copy-done.9), channel_id=1, source_target_pairs={{1,0},{2,1},{3,2},{4,3},{5,4},{6,5},{7,6},{8,7},{9,8},{10,9},{11,1... | collective-permute-start | bytes 1179656 | tf_op jit(solution)/shard_map/ppermute | solution.py:42
  61.7 8.2 %collective-permute-start.7 = (bf16[512,256]{1,0:T(8,128)(2,1)S(1)}, bf16[512,256]{1,0:T(8,128)(2,1)S(1)}, u32[]{:S(2)}, u32[]{:S(2)}) collective-permute-start(bf16[512,256]{1,0:T(8,128)(2,1)S(1)} %attend.4.refs_0_), channel_id=1, source_target_pairs={{16,0},{0,16},{17,1},{1,17},{18,2},{2,18},{19,3},{3,19},{20,4},{4,... | collective-permute-start | bytes 786440 | tf_op jit(solution)/shard_map/ppermute | solution.py:33
  62.0 7.9 %copy-start = (bf16[640,1280]{1,0:T(8,128)(2,1)S(1)}, bf16[640,1280]{1,0:T(8,128)(2,1)}, u32[]{:S(2)}) copy-start(bf16[640,1280]{1,0:T(8,128)(2,1)} %w_mine.5) | copy-start | bytes 4915204
  83.9 6.4 %collective-permute-start.12 = (bf16[512,128]{1,0:T(8,128)(2,1)S(1)}, bf16[512,128]{1,0:T(8,128)(2,1)S(1)}, u32[]{:S(2)}, u32[]{:S(2)}) collective-permute-start(bf16[512,128]{1,0:T(8,128)(2,1)S(1)} %attend_rest.3.refs_0_), channel_id=1, source_target_pairs={{16,0},{0,16},{17,1},{1,17},{18,2},{2,18},{19,3},{3,19},{20,4},{4,... | collective-permute-start | bytes 393224 | tf_op jit(solution)/shard_map/ppermute | solution.py:33
  86.8 6.5 %collective-permute-start.13 = (bf16[512,128]{1,0:T(8,128)(2,1)S(1)}, bf16[512,128]{1,0:T(8,128)(2,1)S(1)}, u32[]{:S(2)}, u32[]{:S(2)}) collective-permute-start(bf16[512,128]{1,0:T(8,128)(2,1)S(1)} %attend_rest.4.refs_1_), channel_id=1, source_target_pairs={{16,0},{0,16},{17,1},{1,17},{18,2},{2,18},{19,3},{3,19},{20,4},{4,... | collective-permute-start | bytes 393224 | tf_op jit(solution)/shard_map/ppermute | solution.py:33
  88.1 7.6 %collective-permute-start.14 = (bf16[512,128]{1,0:T(8,128)(2,1)S(1)}, bf16[512,128]{1,0:T(8,128)(2,1)S(1)}, u32[]{:S(2)}, u32[]{:S(2)}) collective-permute-start(bf16[512,128]{1,0:T(8,128)(2,1)S(1)} %attend_rest.5.refs_0_), channel_id=1, source_target_pairs={{16,0},{0,16},{17,1},{1,17},{18,2},{2,18},{19,3},{3,19},{20,4},{4,... | collective-permute-start | bytes 393224 | tf_op jit(solution)/shard_map/ppermute | solution.py:33
  (5 other events, 25.8 us)

commit v7 on v6

--- a/solution.py
+++ b/solution.py
@@ -17,7 +17,7 @@
 PARTS = 4
 SLOT_ORDER = (2, 1, 3)
 PAGE_ORDER = (2, 1, 3, 0)
-EARLY = 2
+EARLY = 1
 VMEM_LIMIT = 16 * 1024 * 1024
 FIRST_LIMIT = 58 * 1024 * 1024
 

time: 98.5 us -> 95.6 us (0.971)
  the two profiles are of different devices: /device:TPU:8 before, /device:TPU:16 now
where the time goes in v7:
time: 95.6 us; the launch traced here: 95.3 us
  waiting for transfers between devices  35.7 us (37%)
  Pallas kernels  33.6 us (35%)
  starting transfers between devices  20.8 us (22%)
  local copies, waits for them, and re-layouts  2.92 us (3%)
  between operations  2.31 us (2%)
    ppermute x9, waiting for transfers between devices, over_blk(): return lax.ppermute(block, ('kv', 'blk'), route)  23.9 us
    ppermute x6, waiting for transfers between devices, from_behind(): return lax.ppermute(block, axis, route)  11.8 us
    ppermute x6, starting transfers between devices, from_behind(): return lax.ppermute(block, axis, route)  11.1 us
    ppermute x9, starting transfers between devices, over_blk(): return lax.ppermute(block, ('kv', 'blk'), route)  9.66 us
    pallas_call x1, Pallas kernels, project(): pl.pallas_call(functools.partial(project_kernel, slices), out_shape=outs,...  7 us
    pallas_call x4, Pallas kernels, attend(): pl.pallas_call(functools.partial(attend_kernel, inner, slots), in_specs=[...  6.44 us
    pallas_call x1, Pallas kernels, relay_project(): pl.pallas_call(functools.partial(relay_kernel, group_slices(width), block...  5.11 us
    pallas_call x1, Pallas kernels, pack(): pl.pallas_call(functools.partial(pack_kernel, slices, devices, offsets),...  4.11 us
  transfers between devices with their start and end apart: 15, of which 10 were waited for; matrix products, arithmetic and copies ran while one was open for 0% of the time, Pallas kernels for 32%

profile of v7, /device:TPU:16, one launch (start us, length us, event | category | flops | bytes accessed | tf_op | source)
XLA Modules:
  0.0 95.3 jit_solution(8680441429062327362)
XLA Ops:
  0.6 1.6 %collective-permute-start = (bf16[640,1280]{1,0:T(8,128)(2,1)}, bf16[640,1280]{1,0:T(8,128)(2,1)S(1)}, u32[]{:S(2)}, u32[]{:S(2)}) collective-permute-start(bf16[640,1280]{1,0:T(8,128)(2,1)} %w_mine.5), channel_id=1, source_target_pairs={{16,0},{0,16},{17,1},{1,17},{18,2},{2,18},{19,3},{3,19},{20,4},{4,... | collective-permute-start | bytes 4915208 | tf_op jit(solution)/shard_map/ppermute | solution.py:33
  2.2 2.0 %split_rows.1._ = bf16[256,1280]{1,0:T(8,128)(2,1)} custom-call(s32[1]{0:T(128)} %bitcast.kv_ref, bf16[512,1280]{1,0:T(8,128)(2,1)} %hidden.5), custom_call_target="tpu_custom_call" | custom-call | flops 1 | bytes 1 | tf_op jit(solution)/shard_map/split_rows/pallas_call | solution.py:91
  4.2 1.6 %collective-permute-start.1 = (bf16[256,1280]{1,0:T(8,128)(2,1)}, bf16[256,1280]{1,0:T(8,128)(2,1)}, u32[]{:S(2)}, u32[]{:S(2)}) collective-permute-start(bf16[256,1280]{1,0:T(8,128)(2,1)} %split_rows.1._), channel_id=1, source_target_pairs={{12,0},{13,1},{14,2},{15,3},{0,4},{1,5},{2,6},{3,7},{4,8},{5,9},{6... | collective-permute-start | bytes 1966088 | tf_op jit(solution)/shard_map/ppermute | solution.py:42
  5.9 4.1 %pack.1 = (bf16[2,256,256]{2,1,0:T(8,128)(2,1)}, bf16[2,256,256]{2,1,0:T(8,128)(2,1)}, bf16[2,256,256]{2,1,0:T(8,128)(2,1)}, bf16[2,256,256]{2,1,0:T(8,128)(2,1)...) custom-call(s32[1]{0:T(128)} %bitcast.1.here_ref, ...), custom_call_target="tpu_custom_call" | custom-call | flops 1 | bytes 1 | tf_op jit(solution)/shard_map/pack/pallas_call | solution.py:130
  10.2 3.5 %collective-permute-start.3 = (bf16[2,256,256]{2,1,0:T(8,128)(2,1)}, bf16[2,256,256]{2,1,0:T(8,128)(2,1)S(1)}, u32[]{:S(2)}, u32[]{:S(2)}) collective-permute-start(bf16[2,256,256]{2,1,0:T(8,128)(2,1)} %get-tuple-element.47), channel_id=1, source_target_pairs={{5,0},{6,1},{7,2},{8,3},{9,4},{10,5},{11,6},{12,7},{13,8},{14,9},{... | collective-permute-start | bytes 786440 | tf_op jit(solution)/shard_map/ppermute | solution.py:42
  15.1 1.4 %copy-done.5 = bf16[1280,640]{1,0:T(8,128)(2,1)S(1)} copy-done((bf16[1280,640]{1,0:T(8,128)(2,1)S(1)}, bf16[1280,640]{1,0:T(8,128)(2,1)}, u32[]{:S(2)}) %copy-start.5) | copy-done | bytes 1638424
  16.5 7.0 %project.1 = (bf16[512,256]{1,0:T(8,128)(2,1)S(1)}, bf16[512,256]{1,0:T(8,128)(2,1)S(1)}, bf16[512,256]{1,0:T(8,128)(2,1)S(1)}, bf16[512,128]{1,0:T(8,128)(2,1)S...) custom-call(bf16[512,1280]{1,0:T(8,128)(2,1)S(1)} %copy-done.1, ...), custom_call_target="tpu_custom_call" | custom-call | flops 1 | bytes 1 | tf_op jit(solution)/shard_map/project/pallas_call | solution.py:195
  23.6 1.7 %collective-permute-done.1.refs_0_ = bf16[256,1280]{1,0:T(8,128)(2,1)} collective-permute-done((bf16[256,1280]{1,0:T(8,128)(2,1)}, bf16[256,1280]{1,0:T(8,128)(2,1)}, u32[]{:S(2)}, u32[]{:S(2)}) %collective-permute-start.1) | collective-permute-done | bytes 655392 | tf_op jit(solution)/shard_map/ppermute | solution.py:42
  25.3 5.4 %collective-permute-done.2.refs_0_ = bf16[2,256,256]{2,1,0:T(8,128)(2,1)S(1)} collective-permute-done((bf16[2,256,256]{2,1,0:T(8,128)(2,1)}, bf16[2,256,256]{2,1,0:T(8,128)(2,1)S(1)}, u32[]{:S(2)}, u32[]{:S(2)}) %collective-permute-start.2) | collective-permute-done | bytes 262176 | tf_op jit(solution)/shard_map/ppermute | solution.py:42
  30.7 5.9 %collective-permute-done.3.refs_1_ = bf16[2,256,256]{2,1,0:T(8,128)(2,1)S(1)} collective-permute-done((bf16[2,256,256]{2,1,0:T(8,128)(2,1)}, bf16[2,256,256]{2,1,0:T(8,128)(2,1)S(1)}, u32[]{:S(2)}, u32[]{:S(2)}) %collective-permute-start.3) | collective-permute-done | bytes 262176 | tf_op jit(solution)/shard_map/ppermute | solution.py:42
  36.6 5.1 %collective-permute-done.4.refs_2_ = bf16[2,256,256]{2,1,0:T(8,128)(2,1)S(1)} collective-permute-done((bf16[2,256,256]{2,1,0:T(8,128)(2,1)}, bf16[2,256,256]{2,1,0:T(8,128)(2,1)S(1)}, u32[]{:S(2)}, u32[]{:S(2)}) %collective-permute-start.4) | collective-permute-done | bytes 262176 | tf_op jit(solution)/shard_map/ppermute | solution.py:42
  42.0 3.6 %collective-permute-start.6 = (bf16[256,1280]{1,0:T(8,128)(2,1)}, bf16[256,1280]{1,0:T(8,128)(2,1)S(1)}, u32[]{:S(2)}, u32[]{:S(2)}) collective-permute-start(bf16[256,1280]{1,0:T(8,128)(2,1)} %collective-permute-done.1.refs_0_), channel_id=1, source_target_pairs={{16,0},{0,16},{17,1},{1,17},{18,2},{2,18},{19,3},{3,19},{20,4},{4,... | collective-permute-start | bytes 1966088 | tf_op jit(solution)/shard_map/ppermute | solution.py:33
  45.6 1.5 %collective-permute-start.8 = (bf16[2,256,384]{2,1,0:T(8,128)(2,1)S(1)}, bf16[2,256,384]{2,1,0:T(8,128)(2,1)S(1)}, u32[]{:S(2)}, u32[]{:S(2)}) collective-permute-start(bf16[2,256,384]{2,1,0:T(8,128)(2,1)S(1)} %copy-done.12), channel_id=1, source_target_pairs={{9,0},{10,1},{11,2},{12,3},{13,4},{14,5},{15,6},{0,7},{1,8},{2,9},... | collective-permute-start | bytes 1179656 | tf_op jit(solution)/shard_map/ppermute | solution.py:42
  47.1 2.1 %collective-permute-start.9 = (bf16[2,256,384]{2,1,0:T(8,128)(2,1)S(1)}, bf16[2,256,384]{2,1,0:T(8,128)(2,1)S(1)}, u32[]{:S(2)}, u32[]{:S(2)}) collective-permute-start(bf16[2,256,384]{2,1,0:T(8,128)(2,1)S(1)} %copy-done.11), channel_id=1, source_target_pairs={{5,0},{6,1},{7,2},{8,3},{9,4},{10,5},{11,6},{12,7},{13,8},{14,9},{... | collective-permute-start | bytes 1179656 | tf_op jit(solution)/shard_map/ppermute | solution.py:42
  51.3 3.4 %attend.4.refs_0_ = bf16[512,256]{1,0:T(8,128)(2,1)S(1)} custom-call(s32[1]{0:T(128)S(6)} %copy.16.live_ref, s32[1]{0:T(128)S(6)} %copy.17.depth_ref, bf16[512,256]{1,0:T(8,128)(2,1)S(1)} %get-tuple-element.50.q_ref, bf16[512,256]{1,0:T(8,128)(2,1)S(1)} %get-tuple-element.55.k_ref, bf16[512,256]{1,0:T(8,128)(2,1)S(1)} %get-tuple-element.56.v_ref, ...), custom_call_target="tpu_custom_call" | custom-call | flops 1 | bytes 1 | tf_op jit(solution)/shard_map/attend/pallas_call | solution.py:311
  54.7 6.7 %collective-permute-done.6.refs_1_ = bf16[256,1280]{1,0:T(8,128)(2,1)S(1)} collective-permute-done((bf16[256,1280]{1,0:T(8,128)(2,1)}, bf16[256,1280]{1,0:T(8,128)(2,1)S(1)}, u32[]{:S(2)}, u32[]{:S(2)}) %collective-permute-start.6) | collective-permute-done | bytes 655392 | tf_op jit(solution)/shard_map/ppermute | solution.py:33
  61.3 1.8 %collective-permute-start.7 = (bf16[512,256]{1,0:T(8,128)(2,1)S(1)}, bf16[512,256]{1,0:T(8,128)(2,1)S(1)}, u32[]{:S(2)}, u32[]{:S(2)}) collective-permute-start(bf16[512,256]{1,0:T(8,128)(2,1)S(1)} %attend.4.refs_0_), channel_id=1, source_target_pairs={{16,0},{0,16},{17,1},{1,17},{18,2},{2,18},{19,3},{3,19},{20,4},{4,... | collective-permute-start | bytes 786440 | tf_op jit(solution)/shard_map/ppermute | solution.py:33
  63.2 5.1 %relay_project.1 = (bf16[2,256,640]{2,1,0:T(8,128)(2,1)}, bf16[2,256,640]{2,1,0:T(8,128)(2,1)}) custom-call(s32[1]{0:T(128)} %bitcast.kv_ref, s32[1]{0:T(128)} %bitcast.1.here_ref, s32[32]{0:T(128)S(1)} %copy-done.6, bf16[256,1280]{1,0:T(8,128)(2,1)} %collective-permute-done.1.refs_0_, bf16[256,1280]{1,0:T(8,128)(2,1)S(1)} %collective-permute-done.6.refs_1_, ...), custom_call_target="tpu_custom_call" | custom-call | flops 1 | bytes 1 | tf_op jit(solution)/shard_map/relay_project/pallas_call | solution.py:228
  74.1 5.4 %collective-permute-done.10.refs_1_ = bf16[2,256,384]{2,1,0:T(8,128)(2,1)S(1)} collective-permute-done((bf16[2,256,384]{2,1,0:T(8,128)(2,1)S(1)}, bf16[2,256,384]{2,1,0:T(8,128)(2,1)S(1)}, u32[]{:S(2)}, u32[]{:S(2)}) %collective-permute-start.10) | collective-permute-done | bytes 393248 | tf_op jit(solution)/shard_map/ppermute | solution.py:42
  80.7 2.0 %collective-permute-start.12 = (bf16[512,128]{1,0:T(8,128)(2,1)S(1)}, bf16[512,128]{1,0:T(8,128)(2,1)S(1)}, u32[]{:S(2)}, u32[]{:S(2)}) collective-permute-start(bf16[512,128]{1,0:T(8,128)(2,1)S(1)} %attend_rest.3.refs_0_), channel_id=1, source_target_pairs={{16,0},{0,16},{17,1},{1,17},{18,2},{2,18},{19,3},{3,19},{20,4},{4,... | collective-permute-start | bytes 393224 | tf_op jit(solution)/shard_map/ppermute | solution.py:33
  85.4 2.0 %collective-permute-start.14 = (bf16[512,128]{1,0:T(8,128)(2,1)S(1)}, bf16[512,128]{1,0:T(8,128)(2,1)S(1)}, u32[]{:S(2)}, u32[]{:S(2)}) collective-permute-start(bf16[512,128]{1,0:T(8,128)(2,1)S(1)} %attend_rest.5.refs_0_), channel_id=1, source_target_pairs={{16,0},{0,16},{17,1},{1,17},{18,2},{2,18},{19,3},{3,19},{20,4},{4,... | collective-permute-start | bytes 393224 | tf_op jit(solution)/shard_map/ppermute | solution.py:33
  87.4 3.2 %collective-permute-done.13.refs_3_ = bf16[512,128]{1,0:T(8,128)(2,1)S(1)} collective-permute-done((bf16[512,128]{1,0:T(8,128)(2,1)S(1)}, bf16[512,128]{1,0:T(8,128)(2,1)S(1)}, u32[]{:S(2)}, u32[]{:S(2)}) %collective-permute-start.13) | collective-permute-done | bytes 131104 | tf_op jit(solution)/shard_map/ppermute | solution.py:33
  90.6 1.6 %add_branch.1.begun = f32[512,1280]{1,0:T(8,128)S(1)} custom-call(f32[512,1280]{1,0:T(8,128)S(1)} %get-tuple-element.58.begun, bf16[640,1280]{1,0:T(8,128)(2,1)S(1)} %copy-done, bf16[640,1280]{1,0:T(8,128)(2,1)S(1)} %collective-permute-done.w_theirs, bf16[512,128]{1,0:T(8,128)(2,1)S(1)} %attend_rest.3.refs_0_, bf16[512,128]{1,0:T(8,128)(2,1)S(1)} %attend_rest.4.refs_1_, ...), custom_call_target="tpu_custom_call" | custom-call | flops 1 | bytes 1 | tf_op jit(solution)/shard_map/add_branch/pallas_call | solution.py:400
  92.8 2.3 %finish.1 = bf16[512,1280]{1,0:T(8,128)(2,1)} custom-call(f32[512,1280]{1,0:T(8,128)S(1)} %get-tuple-element.57.base, bf16[640,1280]{1,0:T(8,128)(2,1)S(1)} %copy-done, bf16[640,1280]{1,0:T(8,128)(2,1)S(1)} %collective-permute-done.w_theirs, f32[1,1280]{1,0:T(1,128)S(1)} %reshape.18.rate, f32[512,1280]{1,0:T(8,128)S(1)} %add_branch.1.begun, ...), custom_call_target="tpu_custom_call" | custom-call | flops 1 | bytes 1 | tf_op jit(solution)/shard_map/finish/pallas_call | solution.py:435
  (50 shorter events, 13.0 us)
Async XLA Ops:
  0.6 41.4 %collective-permute-start = (bf16[640,1280]{1,0:T(8,128)(2,1)}, bf16[640,1280]{1,0:T(8,128)(2,1)S(1)}, u32[]{:S(2)}, u32[]{:S(2)}) collective-permute-start(bf16[640,1280]{1,0:T(8,128)(2,1)} %w_mine.5), channel_id=1, source_target_pairs={{16,0},{0,16},{17,1},{1,17},{18,2},{2,18},{19,3},{3,19},{20,4},{4,... | collective-permute-start | bytes 4915208 | tf_op jit(solution)/shard_map/ppermute | solution.py:33
  4.2 21.1 %collective-permute-start.1 = (bf16[256,1280]{1,0:T(8,128)(2,1)}, bf16[256,1280]{1,0:T(8,128)(2,1)}, u32[]{:S(2)}, u32[]{:S(2)}) collective-permute-start(bf16[256,1280]{1,0:T(8,128)(2,1)} %split_rows.1._), channel_id=1, source_target_pairs={{12,0},{13,1},{14,2},{15,3},{0,4},{1,5},{2,6},{3,7},{4,8},{5,9},{6... | collective-permute-start | bytes 1966088 | tf_op jit(solution)/shard_map/ppermute | solution.py:42
  5.9 7.8 %copy-start.2 = (bf16[1280,640]{1,0:T(8,128)(2,1)S(1)}, bf16[1280,640]{1,0:T(8,128)(2,1)}, u32[]{:S(2)}) copy-start(bf16[1280,640]{1,0:T(8,128)(2,1)} %refs_2_.1) | copy-start | bytes 4915204
  10.0 20.7 %collective-permute-start.2 = (bf16[2,256,256]{2,1,0:T(8,128)(2,1)}, bf16[2,256,256]{2,1,0:T(8,128)(2,1)S(1)}, u32[]{:S(2)}, u32[]{:S(2)}) collective-permute-start(bf16[2,256,256]{2,1,0:T(8,128)(2,1)} %get-tuple-element.46), channel_id=1, source_target_pairs={{9,0},{10,1},{11,2},{12,3},{13,4},{14,5},{15,6},{0,7},{1,8},{2,9},... | collective-permute-start | bytes 786440 | tf_op jit(solution)/shard_map/ppermute | solution.py:42
  10.2 26.5 %collective-permute-start.3 = (bf16[2,256,256]{2,1,0:T(8,128)(2,1)}, bf16[2,256,256]{2,1,0:T(8,128)(2,1)S(1)}, u32[]{:S(2)}, u32[]{:S(2)}) collective-permute-start(bf16[2,256,256]{2,1,0:T(8,128)(2,1)} %get-tuple-element.47), channel_id=1, source_target_pairs={{5,0},{6,1},{7,2},{8,3},{9,4},{10,5},{11,6},{12,7},{13,8},{14,9},{... | collective-permute-start | bytes 786440 | tf_op jit(solution)/shard_map/ppermute | solution.py:42
  13.6 28.1 %collective-permute-start.4 = (bf16[2,256,256]{2,1,0:T(8,128)(2,1)}, bf16[2,256,256]{2,1,0:T(8,128)(2,1)S(1)}, u32[]{:S(2)}, u32[]{:S(2)}) collective-permute-start(bf16[2,256,256]{2,1,0:T(8,128)(2,1)} %get-tuple-element.48), channel_id=1, source_target_pairs={{13,0},{14,1},{15,2},{0,3},{1,4},{2,5},{3,6},{4,7},{5,8},{6,9},{7,... | collective-permute-start | bytes 786440 | tf_op jit(solution)/shard_map/ppermute | solution.py:42
  16.5 8.8 %copy-start.13 = (bf16[2,256,256]{2,1,0:T(8,128)(2,1)S(1)}, bf16[2,256,256]{2,1,0:T(8,128)(2,1)}, u32[]{:S(2)}) copy-start(bf16[2,256,256]{2,1,0:T(8,128)(2,1)} %get-tuple-element.51) | copy-start | bytes 786436
  16.5 29.1 %copy-start.12 = (bf16[2,256,384]{2,1,0:T(8,128)(2,1)S(1)}, bf16[2,256,384]{2,1,0:T(8,128)(2,1)}, u32[]{:S(2)}) copy-start(bf16[2,256,384]{2,1,0:T(8,128)(2,1)} %get-tuple-element.64) | copy-start | bytes 1179652
  16.5 30.6 %copy-start.11 = (bf16[2,256,384]{2,1,0:T(8,128)(2,1)S(1)}, bf16[2,256,384]{2,1,0:T(8,128)(2,1)}, u32[]{:S(2)}) copy-start(bf16[2,256,384]{2,1,0:T(8,128)(2,1)} %get-tuple-element.79) | copy-start | bytes 1179652
  16.5 32.7 %copy-start.10 = (bf16[2,256,384]{2,1,0:T(8,128)(2,1)S(1)}, bf16[2,256,384]{2,1,0:T(8,128)(2,1)}, u32[]{:S(2)}) copy-start(bf16[2,256,384]{2,1,0:T(8,128)(2,1)} %get-tuple-element.81) | copy-start | bytes 1179652
  16.5 32.7 %copy-start.9 = (bf16[2,256,384]{2,1,0:T(8,128)(2,1)S(1)}, bf16[2,256,384]{2,1,0:T(8,128)(2,1)}, u32[]{:S(2)}) copy-start(bf16[2,256,384]{2,1,0:T(8,128)(2,1)} %get-tuple-element.83) | copy-start | bytes 1179652
  23.5 39.6 %copy-start.7 = (f32[1280]{0:T(1024)S(1)}, f32[1280]{0:T(1024)}, u32[]{:S(2)}) copy-start(f32[1280]{0:T(1024)} %param.19) | copy-start | bytes 15364
  23.6 39.6 %copy-start.4 = (bf16[1280,640]{1,0:T(8,128)(2,1)S(1)}, bf16[1280,640]{1,0:T(8,128)(2,1)}, u32[]{:S(2)}) copy-start(bf16[1280,640]{1,0:T(8,128)(2,1)} %refs_3_.1) | copy-start | bytes 4915204
  23.6 39.6 %copy-start.6 = (s32[32]{0:T(128)S(1)}, s32[32]{0:T(128)}, u32[]{:S(2)}) copy-start(s32[32]{0:T(128)} %placement.1) | copy-start | bytes 388
  25.3 16.7 %collective-permute-start.5 = (bf16[2,256,256]{2,1,0:T(8,128)(2,1)S(1)}, bf16[2,256,256]{2,1,0:T(8,128)(2,1)S(1)}, u32[]{:S(2)}, u32[]{:S(2)}) collective-permute-start(bf16[2,256,256]{2,1,0:T(8,128)(2,1)S(1)} %copy-done.13), channel_id=1, source_target_pairs={{1,0},{2,1},{3,2},{4,3},{5,4},{6,5},{7,6},{8,7},{9,8},{10,9},{11,1... | collective-permute-start | bytes 786440 | tf_op jit(solution)/shard_map/ppermute | solution.py:42
  42.0 19.3 %collective-permute-start.6 = (bf16[256,1280]{1,0:T(8,128)(2,1)}, bf16[256,1280]{1,0:T(8,128)(2,1)S(1)}, u32[]{:S(2)}, u32[]{:S(2)}) collective-permute-start(bf16[256,1280]{1,0:T(8,128)(2,1)} %collective-permute-done.1.refs_0_), channel_id=1, source_target_pairs={{16,0},{0,16},{17,1},{1,17},{18,2},{2,18},{19,3},{3,19},{20,4},{4,... | collective-permute-start | bytes 1966088 | tf_op jit(solution)/shard_map/ppermute | solution.py:33
  45.6 25.3 %collective-permute-start.8 = (bf16[2,256,384]{2,1,0:T(8,128)(2,1)S(1)}, bf16[2,256,384]{2,1,0:T(8,128)(2,1)S(1)}, u32[]{:S(2)}, u32[]{:S(2)}) collective-permute-start(bf16[2,256,384]{2,1,0:T(8,128)(2,1)S(1)} %copy-done.12), channel_id=1, source_target_pairs={{9,0},{10,1},{11,2},{12,3},{13,4},{14,5},{15,6},{0,7},{1,8},{2,9},... | collective-permute-start | bytes 1179656 | tf_op jit(solution)/shard_map/ppermute | solution.py:42
  47.1 26.9 %collective-permute-start.9 = (bf16[2,256,384]{2,1,0:T(8,128)(2,1)S(1)}, bf16[2,256,384]{2,1,0:T(8,128)(2,1)S(1)}, u32[]{:S(2)}, u32[]{:S(2)}) collective-permute-start(bf16[2,256,384]{2,1,0:T(8,128)(2,1)S(1)} %copy-done.11), channel_id=1, source_target_pairs={{5,0},{6,1},{7,2},{8,3},{9,4},{10,5},{11,6},{12,7},{13,8},{14,9},{... | collective-permute-start | bytes 1179656 | tf_op jit(solution)/shard_map/ppermute | solution.py:42
  49.2 30.3 %collective-permute-start.10 = (bf16[2,256,384]{2,1,0:T(8,128)(2,1)S(1)}, bf16[2,256,384]{2,1,0:T(8,128)(2,1)S(1)}, u32[]{:S(2)}, u32[]{:S(2)}) collective-permute-start(bf16[2,256,384]{2,1,0:T(8,128)(2,1)S(1)} %copy-done.10), channel_id=1, source_target_pairs={{13,0},{14,1},{15,2},{0,3},{1,4},{2,5},{3,6},{4,7},{5,8},{6,9},{7,... | collective-permute-start | bytes 1179656 | tf_op jit(solution)/shard_map/ppermute | solution.py:42
  49.2 30.3 %collective-permute-start.11 = (bf16[2,256,384]{2,1,0:T(8,128)(2,1)S(1)}, bf16[2,256,384]{2,1,0:T(8,128)(2,1)S(1)}, u32[]{:S(2)}, u32[]{:S(2)}) collective-permute-start(bf16[2,256,384]{2,1,0:T(8,128)(2,1)S(1)} %copy-done.9), channel_id=1, source_target_pairs={{1,0},{2,1},{3,2},{4,3},{5,4},{6,5},{7,6},{8,7},{9,8},{10,9},{11,1... | collective-permute-start | bytes 1179656 | tf_op jit(solution)/shard_map/ppermute | solution.py:42
  61.3 8.4 %collective-permute-start.7 = (bf16[512,256]{1,0:T(8,128)(2,1)S(1)}, bf16[512,256]{1,0:T(8,128)(2,1)S(1)}, u32[]{:S(2)}, u32[]{:S(2)}) collective-permute-start(bf16[512,256]{1,0:T(8,128)(2,1)S(1)} %attend.4.refs_0_), channel_id=1, source_target_pairs={{16,0},{0,16},{17,1},{1,17},{18,2},{2,18},{19,3},{3,19},{20,4},{4,... | collective-permute-start | bytes 786440 | tf_op jit(solution)/shard_map/ppermute | solution.py:33
  80.7 6.7 %collective-permute-start.12 = (bf16[512,128]{1,0:T(8,128)(2,1)S(1)}, bf16[512,128]{1,0:T(8,128)(2,1)S(1)}, u32[]{:S(2)}, u32[]{:S(2)}) collective-permute-start(bf16[512,128]{1,0:T(8,128)(2,1)S(1)} %attend_rest.3.refs_0_), channel_id=1, source_target_pairs={{16,0},{0,16},{17,1},{1,17},{18,2},{2,18},{19,3},{3,19},{20,4},{4,... | collective-permute-start | bytes 393224 | tf_op jit(solution)/shard_map/ppermute | solution.py:33
  84.1 6.5 %collective-permute-start.13 = (bf16[512,128]{1,0:T(8,128)(2,1)S(1)}, bf16[512,128]{1,0:T(8,128)(2,1)S(1)}, u32[]{:S(2)}, u32[]{:S(2)}) collective-permute-start(bf16[512,128]{1,0:T(8,128)(2,1)S(1)} %attend_rest.4.refs_1_), channel_id=1, source_target_pairs={{16,0},{0,16},{17,1},{1,17},{18,2},{2,18},{19,3},{3,19},{20,4},{4,... | collective-permute-start | bytes 393224 | tf_op jit(solution)/shard_map/ppermute | solution.py:33
  85.4 7.3 %collective-permute-start.14 = (bf16[512,128]{1,0:T(8,128)(2,1)S(1)}, bf16[512,128]{1,0:T(8,128)(2,1)S(1)}, u32[]{:S(2)}, u32[]{:S(2)}) collective-permute-start(bf16[512,128]{1,0:T(8,128)(2,1)S(1)} %attend_rest.5.refs_0_), channel_id=1, source_target_pairs={{16,0},{0,16},{17,1},{1,17},{18,2},{2,18},{19,3},{3,19},{20,4},{4,... | collective-permute-start | bytes 393224 | tf_op jit(solution)/shard_map/ppermute | solution.py:33
  (5 other events, 24.9 us)

commit v8 on v7

--- a/solution.py
+++ b/solution.py
@@ -12,8 +12,8 @@
 PAGE = 256
 PMAX = 4
 LANES = 128
-GROUPS = (256, 384)
-UNITS = ((256,), (128, 128, 128))
+GROUPS = (384, 256)
+UNITS = ((128, 256), (128, 128))
 PARTS = 4
 SLOT_ORDER = (2, 1, 3)
 PAGE_ORDER = (2, 1, 3, 0)
@@ -493,10 +493,6 @@
     pages = [[got[slot] for slot in PAGE_ORDER] for got in (first, second)]
     w_theirs = from_behind(w_out, "kv", 1)
     relay_theirs = from_behind(after(relay_mine, w_theirs, *arrived, first[0]), "kv", 1)
-    new_keys, new_values = relay_project(
-        relay_mine, relay_theirs, w_key, w_value, gain, kv_index, here, placement, block_offsets
-    )
-
     mine, theirs, slices = [[], []], [[], []], [[], []]
     units = list(zip(unit_slices(), projected))
 
@@ -505,9 +501,14 @@
         theirs[g].append(from_behind(attended, "kv", 1))
         slices[g].append((start, size))
 
-    for (g, inner, start, size), (q, k, v) in units:
-        if g == 0:
-            swap(g, start, size, attend(req_len, prefix_len, q, k, v, pages[0], PAGE_ORDER, inner))
+    (g, inner, start, size), (q, k, v) = units[0]
+    swap(0, start, size, attend(req_len, prefix_len, q, k, v, pages[0], PAGE_ORDER, inner))
+    (g, inner, start, size), (q, k, v) = units[1]
+    q = after(q, theirs[0][0])
+    swap(1, start, size, attend(req_len, prefix_len, q, k, v, pages[0], PAGE_ORDER, inner))
+    new_keys, new_values = relay_project(
+        after(relay_mine, mine[1][0]), relay_theirs, w_key, w_value, gain, kv_index, here, placement, block_offsets
+    )
     base, begun = partial_branch(
         slices[0], hidden_in, rate, w_out, after(w_theirs, new_keys), mine[0], theirs[0]
     )

time: 95.6 us -> 102 us (1.067)
  waiting for transfers between devices: 35.7 us -> 44.9 us
  starting transfers between devices: 20.8 us -> 18.2 us
    ppermute x9, waiting for transfers between devices: 23.9 us -> 29.7 us  [over_blk(): return lax.ppermute(block, ('kv', 'blk'), route)]
    ppermute x6, waiting for transfers between devices: 11.8 us -> 15.2 us  [from_behind(): return lax.ppermute(block, axis, route)]
    ppermute x6, starting transfers between devices: 11.1 us -> 9.28 us  [from_behind(): return lax.ppermute(block, axis, route)]
    pallas_call x3 -> x2, Pallas kernels: 3.76 us -> 2.37 us  [attend_rest(): pl.pallas_call(functools.partial(attend_rest_kernel, inner, slots), in_sp...]
  transfers between devices with their start and end apart: 15 -> 15, of which waited for: 10 -> 8; matrix products, arithmetic and copies ran while one was open for 0% -> 0% of each run, Pallas kernels for 32% -> 31%
where the time goes in v8:
time: 102 us
  waiting for transfers between devices  44.9 us (44%)
  Pallas kernels  33.4 us (33%)
  starting transfers between devices  18.2 us (18%)
  local copies, waits for them, and re-layouts  2.92 us (3%)
  between operations  2.34 us (2%)
    ppermute x9, waiting for transfers between devices, over_blk(): return lax.ppermute(block, ('kv', 'blk'), route)  29.7 us
    ppermute x6, waiting for transfers between devices, from_behind(): return lax.ppermute(block, axis, route)  15.2 us
    ppermute x6, starting transfers between devices, from_behind(): return lax.ppermute(block, axis, route)  9.28 us
    ppermute x9, starting transfers between devices, over_blk(): return lax.ppermute(block, ('kv', 'blk'), route)  8.93 us
    pallas_call x4, Pallas kernels, attend(): pl.pallas_call(functools.partial(attend_kernel, inner, slots), in_specs=[...  7.31 us
    pallas_call x1, Pallas kernels, project(): pl.pallas_call(functools.partial(project_kernel, slices), out_shape=outs,...  7 us
    pallas_call x1, Pallas kernels, relay_project(): pl.pallas_call(functools.partial(relay_kernel, group_slices(width), block...  5.51 us
    pallas_call x1, Pallas kernels, pack(): pl.pallas_call(functools.partial(pack_kernel, slices, devices, offsets),...  4.1 us
  transfers between devices with their start and end apart: 15, of which 8 were waited for; matrix products, arithmetic and copies ran while one was open for 0% of the time, Pallas kernels for 31%

profile of v8, /device:TPU:16, one launch (start us, length us, event | category | flops | bytes accessed | tf_op | source)
XLA Modules:
  0.0 101.7 jit_solution(10917390422249349860)
XLA Ops:
  0.6 1.6 %collective-permute-start = (bf16[640,1280]{1,0:T(8,128)(2,1)}, bf16[640,1280]{1,0:T(8,128)(2,1)S(1)}, u32[]{:S(2)}, u32[]{:S(2)}) collective-permute-start(bf16[640,1280]{1,0:T(8,128)(2,1)} %w_mine.5), channel_id=1, source_target_pairs={{16,0},{0,16},{17,1},{1,17},{18,2},{2,18},{19,3},{3,19},{20,4},{4,... | collective-permute-start | bytes 4915208 | tf_op jit(solution)/shard_map/ppermute | solution.py:33
  2.2 2.0 %split_rows.1._ = bf16[256,1280]{1,0:T(8,128)(2,1)} custom-call(s32[1]{0:T(128)} %bitcast.kv_ref, bf16[512,1280]{1,0:T(8,128)(2,1)} %hidden.5), custom_call_target="tpu_custom_call" | custom-call | flops 1 | bytes 1 | tf_op jit(solution)/shard_map/split_rows/pallas_call | solution.py:91
  4.2 1.6 %collective-permute-start.1 = (bf16[256,1280]{1,0:T(8,128)(2,1)}, bf16[256,1280]{1,0:T(8,128)(2,1)}, u32[]{:S(2)}, u32[]{:S(2)}) collective-permute-start(bf16[256,1280]{1,0:T(8,128)(2,1)} %split_rows.1._), channel_id=1, source_target_pairs={{12,0},{13,1},{14,2},{15,3},{0,4},{1,5},{2,6},{3,7},{4,8},{5,9},{6... | collective-permute-start | bytes 1966088 | tf_op jit(solution)/shard_map/ppermute | solution.py:42
  5.9 4.1 %pack.1 = (bf16[2,256,384]{2,1,0:T(8,128)(2,1)}, bf16[2,256,384]{2,1,0:T(8,128)(2,1)}, bf16[2,256,384]{2,1,0:T(8,128)(2,1)}, bf16[2,256,384]{2,1,0:T(8,128)(2,1)...) custom-call(s32[1]{0:T(128)} %bitcast.1.here_ref, ...), custom_call_target="tpu_custom_call" | custom-call | flops 1 | bytes 1 | tf_op jit(solution)/shard_map/pack/pallas_call | solution.py:130
  10.1 3.5 %collective-permute-start.3 = (bf16[2,256,384]{2,1,0:T(8,128)(2,1)}, bf16[2,256,384]{2,1,0:T(8,128)(2,1)S(1)}, u32[]{:S(2)}, u32[]{:S(2)}) collective-permute-start(bf16[2,256,384]{2,1,0:T(8,128)(2,1)} %get-tuple-element.49), channel_id=1, source_target_pairs={{5,0},{6,1},{7,2},{8,3},{9,4},{10,5},{11,6},{12,7},{13,8},{14,9},{... | collective-permute-start | bytes 1179656 | tf_op jit(solution)/shard_map/ppermute | solution.py:42
  13.7 1.4 %copy-done.3 = bf16[1280,640]{1,0:T(8,128)(2,1)S(1)} copy-done((bf16[1280,640]{1,0:T(8,128)(2,1)S(1)}, bf16[1280,640]{1,0:T(8,128)(2,1)}, u32[]{:S(2)}) %copy-start.3) | copy-done | bytes 1638424
  15.1 1.4 %copy-done.5 = bf16[1280,640]{1,0:T(8,128)(2,1)S(1)} copy-done((bf16[1280,640]{1,0:T(8,128)(2,1)S(1)}, bf16[1280,640]{1,0:T(8,128)(2,1)}, u32[]{:S(2)}) %copy-start.5) | copy-done | bytes 1638424
  16.5 7.0 %project.1 = (bf16[512,128]{1,0:T(8,128)(2,1)S(1)}, bf16[512,128]{1,0:T(8,128)(2,1)S(1)}, bf16[512,128]{1,0:T(8,128)(2,1)S(1)}, bf16[512,256]{1,0:T(8,128)(2,1)S...) custom-call(bf16[512,1280]{1,0:T(8,128)(2,1)S(1)} %copy-done.1, ...), custom_call_target="tpu_custom_call" | custom-call | flops 1 | bytes 1 | tf_op jit(solution)/shard_map/project/pallas_call | solution.py:195
  23.6 1.8 %collective-permute-done.1.refs_0_ = bf16[256,1280]{1,0:T(8,128)(2,1)} collective-permute-done((bf16[256,1280]{1,0:T(8,128)(2,1)}, bf16[256,1280]{1,0:T(8,128)(2,1)}, u32[]{:S(2)}, u32[]{:S(2)}) %collective-permute-start.1) | collective-permute-done | bytes 655392 | tf_op jit(solution)/shard_map/ppermute | solution.py:42
  25.3 10.1 %collective-permute-done.2.refs_0_ = bf16[2,256,384]{2,1,0:T(8,128)(2,1)S(1)} collective-permute-done((bf16[2,256,384]{2,1,0:T(8,128)(2,1)}, bf16[2,256,384]{2,1,0:T(8,128)(2,1)S(1)}, u32[]{:S(2)}, u32[]{:S(2)}) %collective-permute-start.2) | collective-permute-done | bytes 393248 | tf_op jit(solution)/shard_map/ppermute | solution.py:42
  35.4 9.6 %collective-permute-done.3.refs_1_ = bf16[2,256,384]{2,1,0:T(8,128)(2,1)S(1)} collective-permute-done((bf16[2,256,384]{2,1,0:T(8,128)(2,1)}, bf16[2,256,384]{2,1,0:T(8,128)(2,1)S(1)}, u32[]{:S(2)}, u32[]{:S(2)}) %collective-permute-start.3) | collective-permute-done | bytes 393248 | tf_op jit(solution)/shard_map/ppermute | solution.py:42
  45.0 7.9 %collective-permute-done.4.refs_2_ = bf16[2,256,384]{2,1,0:T(8,128)(2,1)S(1)} collective-permute-done((bf16[2,256,384]{2,1,0:T(8,128)(2,1)}, bf16[2,256,384]{2,1,0:T(8,128)(2,1)S(1)}, u32[]{:S(2)}, u32[]{:S(2)}) %collective-permute-start.4) | collective-permute-done | bytes 393248 | tf_op jit(solution)/shard_map/ppermute | solution.py:42
  53.3 3.6 %collective-permute-start.7 = (bf16[256,1280]{1,0:T(8,128)(2,1)}, bf16[256,1280]{1,0:T(8,128)(2,1)S(1)}, u32[]{:S(2)}, u32[]{:S(2)}) collective-permute-start(bf16[256,1280]{1,0:T(8,128)(2,1)} %collective-permute-done.1.refs_0_), channel_id=1, source_target_pairs={{16,0},{0,16},{17,1},{1,17},{18,2},{2,18},{19,3},{3,19},{20,4},{4,... | collective-permute-start | bytes 1966088 | tf_op jit(solution)/shard_map/ppermute | solution.py:33
  58.1 1.9 %attend.4.refs_0_ = bf16[512,128]{1,0:T(8,128)(2,1)S(1)} custom-call(s32[1]{0:T(128)S(6)} %copy.16.live_ref, s32[1]{0:T(128)S(6)} %copy.17.depth_ref, bf16[512,128]{1,0:T(8,128)(2,1)S(1)} %get-tuple-element.45.q_ref, bf16[512,128]{1,0:T(8,128)(2,1)S(1)} %get-tuple-element.46.k_ref, bf16[512,128]{1,0:T(8,128)(2,1)S(1)} %get-tuple-element.47.v_ref, ...), custom_call_target="tpu_custom_call" | custom-call | flops 1 | bytes 1 | tf_op jit(solution)/shard_map/attend/pallas_call | solution.py:311
  60.1 1.6 %collective-permute-start.8 = (bf16[2,256,256]{2,1,0:T(8,128)(2,1)S(1)}, bf16[2,256,256]{2,1,0:T(8,128)(2,1)S(1)}, u32[]{:S(2)}, u32[]{:S(2)}) collective-permute-start(bf16[2,256,256]{2,1,0:T(8,128)(2,1)S(1)} %copy-done.13), channel_id=1, source_target_pairs={{9,0},{10,1},{11,2},{12,3},{13,4},{14,5},{15,6},{0,7},{1,8},{2,9},... | collective-permute-start | bytes 786440 | tf_op jit(solution)/shard_map/ppermute | solution.py:42
  61.7 2.1 %collective-permute-start.9 = (bf16[2,256,256]{2,1,0:T(8,128)(2,1)S(1)}, bf16[2,256,256]{2,1,0:T(8,128)(2,1)S(1)}, u32[]{:S(2)}, u32[]{:S(2)}) collective-permute-start(bf16[2,256,256]{2,1,0:T(8,128)(2,1)S(1)} %copy-done.12), channel_id=1, source_target_pairs={{5,0},{6,1},{7,2},{8,3},{9,4},{10,5},{11,6},{12,7},{13,8},{14,9},{... | collective-permute-start | bytes 786440 | tf_op jit(solution)/shard_map/ppermute | solution.py:42
  63.8 11.6 %collective-permute-done.6.refs_1_ = bf16[512,128]{1,0:T(8,128)(2,1)S(1)} collective-permute-done((bf16[512,128]{1,0:T(8,128)(2,1)S(1)}, bf16[512,128]{1,0:T(8,128)(2,1)S(1)}, u32[]{:S(2)}, u32[]{:S(2)}) %collective-permute-start.6) | collective-permute-done | bytes 131104 | tf_op jit(solution)/shard_map/ppermute | solution.py:33
  75.4 3.4 %attend.5.refs_0_ = bf16[512,256]{1,0:T(8,128)(2,1)S(1)} custom-call(s32[1]{0:T(128)S(6)} %copy.16.live_ref, s32[1]{0:T(128)S(6)} %copy.17.depth_ref, bf16[512,256]{1,0:T(8,128)(2,1)S(1)} %get-tuple-element.53.q_ref, bf16[512,256]{1,0:T(8,128)(2,1)S(1)} %get-tuple-element.54.k_ref, bf16[512,256]{1,0:T(8,128)(2,1)S(1)} %get-tuple-element.55.v_ref, ...), custom_call_target="tpu_custom_call" | custom-call | flops 1 | bytes 1 | tf_op jit(solution)/shard_map/attend/pallas_call | solution.py:311
  78.8 1.9 %collective-permute-start.12 = (bf16[512,256]{1,0:T(8,128)(2,1)S(1)}, bf16[512,256]{1,0:T(8,128)(2,1)S(1)}, u32[]{:S(2)}, u32[]{:S(2)}) collective-permute-start(bf16[512,256]{1,0:T(8,128)(2,1)S(1)} %attend.5.refs_0_), channel_id=1, source_target_pairs={{16,0},{0,16},{17,1},{1,17},{18,2},{2,18},{19,3},{3,19},{20,4},{4,... | collective-permute-start | bytes 786440 | tf_op jit(solution)/shard_map/ppermute | solution.py:33
  80.7 5.5 %relay_project.1 = (bf16[2,256,640]{2,1,0:T(8,128)(2,1)}, bf16[2,256,640]{2,1,0:T(8,128)(2,1)}) custom-call(s32[1]{0:T(128)} %bitcast.kv_ref, s32[1]{0:T(128)} %bitcast.1.here_ref, s32[32]{0:T(128)S(1)} %copy-done.6, bf16[256,1280]{1,0:T(8,128)(2,1)} %collective-permute-done.1.refs_0_, bf16[256,1280]{1,0:T(8,128)(2,1)S(1)} %collective-permute-done.7.refs_1_, ...), custom_call_target="tpu_custom_call" | custom-call | flops 1 | bytes 1 | tf_op jit(solution)/shard_map/relay_project/pallas_call | solution.py:228
  92.2 1.9 %collective-permute-start.14 = (bf16[512,128]{1,0:T(8,128)(2,1)S(1)}, bf16[512,128]{1,0:T(8,128)(2,1)S(1)}, u32[]{:S(2)}, u32[]{:S(2)}) collective-permute-start(bf16[512,128]{1,0:T(8,128)(2,1)S(1)} %attend_rest.3.refs_0_), channel_id=1, source_target_pairs={{16,0},{0,16},{17,1},{1,17},{18,2},{2,18},{19,3},{3,19},{20,4},{4,... | collective-permute-start | bytes 393224 | tf_op jit(solution)/shard_map/ppermute | solution.py:33
  94.1 3.0 %collective-permute-done.13.refs_3_ = bf16[512,128]{1,0:T(8,128)(2,1)S(1)} collective-permute-done((bf16[512,128]{1,0:T(8,128)(2,1)S(1)}, bf16[512,128]{1,0:T(8,128)(2,1)S(1)}, u32[]{:S(2)}, u32[]{:S(2)}) %collective-permute-start.13) | collective-permute-done | bytes 131104 | tf_op jit(solution)/shard_map/ppermute | solution.py:33
  97.1 1.6 %add_branch.1.begun = f32[512,1280]{1,0:T(8,128)S(1)} custom-call(f32[512,1280]{1,0:T(8,128)S(1)} %get-tuple-element.61.begun, bf16[640,1280]{1,0:T(8,128)(2,1)S(1)} %copy-done, bf16[640,1280]{1,0:T(8,128)(2,1)S(1)} %collective-permute-done.w_theirs, bf16[512,256]{1,0:T(8,128)(2,1)S(1)} %attend.5.refs_0_, bf16[512,128]{1,0:T(8,128)(2,1)S(1)} %attend_rest.2.refs_1_, ...), custom_call_target="tpu_custom_call" | custom-call | flops 1 | bytes 1 | tf_op jit(solution)/shard_map/add_branch/pallas_call | solution.py:400
  99.2 2.3 %finish.1 = bf16[512,1280]{1,0:T(8,128)(2,1)} custom-call(f32[512,1280]{1,0:T(8,128)S(1)} %get-tuple-element.60.base, bf16[640,1280]{1,0:T(8,128)(2,1)S(1)} %copy-done, bf16[640,1280]{1,0:T(8,128)(2,1)S(1)} %collective-permute-done.w_theirs, f32[1,1280]{1,0:T(1,128)S(1)} %reshape.18.rate, f32[512,1280]{1,0:T(8,128)S(1)} %add_branch.1.begun, ...), custom_call_target="tpu_custom_call" | custom-call | flops 1 | bytes 1 | tf_op jit(solution)/shard_map/finish/pallas_call | solution.py:435
  (49 shorter events, 7.0 us)
Async XLA Ops:
  0.6 52.6 %collective-permute-start = (bf16[640,1280]{1,0:T(8,128)(2,1)}, bf16[640,1280]{1,0:T(8,128)(2,1)S(1)}, u32[]{:S(2)}, u32[]{:S(2)}) collective-permute-start(bf16[640,1280]{1,0:T(8,128)(2,1)} %w_mine.5), channel_id=1, source_target_pairs={{16,0},{0,16},{17,1},{1,17},{18,2},{2,18},{19,3},{3,19},{20,4},{4,... | collective-permute-start | bytes 4915208 | tf_op jit(solution)/shard_map/ppermute | solution.py:33
  4.2 21.1 %collective-permute-start.1 = (bf16[256,1280]{1,0:T(8,128)(2,1)}, bf16[256,1280]{1,0:T(8,128)(2,1)}, u32[]{:S(2)}, u32[]{:S(2)}) collective-permute-start(bf16[256,1280]{1,0:T(8,128)(2,1)} %split_rows.1._), channel_id=1, source_target_pairs={{12,0},{13,1},{14,2},{15,3},{0,4},{1,5},{2,6},{3,7},{4,8},{5,9},{6... | collective-permute-start | bytes 1966088 | tf_op jit(solution)/shard_map/ppermute | solution.py:42
  5.9 7.8 %copy-start.2 = (bf16[1280,640]{1,0:T(8,128)(2,1)S(1)}, bf16[1280,640]{1,0:T(8,128)(2,1)}, u32[]{:S(2)}) copy-start(bf16[1280,640]{1,0:T(8,128)(2,1)} %refs_2_.1) | copy-start | bytes 4915204
  10.0 25.4 %collective-permute-start.2 = (bf16[2,256,384]{2,1,0:T(8,128)(2,1)}, bf16[2,256,384]{2,1,0:T(8,128)(2,1)S(1)}, u32[]{:S(2)}, u32[]{:S(2)}) collective-permute-start(bf16[2,256,384]{2,1,0:T(8,128)(2,1)} %get-tuple-element.48), channel_id=1, source_target_pairs={{9,0},{10,1},{11,2},{12,3},{13,4},{14,5},{15,6},{0,7},{1,8},{2,9},... | collective-permute-start | bytes 1179656 | tf_op jit(solution)/shard_map/ppermute | solution.py:42
  10.1 34.9 %collective-permute-start.3 = (bf16[2,256,384]{2,1,0:T(8,128)(2,1)}, bf16[2,256,384]{2,1,0:T(8,128)(2,1)S(1)}, u32[]{:S(2)}, u32[]{:S(2)}) collective-permute-start(bf16[2,256,384]{2,1,0:T(8,128)(2,1)} %get-tuple-element.49), channel_id=1, source_target_pairs={{5,0},{6,1},{7,2},{8,3},{9,4},{10,5},{11,6},{12,7},{13,8},{14,9},{... | collective-permute-start | bytes 1179656 | tf_op jit(solution)/shard_map/ppermute | solution.py:42
  13.6 39.3 %collective-permute-start.4 = (bf16[2,256,384]{2,1,0:T(8,128)(2,1)}, bf16[2,256,384]{2,1,0:T(8,128)(2,1)S(1)}, u32[]{:S(2)}, u32[]{:S(2)}) collective-permute-start(bf16[2,256,384]{2,1,0:T(8,128)(2,1)} %get-tuple-element.50), channel_id=1, source_target_pairs={{13,0},{14,1},{15,2},{0,3},{1,4},{2,5},{3,6},{4,7},{5,8},{6,9},{7,... | collective-permute-start | bytes 1179656 | tf_op jit(solution)/shard_map/ppermute | solution.py:42
  16.5 8.8 %copy-start.9 = (bf16[2,256,384]{2,1,0:T(8,128)(2,1)S(1)}, bf16[2,256,384]{2,1,0:T(8,128)(2,1)}, u32[]{:S(2)}) copy-start(bf16[2,256,384]{2,1,0:T(8,128)(2,1)} %get-tuple-element.52) | copy-start | bytes 1179652
  23.5 36.6 %copy-start.13 = (bf16[2,256,256]{2,1,0:T(8,128)(2,1)S(1)}, bf16[2,256,256]{2,1,0:T(8,128)(2,1)}, u32[]{:S(2)}) copy-start(bf16[2,256,256]{2,1,0:T(8,128)(2,1)} %get-tuple-element.67) | copy-start | bytes 786436
  23.5 38.2 %copy-start.12 = (bf16[2,256,256]{2,1,0:T(8,128)(2,1)S(1)}, bf16[2,256,256]{2,1,0:T(8,128)(2,1)}, u32[]{:S(2)}) copy-start(bf16[2,256,256]{2,1,0:T(8,128)(2,1)} %get-tuple-element.77) | copy-start | bytes 786436
  23.5 40.3 %copy-start.11 = (bf16[2,256,256]{2,1,0:T(8,128)(2,1)S(1)}, bf16[2,256,256]{2,1,0:T(8,128)(2,1)}, u32[]{:S(2)}) copy-start(bf16[2,256,256]{2,1,0:T(8,128)(2,1)} %get-tuple-element.79) | copy-start | bytes 786436
  23.5 51.8 %copy-start.10 = (bf16[2,256,256]{2,1,0:T(8,128)(2,1)S(1)}, bf16[2,256,256]{2,1,0:T(8,128)(2,1)}, u32[]{:S(2)}) copy-start(bf16[2,256,256]{2,1,0:T(8,128)(2,1)} %get-tuple-element.81) | copy-start | bytes 786436
  25.3 28.0 %collective-permute-start.5 = (bf16[2,256,384]{2,1,0:T(8,128)(2,1)S(1)}, bf16[2,256,384]{2,1,0:T(8,128)(2,1)S(1)}, u32[]{:S(2)}, u32[]{:S(2)}) collective-permute-start(bf16[2,256,384]{2,1,0:T(8,128)(2,1)S(1)} %copy-done.9), channel_id=1, source_target_pairs={{1,0},{2,1},{3,2},{4,3},{5,4},{6,5},{7,6},{8,7},{9,8},{10,9},{11,1... | collective-permute-start | bytes 1179656 | tf_op jit(solution)/shard_map/ppermute | solution.py:42
  53.3 25.5 %collective-permute-start.7 = (bf16[256,1280]{1,0:T(8,128)(2,1)}, bf16[256,1280]{1,0:T(8,128)(2,1)S(1)}, u32[]{:S(2)}, u32[]{:S(2)}) collective-permute-start(bf16[256,1280]{1,0:T(8,128)(2,1)} %collective-permute-done.1.refs_0_), channel_id=1, source_target_pairs={{16,0},{0,16},{17,1},{1,17},{18,2},{2,18},{19,3},{3,19},{20,4},{4,... | collective-permute-start | bytes 1966088 | tf_op jit(solution)/shard_map/ppermute | solution.py:33
  60.0 20.7 %copy-start.7 = (f32[1280]{0:T(1024)S(1)}, f32[1280]{0:T(1024)}, u32[]{:S(2)}) copy-start(f32[1280]{0:T(1024)} %param.19) | copy-start | bytes 15364
  60.0 20.7 %copy-start.4 = (bf16[1280,640]{1,0:T(8,128)(2,1)S(1)}, bf16[1280,640]{1,0:T(8,128)(2,1)}, u32[]{:S(2)}) copy-start(bf16[1280,640]{1,0:T(8,128)(2,1)} %refs_3_.1) | copy-start | bytes 4915204
  60.0 20.7 %copy-start.6 = (s32[32]{0:T(128)S(1)}, s32[32]{0:T(128)}, u32[]{:S(2)}) copy-start(s32[32]{0:T(128)} %placement.1) | copy-start | bytes 388
  60.0 15.3 %collective-permute-start.6 = (bf16[512,128]{1,0:T(8,128)(2,1)S(1)}, bf16[512,128]{1,0:T(8,128)(2,1)S(1)}, u32[]{:S(2)}, u32[]{:S(2)}) collective-permute-start(bf16[512,128]{1,0:T(8,128)(2,1)S(1)} %attend.4.refs_0_), channel_id=1, source_target_pairs={{16,0},{0,16},{17,1},{1,17},{18,2},{2,18},{19,3},{3,19},{20,4},{4,... | collective-permute-start | bytes 393224 | tf_op jit(solution)/shard_map/ppermute | solution.py:33
  60.1 27.3 %collective-permute-start.8 = (bf16[2,256,256]{2,1,0:T(8,128)(2,1)S(1)}, bf16[2,256,256]{2,1,0:T(8,128)(2,1)S(1)}, u32[]{:S(2)}, u32[]{:S(2)}) collective-permute-start(bf16[2,256,256]{2,1,0:T(8,128)(2,1)S(1)} %copy-done.13), channel_id=1, source_target_pairs={{9,0},{10,1},{11,2},{12,3},{13,4},{14,5},{15,6},{0,7},{1,8},{2,9},... | collective-permute-start | bytes 786440 | tf_op jit(solution)/shard_map/ppermute | solution.py:42
  61.7 27.8 %collective-permute-start.9 = (bf16[2,256,256]{2,1,0:T(8,128)(2,1)S(1)}, bf16[2,256,256]{2,1,0:T(8,128)(2,1)S(1)}, u32[]{:S(2)}, u32[]{:S(2)}) collective-permute-start(bf16[2,256,256]{2,1,0:T(8,128)(2,1)S(1)} %copy-done.12), channel_id=1, source_target_pairs={{5,0},{6,1},{7,2},{8,3},{9,4},{10,5},{11,6},{12,7},{13,8},{14,9},{... | collective-permute-start | bytes 786440 | tf_op jit(solution)/shard_map/ppermute | solution.py:42
  63.8 25.7 %collective-permute-start.10 = (bf16[2,256,256]{2,1,0:T(8,128)(2,1)S(1)}, bf16[2,256,256]{2,1,0:T(8,128)(2,1)S(1)}, u32[]{:S(2)}, u32[]{:S(2)}) collective-permute-start(bf16[2,256,256]{2,1,0:T(8,128)(2,1)S(1)} %copy-done.11), channel_id=1, source_target_pairs={{13,0},{14,1},{15,2},{0,3},{1,4},{2,5},{3,6},{4,7},{5,8},{6,9},{7,... | collective-permute-start | bytes 786440 | tf_op jit(solution)/shard_map/ppermute | solution.py:42
  75.4 14.1 %collective-permute-start.11 = (bf16[2,256,256]{2,1,0:T(8,128)(2,1)S(1)}, bf16[2,256,256]{2,1,0:T(8,128)(2,1)S(1)}, u32[]{:S(2)}, u32[]{:S(2)}) collective-permute-start(bf16[2,256,256]{2,1,0:T(8,128)(2,1)S(1)} %copy-done.10), channel_id=1, source_target_pairs={{1,0},{2,1},{3,2},{4,3},{5,4},{6,5},{7,6},{8,7},{9,8},{10,9},{11,1... | collective-permute-start | bytes 786440 | tf_op jit(solution)/shard_map/ppermute | solution.py:42
  78.8 15.3 %collective-permute-start.12 = (bf16[512,256]{1,0:T(8,128)(2,1)S(1)}, bf16[512,256]{1,0:T(8,128)(2,1)S(1)}, u32[]{:S(2)}, u32[]{:S(2)}) collective-permute-start(bf16[512,256]{1,0:T(8,128)(2,1)S(1)} %attend.5.refs_0_), channel_id=1, source_target_pairs={{16,0},{0,16},{17,1},{1,17},{18,2},{2,18},{19,3},{3,19},{20,4},{4,... | collective-permute-start | bytes 786440 | tf_op jit(solution)/shard_map/ppermute | solution.py:33
  90.7 6.4 %collective-permute-start.13 = (bf16[512,128]{1,0:T(8,128)(2,1)S(1)}, bf16[512,128]{1,0:T(8,128)(2,1)S(1)}, u32[]{:S(2)}, u32[]{:S(2)}) collective-permute-start(bf16[512,128]{1,0:T(8,128)(2,1)S(1)} %attend_rest.2.refs_1_), channel_id=1, source_target_pairs={{16,0},{0,16},{17,1},{1,17},{18,2},{2,18},{19,3},{3,19},{20,4},{4,... | collective-permute-start | bytes 393224 | tf_op jit(solution)/shard_map/ppermute | solution.py:33
  92.2 7.1 %collective-permute-start.14 = (bf16[512,128]{1,0:T(8,128)(2,1)S(1)}, bf16[512,128]{1,0:T(8,128)(2,1)S(1)}, u32[]{:S(2)}, u32[]{:S(2)}) collective-permute-start(bf16[512,128]{1,0:T(8,128)(2,1)S(1)} %attend_rest.3.refs_0_), channel_id=1, source_target_pairs={{16,0},{0,16},{17,1},{1,17},{18,2},{2,18},{19,3},{3,19},{20,4},{4,... | collective-permute-start | bytes 393224 | tf_op jit(solution)/shard_map/ppermute | solution.py:33
  (5 other events, 23.9 us)

commit v9 on v7

--- a/solution.py
+++ b/solution.py
@@ -72,32 +72,6 @@
 
 def cost():
     return pl.CostEstimate(flops=1, bytes_accessed=1, transcendentals=0)
-
-
-def split_kernel(kv_ref, hidden, out, sem):
-    part = PAGE // PARTS
-    copies = []
-    for i in range(PARTS):
-        rows = pl.ds(pl.multiple_of(kv_ref[0] * PAGE + i * part, part), part)
-        target = out.at[pl.ds(i * part, part)]
-        copies.append(pltpu.make_async_copy(hidden.at[rows], target, sem.at[i]))
-    for copy in copies:
-        copy.start()
-    for copy in copies:
-        copy.wait()
-
-
-def split_rows(hidden_in, kv_index):
-    return pl.pallas_call(
-        split_kernel,
-        in_specs=[pl.BlockSpec(memory_space=pltpu.SMEM), pl.BlockSpec(memory_space=pltpu.HBM)],
-        out_specs=pl.BlockSpec(memory_space=pltpu.VMEM),
-        out_shape=jax.ShapeDtypeStruct((PAGE, hidden_in.shape[1]), bf16),
-        scratch_shapes=[pltpu.SemaphoreType.DMA((PARTS,))],
-        compiler_params=params(FIRST_LIMIT),
-        cost_estimate=cost(),
-        name="split_rows",
-    )(kv_index, hidden_in)
 
 
 def pack_kernel(slices, devices, offsets, here_ref, table, keys, values, _, *rest):
@@ -472,7 +446,7 @@
     block_offsets = [(2 * b + 1) * devices // (2 * blocks) for b in range(blocks)]
 
     assert blocks == lax.axis_size("kv") == 2
-    relay_send = split_rows(hidden_in, kv_index)
+    relay_send = lax.dynamic_slice_in_dim(hidden_in, lax.axis_index("kv") * PAGE, PAGE, axis=0)
     page_send = pack(
         pool_keys, pool_values, prefix_pages.T, here, devices, page_offsets, relay_send
     )

time: 95.6 us -> 95.4 us (level)
  Pallas kernels: 33.6 us -> 31.3 us
  local copies, waits for them, and re-layouts: 2.92 us -> 4.88 us
    pallas_call x1 -> x0, Pallas kernels: 2.02 us -> none  [split_rows(): pl.pallas_call(split_kernel, in_specs=[pl.BlockSpec(memory_space=pltpu.SM...]
    dynamic_slice x0 -> x1, local copies, waits for them, and re-layouts: none -> 1.96 us  [body(): lax.dynamic_slice_in_dim(hidden_in, lax.axis_index('kv') * PAGE, PAGE, ax...]
  transfers between devices with their start and end apart: 15 -> 15, of which waited for: 10 -> 10; matrix products, arithmetic and copies ran while one was open for 0% -> 2% of each run, Pallas kernels for 32% -> 29%
where the time goes in v9:
time: 95.4 us; the launch traced here: 95.1 us
  waiting for transfers between devices  35.8 us (38%)
  Pallas kernels  31.3 us (33%)
  starting transfers between devices  20.8 us (22%)
  local copies, waits for them, and re-layouts  4.88 us (5%)
  between operations  2.31 us (2%)
    ppermute x9, waiting for transfers between devices, over_blk(): return lax.ppermute(block, ('kv', 'blk'), route)  24 us
    ppermute x6, waiting for transfers between devices, from_behind(): return lax.ppermute(block, axis, route)  11.9 us
    ppermute x6, starting transfers between devices, from_behind(): return lax.ppermute(block, axis, route)  11.2 us
    ppermute x9, starting transfers between devices, over_blk(): return lax.ppermute(block, ('kv', 'blk'), route)  9.63 us
    pallas_call x1, Pallas kernels, project(): pl.pallas_call(functools.partial(project_kernel, slices), out_shape=outs,...  6.94 us
    pallas_call x4, Pallas kernels, attend(): pl.pallas_call(functools.partial(attend_kernel, inner, slots), in_specs=[...  6.44 us
    pallas_call x1, Pallas kernels, relay_project(): pl.pallas_call(functools.partial(relay_kernel, group_slices(width), block...  5.05 us
    pallas_call x1, Pallas kernels, pack(): pl.pallas_call(functools.partial(pack_kernel, slices, devices, offsets),...  4.11 us
  transfers between devices with their start and end apart: 15, of which 10 were waited for; matrix products, arithmetic and copies ran while one was open for 2% of the time, Pallas kernels for 29%

profile of v9, /device:TPU:16, one launch (start us, length us, event | category | flops | bytes accessed | tf_op | source)
XLA Modules:
  0.0 95.1 jit_solution(903114495488319377)
XLA Ops:
  0.6 1.6 %collective-permute-start = (bf16[640,1280]{1,0:T(8,128)(2,1)}, bf16[640,1280]{1,0:T(8,128)(2,1)S(1)}, u32[]{:S(2)}, u32[]{:S(2)}) collective-permute-start(bf16[640,1280]{1,0:T(8,128)(2,1)} %w_mine.5), channel_id=1, source_target_pairs={{16,0},{0,16},{17,1},{1,17},{18,2},{2,18},{19,3},{3,19},{20,4},{4,... | collective-permute-start | bytes 4915208 | tf_op jit(solution)/shard_map/ppermute | solution.py:33
  2.2 2.0 %constant_dynamic-slice_fusion._ = bf16[256,1280]{1,0:T(8,128)(2,1)} fusion(bf16[512,1280]{1,0:T(8,128)(2,1)} %hidden.3, s32[]{:T(128)S(6)} %select_n.3), kind=kLoop, calls=%fused_computation | loop fusion | bytes 1310724 | tf_op jit(solution)/shard_map/dynamic_slice | solution.py:449
  4.2 1.6 %collective-permute-start.1 = (bf16[256,1280]{1,0:T(8,128)(2,1)}, bf16[256,1280]{1,0:T(8,128)(2,1)}, u32[]{:S(2)}, u32[]{:S(2)}) collective-permute-start(bf16[256,1280]{1,0:T(8,128)(2,1)} %constant_dynamic-slice_fusion._), channel_id=1, source_target_pairs={{12,0},{13,1},{14,2},{15,3},{0,4},{1,5},{2,6},{3,7},{4,8},{5,9},{6... | collective-permute-start | bytes 1966088 | tf_op jit(solution)/shard_map/ppermute | solution.py:42
  5.8 4.1 %pack.1 = (bf16[2,256,256]{2,1,0:T(8,128)(2,1)}, bf16[2,256,256]{2,1,0:T(8,128)(2,1)}, bf16[2,256,256]{2,1,0:T(8,128)(2,1)}, bf16[2,256,256]{2,1,0:T(8,128)(2,1)...) custom-call(s32[1]{0:T(128)} %bitcast.1.here_ref, ...), custom_call_target="tpu_custom_call" | custom-call | flops 1 | bytes 1 | tf_op jit(solution)/shard_map/pack/pallas_call | solution.py:104
  10.0 3.5 %collective-permute-start.3 = (bf16[2,256,256]{2,1,0:T(8,128)(2,1)}, bf16[2,256,256]{2,1,0:T(8,128)(2,1)S(1)}, u32[]{:S(2)}, u32[]{:S(2)}) collective-permute-start(bf16[2,256,256]{2,1,0:T(8,128)(2,1)} %get-tuple-element.47), channel_id=1, source_target_pairs={{5,0},{6,1},{7,2},{8,3},{9,4},{10,5},{11,6},{12,7},{13,8},{14,9},{... | collective-permute-start | bytes 786440 | tf_op jit(solution)/shard_map/ppermute | solution.py:42
  16.4 6.9 %project.1 = (bf16[512,256]{1,0:T(8,128)(2,1)S(1)}, bf16[512,256]{1,0:T(8,128)(2,1)S(1)}, bf16[512,256]{1,0:T(8,128)(2,1)S(1)}, bf16[512,128]{1,0:T(8,128)(2,1)S...) custom-call(bf16[512,1280]{1,0:T(8,128)(2,1)S(1)} %copy-done.1, ...), custom_call_target="tpu_custom_call" | custom-call | flops 1 | bytes 1 | tf_op jit(solution)/shard_map/project/pallas_call | solution.py:169
  23.4 1.8 %collective-permute-done.1.refs_0_ = bf16[256,1280]{1,0:T(8,128)(2,1)} collective-permute-done((bf16[256,1280]{1,0:T(8,128)(2,1)}, bf16[256,1280]{1,0:T(8,128)(2,1)}, u32[]{:S(2)}, u32[]{:S(2)}) %collective-permute-start.1) | collective-permute-done | bytes 655392 | tf_op jit(solution)/shard_map/ppermute | solution.py:42
  25.2 5.4 %collective-permute-done.2.refs_0_ = bf16[2,256,256]{2,1,0:T(8,128)(2,1)S(1)} collective-permute-done((bf16[2,256,256]{2,1,0:T(8,128)(2,1)}, bf16[2,256,256]{2,1,0:T(8,128)(2,1)S(1)}, u32[]{:S(2)}, u32[]{:S(2)}) %collective-permute-start.2) | collective-permute-done | bytes 262176 | tf_op jit(solution)/shard_map/ppermute | solution.py:42
  30.6 5.9 %collective-permute-done.3.refs_1_ = bf16[2,256,256]{2,1,0:T(8,128)(2,1)S(1)} collective-permute-done((bf16[2,256,256]{2,1,0:T(8,128)(2,1)}, bf16[2,256,256]{2,1,0:T(8,128)(2,1)S(1)}, u32[]{:S(2)}, u32[]{:S(2)}) %collective-permute-start.3) | collective-permute-done | bytes 262176 | tf_op jit(solution)/shard_map/ppermute | solution.py:42
  36.5 5.1 %collective-permute-done.4.refs_2_ = bf16[2,256,256]{2,1,0:T(8,128)(2,1)S(1)} collective-permute-done((bf16[2,256,256]{2,1,0:T(8,128)(2,1)}, bf16[2,256,256]{2,1,0:T(8,128)(2,1)S(1)}, u32[]{:S(2)}, u32[]{:S(2)}) %collective-permute-start.4) | collective-permute-done | bytes 262176 | tf_op jit(solution)/shard_map/ppermute | solution.py:42
  41.9 3.6 %collective-permute-start.6 = (bf16[256,1280]{1,0:T(8,128)(2,1)}, bf16[256,1280]{1,0:T(8,128)(2,1)S(1)}, u32[]{:S(2)}, u32[]{:S(2)}) collective-permute-start(bf16[256,1280]{1,0:T(8,128)(2,1)} %collective-permute-done.1.refs_0_), channel_id=1, source_target_pairs={{16,0},{0,16},{17,1},{1,17},{18,2},{2,18},{19,3},{3,19},{20,4},{4,... | collective-permute-start | bytes 1966088 | tf_op jit(solution)/shard_map/ppermute | solution.py:33
  45.5 1.5 %collective-permute-start.8 = (bf16[2,256,384]{2,1,0:T(8,128)(2,1)S(1)}, bf16[2,256,384]{2,1,0:T(8,128)(2,1)S(1)}, u32[]{:S(2)}, u32[]{:S(2)}) collective-permute-start(bf16[2,256,384]{2,1,0:T(8,128)(2,1)S(1)} %copy-done.12), channel_id=1, source_target_pairs={{9,0},{10,1},{11,2},{12,3},{13,4},{14,5},{15,6},{0,7},{1,8},{2,9},... | collective-permute-start | bytes 1179656 | tf_op jit(solution)/shard_map/ppermute | solution.py:42
  47.0 2.1 %collective-permute-start.9 = (bf16[2,256,384]{2,1,0:T(8,128)(2,1)S(1)}, bf16[2,256,384]{2,1,0:T(8,128)(2,1)S(1)}, u32[]{:S(2)}, u32[]{:S(2)}) collective-permute-start(bf16[2,256,384]{2,1,0:T(8,128)(2,1)S(1)} %copy-done.11), channel_id=1, source_target_pairs={{5,0},{6,1},{7,2},{8,3},{9,4},{10,5},{11,6},{12,7},{13,8},{14,9},{... | collective-permute-start | bytes 1179656 | tf_op jit(solution)/shard_map/ppermute | solution.py:42
  51.2 3.4 %attend.4.refs_0_ = bf16[512,256]{1,0:T(8,128)(2,1)S(1)} custom-call(s32[1]{0:T(128)S(6)} %copy.16.live_ref, s32[1]{0:T(128)S(6)} %copy.17.depth_ref, bf16[512,256]{1,0:T(8,128)(2,1)S(1)} %get-tuple-element.50.q_ref, bf16[512,256]{1,0:T(8,128)(2,1)S(1)} %get-tuple-element.55.k_ref, bf16[512,256]{1,0:T(8,128)(2,1)S(1)} %get-tuple-element.56.v_ref, ...), custom_call_target="tpu_custom_call" | custom-call | flops 1 | bytes 1 | tf_op jit(solution)/shard_map/attend/pallas_call | solution.py:285
  54.6 6.6 %collective-permute-done.6.refs_1_ = bf16[256,1280]{1,0:T(8,128)(2,1)S(1)} collective-permute-done((bf16[256,1280]{1,0:T(8,128)(2,1)}, bf16[256,1280]{1,0:T(8,128)(2,1)S(1)}, u32[]{:S(2)}, u32[]{:S(2)}) %collective-permute-start.6) | collective-permute-done | bytes 655392 | tf_op jit(solution)/shard_map/ppermute | solution.py:33
  61.2 1.9 %collective-permute-start.7 = (bf16[512,256]{1,0:T(8,128)(2,1)S(1)}, bf16[512,256]{1,0:T(8,128)(2,1)S(1)}, u32[]{:S(2)}, u32[]{:S(2)}) collective-permute-start(bf16[512,256]{1,0:T(8,128)(2,1)S(1)} %attend.4.refs_0_), channel_id=1, source_target_pairs={{16,0},{0,16},{17,1},{1,17},{18,2},{2,18},{19,3},{3,19},{20,4},{4,... | collective-permute-start | bytes 786440 | tf_op jit(solution)/shard_map/ppermute | solution.py:33
  63.1 5.1 %relay_project.1 = (bf16[2,256,640]{2,1,0:T(8,128)(2,1)}, bf16[2,256,640]{2,1,0:T(8,128)(2,1)}) custom-call(s32[1]{0:T(128)} %bitcast.kv_ref, s32[1]{0:T(128)} %bitcast.1.here_ref, s32[32]{0:T(128)S(1)} %copy-done.6, bf16[256,1280]{1,0:T(8,128)(2,1)} %collective-permute-done.1.refs_0_, bf16[256,1280]{1,0:T(8,128)(2,1)S(1)} %collective-permute-done.6.refs_1_, ...), custom_call_target="tpu_custom_call" | custom-call | flops 1 | bytes 1 | tf_op jit(solution)/shard_map/relay_project/pallas_call | solution.py:202
  68.2 1.4 %collective-permute-done.7.refs_1_ = bf16[512,256]{1,0:T(8,128)(2,1)S(1)} collective-permute-done((bf16[512,256]{1,0:T(8,128)(2,1)S(1)}, bf16[512,256]{1,0:T(8,128)(2,1)S(1)}, u32[]{:S(2)}, u32[]{:S(2)}) %collective-permute-start.7) | collective-permute-done | bytes 262176 | tf_op jit(solution)/shard_map/ppermute | solution.py:33
  73.9 5.5 %collective-permute-done.10.refs_1_ = bf16[2,256,384]{2,1,0:T(8,128)(2,1)S(1)} collective-permute-done((bf16[2,256,384]{2,1,0:T(8,128)(2,1)S(1)}, bf16[2,256,384]{2,1,0:T(8,128)(2,1)S(1)}, u32[]{:S(2)}, u32[]{:S(2)}) %collective-permute-start.10) | collective-permute-done | bytes 393248 | tf_op jit(solution)/shard_map/ppermute | solution.py:42
  80.6 2.0 %collective-permute-start.12 = (bf16[512,128]{1,0:T(8,128)(2,1)S(1)}, bf16[512,128]{1,0:T(8,128)(2,1)S(1)}, u32[]{:S(2)}, u32[]{:S(2)}) collective-permute-start(bf16[512,128]{1,0:T(8,128)(2,1)S(1)} %attend_rest.3.refs_0_), channel_id=1, source_target_pairs={{16,0},{0,16},{17,1},{1,17},{18,2},{2,18},{19,3},{3,19},{20,4},{4,... | collective-permute-start | bytes 393224 | tf_op jit(solution)/shard_map/ppermute | solution.py:33
  85.3 2.0 %collective-permute-start.14 = (bf16[512,128]{1,0:T(8,128)(2,1)S(1)}, bf16[512,128]{1,0:T(8,128)(2,1)S(1)}, u32[]{:S(2)}, u32[]{:S(2)}) collective-permute-start(bf16[512,128]{1,0:T(8,128)(2,1)S(1)} %attend_rest.5.refs_0_), channel_id=1, source_target_pairs={{16,0},{0,16},{17,1},{1,17},{18,2},{2,18},{19,3},{3,19},{20,4},{4,... | collective-permute-start | bytes 393224 | tf_op jit(solution)/shard_map/ppermute | solution.py:33
  87.3 3.2 %collective-permute-done.13.refs_3_ = bf16[512,128]{1,0:T(8,128)(2,1)S(1)} collective-permute-done((bf16[512,128]{1,0:T(8,128)(2,1)S(1)}, bf16[512,128]{1,0:T(8,128)(2,1)S(1)}, u32[]{:S(2)}, u32[]{:S(2)}) %collective-permute-start.13) | collective-permute-done | bytes 131104 | tf_op jit(solution)/shard_map/ppermute | solution.py:33
  90.4 1.5 %add_branch.1.begun = f32[512,1280]{1,0:T(8,128)S(1)} custom-call(f32[512,1280]{1,0:T(8,128)S(1)} %get-tuple-element.58.begun, bf16[640,1280]{1,0:T(8,128)(2,1)S(1)} %copy-done, bf16[640,1280]{1,0:T(8,128)(2,1)S(1)} %collective-permute-done.w_theirs, bf16[512,128]{1,0:T(8,128)(2,1)S(1)} %attend_rest.3.refs_0_, bf16[512,128]{1,0:T(8,128)(2,1)S(1)} %attend_rest.4.refs_1_, ...), custom_call_target="tpu_custom_call" | custom-call | flops 1 | bytes 1 | tf_op jit(solution)/shard_map/add_branch/pallas_call | solution.py:374
  92.6 2.3 %finish.1 = bf16[512,1280]{1,0:T(8,128)(2,1)} custom-call(f32[512,1280]{1,0:T(8,128)S(1)} %get-tuple-element.57.base, bf16[640,1280]{1,0:T(8,128)(2,1)S(1)} %copy-done, bf16[640,1280]{1,0:T(8,128)(2,1)S(1)} %collective-permute-done.w_theirs, f32[1,1280]{1,0:T(1,128)S(1)} %reshape.18.rate, f32[512,1280]{1,0:T(8,128)S(1)} %add_branch.1.begun, ...), custom_call_target="tpu_custom_call" | custom-call | flops 1 | bytes 1 | tf_op jit(solution)/shard_map/finish/pallas_call | solution.py:409
  (50 shorter events, 13.0 us)
Async XLA Ops:
  0.6 41.3 %collective-permute-start = (bf16[640,1280]{1,0:T(8,128)(2,1)}, bf16[640,1280]{1,0:T(8,128)(2,1)S(1)}, u32[]{:S(2)}, u32[]{:S(2)}) collective-permute-start(bf16[640,1280]{1,0:T(8,128)(2,1)} %w_mine.5), channel_id=1, source_target_pairs={{16,0},{0,16},{17,1},{1,17},{18,2},{2,18},{19,3},{3,19},{20,4},{4,... | collective-permute-start | bytes 4915208 | tf_op jit(solution)/shard_map/ppermute | solution.py:33
  4.2 21.0 %collective-permute-start.1 = (bf16[256,1280]{1,0:T(8,128)(2,1)}, bf16[256,1280]{1,0:T(8,128)(2,1)}, u32[]{:S(2)}, u32[]{:S(2)}) collective-permute-start(bf16[256,1280]{1,0:T(8,128)(2,1)} %constant_dynamic-slice_fusion._), channel_id=1, source_target_pairs={{12,0},{13,1},{14,2},{15,3},{0,4},{1,5},{2,6},{3,7},{4,8},{5,9},{6... | collective-permute-start | bytes 1966088 | tf_op jit(solution)/shard_map/ppermute | solution.py:42
  5.8 7.8 %copy-start.2 = (bf16[1280,640]{1,0:T(8,128)(2,1)S(1)}, bf16[1280,640]{1,0:T(8,128)(2,1)}, u32[]{:S(2)}) copy-start(bf16[1280,640]{1,0:T(8,128)(2,1)} %refs_2_.1) | copy-start | bytes 4915204
  9.9 20.7 %collective-permute-start.2 = (bf16[2,256,256]{2,1,0:T(8,128)(2,1)}, bf16[2,256,256]{2,1,0:T(8,128)(2,1)S(1)}, u32[]{:S(2)}, u32[]{:S(2)}) collective-permute-start(bf16[2,256,256]{2,1,0:T(8,128)(2,1)} %get-tuple-element.46), channel_id=1, source_target_pairs={{9,0},{10,1},{11,2},{12,3},{13,4},{14,5},{15,6},{0,7},{1,8},{2,9},... | collective-permute-start | bytes 786440 | tf_op jit(solution)/shard_map/ppermute | solution.py:42
  10.0 26.5 %collective-permute-start.3 = (bf16[2,256,256]{2,1,0:T(8,128)(2,1)}, bf16[2,256,256]{2,1,0:T(8,128)(2,1)S(1)}, u32[]{:S(2)}, u32[]{:S(2)}) collective-permute-start(bf16[2,256,256]{2,1,0:T(8,128)(2,1)} %get-tuple-element.47), channel_id=1, source_target_pairs={{5,0},{6,1},{7,2},{8,3},{9,4},{10,5},{11,6},{12,7},{13,8},{14,9},{... | collective-permute-start | bytes 786440 | tf_op jit(solution)/shard_map/ppermute | solution.py:42
  13.5 28.1 %collective-permute-start.4 = (bf16[2,256,256]{2,1,0:T(8,128)(2,1)}, bf16[2,256,256]{2,1,0:T(8,128)(2,1)S(1)}, u32[]{:S(2)}, u32[]{:S(2)}) collective-permute-start(bf16[2,256,256]{2,1,0:T(8,128)(2,1)} %get-tuple-element.48), channel_id=1, source_target_pairs={{13,0},{14,1},{15,2},{0,3},{1,4},{2,5},{3,6},{4,7},{5,8},{6,9},{7,... | collective-permute-start | bytes 786440 | tf_op jit(solution)/shard_map/ppermute | solution.py:42
  16.4 8.8 %copy-start.13 = (bf16[2,256,256]{2,1,0:T(8,128)(2,1)S(1)}, bf16[2,256,256]{2,1,0:T(8,128)(2,1)}, u32[]{:S(2)}) copy-start(bf16[2,256,256]{2,1,0:T(8,128)(2,1)} %get-tuple-element.51) | copy-start | bytes 786436
  16.4 29.1 %copy-start.12 = (bf16[2,256,384]{2,1,0:T(8,128)(2,1)S(1)}, bf16[2,256,384]{2,1,0:T(8,128)(2,1)}, u32[]{:S(2)}) copy-start(bf16[2,256,384]{2,1,0:T(8,128)(2,1)} %get-tuple-element.64) | copy-start | bytes 1179652
  16.4 30.6 %copy-start.11 = (bf16[2,256,384]{2,1,0:T(8,128)(2,1)S(1)}, bf16[2,256,384]{2,1,0:T(8,128)(2,1)}, u32[]{:S(2)}) copy-start(bf16[2,256,384]{2,1,0:T(8,128)(2,1)} %get-tuple-element.79) | copy-start | bytes 1179652
  16.4 32.7 %copy-start.10 = (bf16[2,256,384]{2,1,0:T(8,128)(2,1)S(1)}, bf16[2,256,384]{2,1,0:T(8,128)(2,1)}, u32[]{:S(2)}) copy-start(bf16[2,256,384]{2,1,0:T(8,128)(2,1)} %get-tuple-element.81) | copy-start | bytes 1179652
  16.4 32.7 %copy-start.9 = (bf16[2,256,384]{2,1,0:T(8,128)(2,1)S(1)}, bf16[2,256,384]{2,1,0:T(8,128)(2,1)}, u32[]{:S(2)}) copy-start(bf16[2,256,384]{2,1,0:T(8,128)(2,1)} %get-tuple-element.83) | copy-start | bytes 1179652
  23.4 39.7 %copy-start.7 = (f32[1280]{0:T(1024)S(1)}, f32[1280]{0:T(1024)}, u32[]{:S(2)}) copy-start(f32[1280]{0:T(1024)} %param.19) | copy-start | bytes 15364
  23.4 39.7 %copy-start.4 = (bf16[1280,640]{1,0:T(8,128)(2,1)S(1)}, bf16[1280,640]{1,0:T(8,128)(2,1)}, u32[]{:S(2)}) copy-start(bf16[1280,640]{1,0:T(8,128)(2,1)} %refs_3_.1) | copy-start | bytes 4915204
  23.4 39.7 %copy-start.6 = (s32[32]{0:T(128)S(1)}, s32[32]{0:T(128)}, u32[]{:S(2)}) copy-start(s32[32]{0:T(128)} %placement.1) | copy-start | bytes 388
  25.2 16.7 %collective-permute-start.5 = (bf16[2,256,256]{2,1,0:T(8,128)(2,1)S(1)}, bf16[2,256,256]{2,1,0:T(8,128)(2,1)S(1)}, u32[]{:S(2)}, u32[]{:S(2)}) collective-permute-start(bf16[2,256,256]{2,1,0:T(8,128)(2,1)S(1)} %copy-done.13), channel_id=1, source_target_pairs={{1,0},{2,1},{3,2},{4,3},{5,4},{6,5},{7,6},{8,7},{9,8},{10,9},{11,1... | collective-permute-start | bytes 786440 | tf_op jit(solution)/shard_map/ppermute | solution.py:42
  41.9 19.3 %collective-permute-start.6 = (bf16[256,1280]{1,0:T(8,128)(2,1)}, bf16[256,1280]{1,0:T(8,128)(2,1)S(1)}, u32[]{:S(2)}, u32[]{:S(2)}) collective-permute-start(bf16[256,1280]{1,0:T(8,128)(2,1)} %collective-permute-done.1.refs_0_), channel_id=1, source_target_pairs={{16,0},{0,16},{17,1},{1,17},{18,2},{2,18},{19,3},{3,19},{20,4},{4,... | collective-permute-start | bytes 1966088 | tf_op jit(solution)/shard_map/ppermute | solution.py:33
  45.5 25.3 %collective-permute-start.8 = (bf16[2,256,384]{2,1,0:T(8,128)(2,1)S(1)}, bf16[2,256,384]{2,1,0:T(8,128)(2,1)S(1)}, u32[]{:S(2)}, u32[]{:S(2)}) collective-permute-start(bf16[2,256,384]{2,1,0:T(8,128)(2,1)S(1)} %copy-done.12), channel_id=1, source_target_pairs={{9,0},{10,1},{11,2},{12,3},{13,4},{14,5},{15,6},{0,7},{1,8},{2,9},... | collective-permute-start | bytes 1179656 | tf_op jit(solution)/shard_map/ppermute | solution.py:42
  47.0 26.9 %collective-permute-start.9 = (bf16[2,256,384]{2,1,0:T(8,128)(2,1)S(1)}, bf16[2,256,384]{2,1,0:T(8,128)(2,1)S(1)}, u32[]{:S(2)}, u32[]{:S(2)}) collective-permute-start(bf16[2,256,384]{2,1,0:T(8,128)(2,1)S(1)} %copy-done.11), channel_id=1, source_target_pairs={{5,0},{6,1},{7,2},{8,3},{9,4},{10,5},{11,6},{12,7},{13,8},{14,9},{... | collective-permute-start | bytes 1179656 | tf_op jit(solution)/shard_map/ppermute | solution.py:42
  49.1 30.3 %collective-permute-start.10 = (bf16[2,256,384]{2,1,0:T(8,128)(2,1)S(1)}, bf16[2,256,384]{2,1,0:T(8,128)(2,1)S(1)}, u32[]{:S(2)}, u32[]{:S(2)}) collective-permute-start(bf16[2,256,384]{2,1,0:T(8,128)(2,1)S(1)} %copy-done.10), channel_id=1, source_target_pairs={{13,0},{14,1},{15,2},{0,3},{1,4},{2,5},{3,6},{4,7},{5,8},{6,9},{7,... | collective-permute-start | bytes 1179656 | tf_op jit(solution)/shard_map/ppermute | solution.py:42
  49.1 30.3 %collective-permute-start.11 = (bf16[2,256,384]{2,1,0:T(8,128)(2,1)S(1)}, bf16[2,256,384]{2,1,0:T(8,128)(2,1)S(1)}, u32[]{:S(2)}, u32[]{:S(2)}) collective-permute-start(bf16[2,256,384]{2,1,0:T(8,128)(2,1)S(1)} %copy-done.9), channel_id=1, source_target_pairs={{1,0},{2,1},{3,2},{4,3},{5,4},{6,5},{7,6},{8,7},{9,8},{10,9},{11,1... | collective-permute-start | bytes 1179656 | tf_op jit(solution)/shard_map/ppermute | solution.py:42
  61.2 8.4 %collective-permute-start.7 = (bf16[512,256]{1,0:T(8,128)(2,1)S(1)}, bf16[512,256]{1,0:T(8,128)(2,1)S(1)}, u32[]{:S(2)}, u32[]{:S(2)}) collective-permute-start(bf16[512,256]{1,0:T(8,128)(2,1)S(1)} %attend.4.refs_0_), channel_id=1, source_target_pairs={{16,0},{0,16},{17,1},{1,17},{18,2},{2,18},{19,3},{3,19},{20,4},{4,... | collective-permute-start | bytes 786440 | tf_op jit(solution)/shard_map/ppermute | solution.py:33
  80.6 6.7 %collective-permute-start.12 = (bf16[512,128]{1,0:T(8,128)(2,1)S(1)}, bf16[512,128]{1,0:T(8,128)(2,1)S(1)}, u32[]{:S(2)}, u32[]{:S(2)}) collective-permute-start(bf16[512,128]{1,0:T(8,128)(2,1)S(1)} %attend_rest.3.refs_0_), channel_id=1, source_target_pairs={{16,0},{0,16},{17,1},{1,17},{18,2},{2,18},{19,3},{3,19},{20,4},{4,... | collective-permute-start | bytes 393224 | tf_op jit(solution)/shard_map/ppermute | solution.py:33
  83.9 6.5 %collective-permute-start.13 = (bf16[512,128]{1,0:T(8,128)(2,1)S(1)}, bf16[512,128]{1,0:T(8,128)(2,1)S(1)}, u32[]{:S(2)}, u32[]{:S(2)}) collective-permute-start(bf16[512,128]{1,0:T(8,128)(2,1)S(1)} %attend_rest.4.refs_1_), channel_id=1, source_target_pairs={{16,0},{0,16},{17,1},{1,17},{18,2},{2,18},{19,3},{3,19},{20,4},{4,... | collective-permute-start | bytes 393224 | tf_op jit(solution)/shard_map/ppermute | solution.py:33
  85.3 7.3 %collective-permute-start.14 = (bf16[512,128]{1,0:T(8,128)(2,1)S(1)}, bf16[512,128]{1,0:T(8,128)(2,1)S(1)}, u32[]{:S(2)}, u32[]{:S(2)}) collective-permute-start(bf16[512,128]{1,0:T(8,128)(2,1)S(1)} %attend_rest.5.refs_0_), channel_id=1, source_target_pairs={{16,0},{0,16},{17,1},{1,17},{18,2},{2,18},{19,3},{3,19},{20,4},{4,... | collective-permute-start | bytes 393224 | tf_op jit(solution)/shard_map/ppermute | solution.py:33
  (5 other events, 24.9 us)

commit v10 on v7

--- a/solution.py
+++ b/solution.py
@@ -414,23 +414,27 @@
     out, buf, sem = refs[2 * count :]
     step = buf.shape[1]
     copies = []
-    for i in range(buf.shape[0]):
-        rows = slice(i * step, (i + 1) * step)
-        branch = begun[rows, :] + projected_heads(slices, rows, mine, theirs, w_mine, w_theirs)
-        mean = jnp.mean(branch * branch, axis=-1, keepdims=True)
-        updated = base[rows, :] + rate[...] * (branch * lax.rsqrt(mean + epsilon))
-        scale = lax.rsqrt(jnp.mean(updated * updated, axis=-1, keepdims=True) + epsilon)
-        buf[i] = (updated * scale).astype(bf16)
-        copy = pltpu.make_async_copy(buf.at[i], out.at[pl.ds(i * step, step)], sem.at[i])
-        copy.start()
-        copies.append(copy)
+    for low in range(0, base.shape[0], PAGE):
+        rows = slice(low, low + PAGE)
+        whole = begun[rows, :] + projected_heads(slices, rows, mine, theirs, w_mine, w_theirs)
+        for inner in range(0, PAGE, step):
+            i = (low + inner) // step
+            rows = slice(i * step, (i + 1) * step)
+            branch = whole[inner : inner + step, :]
+            mean = jnp.mean(branch * branch, axis=-1, keepdims=True)
+            updated = base[rows, :] + rate[...] * (branch * lax.rsqrt(mean + epsilon))
+            scale = lax.rsqrt(jnp.mean(updated * updated, axis=-1, keepdims=True) + epsilon)
+            buf[i] = (updated * scale).astype(bf16)
+            copy = pltpu.make_async_copy(buf.at[i], out.at[pl.ds(i * step, step)], sem.at[i])
+            copy.start()
+            copies.append(copy)
     for copy in copies:
         copy.wait()
 
 
 def finish(slices, base, w_mine, w_theirs, rate, begun, mine, theirs):
     tokens, depth = base.shape
-    steps = 4
+    steps = 8
     vmem = pl.BlockSpec(memory_space=pltpu.VMEM)
     return pl.pallas_call(
         functools.partial(finish_kernel, slices),

time: 95.6 us -> 95.6 us (level)
  no operation moved by 1% of the time
where the time goes in v10:
time: 95.6 us; the launch traced here: 95.3 us
  waiting for transfers between devices  35.6 us (37%)
  Pallas kernels  33.6 us (35%)
  starting transfers between devices  20.8 us (22%)
  local copies, waits for them, and re-layouts  2.92 us (3%)
  between operations  2.31 us (2%)
    ppermute x9, waiting for transfers between devices, over_blk(): return lax.ppermute(block, ('kv', 'blk'), route)  23.8 us
    ppermute x6, waiting for transfers between devices, from_behind(): return lax.ppermute(block, axis, route)  11.8 us
    ppermute x6, starting transfers between devices, from_behind(): return lax.ppermute(block, axis, route)  11.1 us
    ppermute x9, starting transfers between devices, over_blk(): return lax.ppermute(block, ('kv', 'blk'), route)  9.66 us
    pallas_call x1, Pallas kernels, project(): pl.pallas_call(functools.partial(project_kernel, slices), out_shape=outs,...  7 us
    pallas_call x4, Pallas kernels, attend(): pl.pallas_call(functools.partial(attend_kernel, inner, slots), in_specs=[...  6.44 us
    pallas_call x1, Pallas kernels, relay_project(): pl.pallas_call(functools.partial(relay_kernel, group_slices(width), block...  5.11 us
    pallas_call x1, Pallas kernels, pack(): pl.pallas_call(functools.partial(pack_kernel, slices, devices, offsets),...  4.17 us
  transfers between devices with their start and end apart: 15, of which 10 were waited for; matrix products, arithmetic and copies ran while one was open for 0% of the time, Pallas kernels for 32%

profile of v10, /device:TPU:16, one launch (start us, length us, event | category | flops | bytes accessed | tf_op | source)
XLA Modules:
  0.0 95.3 jit_solution(8105080657759606166)
XLA Ops:
  0.6 1.6 %collective-permute-start = (bf16[640,1280]{1,0:T(8,128)(2,1)}, bf16[640,1280]{1,0:T(8,128)(2,1)S(1)}, u32[]{:S(2)}, u32[]{:S(2)}) collective-permute-start(bf16[640,1280]{1,0:T(8,128)(2,1)} %w_mine.5), channel_id=1, source_target_pairs={{16,0},{0,16},{17,1},{1,17},{18,2},{2,18},{19,3},{3,19},{20,4},{4,... | collective-permute-start | bytes 4915208 | tf_op jit(solution)/shard_map/ppermute | solution.py:33
  2.2 2.0 %split_rows.1._ = bf16[256,1280]{1,0:T(8,128)(2,1)} custom-call(s32[1]{0:T(128)} %bitcast.kv_ref, bf16[512,1280]{1,0:T(8,128)(2,1)} %hidden.5), custom_call_target="tpu_custom_call" | custom-call | flops 1 | bytes 1 | tf_op jit(solution)/shard_map/split_rows/pallas_call | solution.py:91
  4.2 1.6 %collective-permute-start.1 = (bf16[256,1280]{1,0:T(8,128)(2,1)}, bf16[256,1280]{1,0:T(8,128)(2,1)}, u32[]{:S(2)}, u32[]{:S(2)}) collective-permute-start(bf16[256,1280]{1,0:T(8,128)(2,1)} %split_rows.1._), channel_id=1, source_target_pairs={{12,0},{13,1},{14,2},{15,3},{0,4},{1,5},{2,6},{3,7},{4,8},{5,9},{6... | collective-permute-start | bytes 1966088 | tf_op jit(solution)/shard_map/ppermute | solution.py:42
  5.9 4.2 %pack.1 = (bf16[2,256,256]{2,1,0:T(8,128)(2,1)}, bf16[2,256,256]{2,1,0:T(8,128)(2,1)}, bf16[2,256,256]{2,1,0:T(8,128)(2,1)}, bf16[2,256,256]{2,1,0:T(8,128)(2,1)...) custom-call(s32[1]{0:T(128)} %bitcast.1.here_ref, ...), custom_call_target="tpu_custom_call" | custom-call | flops 1 | bytes 1 | tf_op jit(solution)/shard_map/pack/pallas_call | solution.py:130
  10.2 3.5 %collective-permute-start.3 = (bf16[2,256,256]{2,1,0:T(8,128)(2,1)}, bf16[2,256,256]{2,1,0:T(8,128)(2,1)S(1)}, u32[]{:S(2)}, u32[]{:S(2)}) collective-permute-start(bf16[2,256,256]{2,1,0:T(8,128)(2,1)} %get-tuple-element.47), channel_id=1, source_target_pairs={{5,0},{6,1},{7,2},{8,3},{9,4},{10,5},{11,6},{12,7},{13,8},{14,9},{... | collective-permute-start | bytes 786440 | tf_op jit(solution)/shard_map/ppermute | solution.py:42
  15.2 1.4 %copy-done.5 = bf16[1280,640]{1,0:T(8,128)(2,1)S(1)} copy-done((bf16[1280,640]{1,0:T(8,128)(2,1)S(1)}, bf16[1280,640]{1,0:T(8,128)(2,1)}, u32[]{:S(2)}) %copy-start.5) | copy-done | bytes 1638424
  16.6 7.0 %project.1 = (bf16[512,256]{1,0:T(8,128)(2,1)S(1)}, bf16[512,256]{1,0:T(8,128)(2,1)S(1)}, bf16[512,256]{1,0:T(8,128)(2,1)S(1)}, bf16[512,128]{1,0:T(8,128)(2,1)S...) custom-call(bf16[512,1280]{1,0:T(8,128)(2,1)S(1)} %copy-done.1, ...), custom_call_target="tpu_custom_call" | custom-call | flops 1 | bytes 1 | tf_op jit(solution)/shard_map/project/pallas_call | solution.py:195
  23.6 1.7 %collective-permute-done.1.refs_0_ = bf16[256,1280]{1,0:T(8,128)(2,1)} collective-permute-done((bf16[256,1280]{1,0:T(8,128)(2,1)}, bf16[256,1280]{1,0:T(8,128)(2,1)}, u32[]{:S(2)}, u32[]{:S(2)}) %collective-permute-start.1) | collective-permute-done | bytes 655392 | tf_op jit(solution)/shard_map/ppermute | solution.py:42
  25.3 5.4 %collective-permute-done.2.refs_0_ = bf16[2,256,256]{2,1,0:T(8,128)(2,1)S(1)} collective-permute-done((bf16[2,256,256]{2,1,0:T(8,128)(2,1)}, bf16[2,256,256]{2,1,0:T(8,128)(2,1)S(1)}, u32[]{:S(2)}, u32[]{:S(2)}) %collective-permute-start.2) | collective-permute-done | bytes 262176 | tf_op jit(solution)/shard_map/ppermute | solution.py:42
  30.7 5.9 %collective-permute-done.3.refs_1_ = bf16[2,256,256]{2,1,0:T(8,128)(2,1)S(1)} collective-permute-done((bf16[2,256,256]{2,1,0:T(8,128)(2,1)}, bf16[2,256,256]{2,1,0:T(8,128)(2,1)S(1)}, u32[]{:S(2)}, u32[]{:S(2)}) %collective-permute-start.3) | collective-permute-done | bytes 262176 | tf_op jit(solution)/shard_map/ppermute | solution.py:42
  36.6 5.1 %collective-permute-done.4.refs_2_ = bf16[2,256,256]{2,1,0:T(8,128)(2,1)S(1)} collective-permute-done((bf16[2,256,256]{2,1,0:T(8,128)(2,1)}, bf16[2,256,256]{2,1,0:T(8,128)(2,1)S(1)}, u32[]{:S(2)}, u32[]{:S(2)}) %collective-permute-start.4) | collective-permute-done | bytes 262176 | tf_op jit(solution)/shard_map/ppermute | solution.py:42
  42.0 3.6 %collective-permute-start.6 = (bf16[256,1280]{1,0:T(8,128)(2,1)}, bf16[256,1280]{1,0:T(8,128)(2,1)S(1)}, u32[]{:S(2)}, u32[]{:S(2)}) collective-permute-start(bf16[256,1280]{1,0:T(8,128)(2,1)} %collective-permute-done.1.refs_0_), channel_id=1, source_target_pairs={{16,0},{0,16},{17,1},{1,17},{18,2},{2,18},{19,3},{3,19},{20,4},{4,... | collective-permute-start | bytes 1966088 | tf_op jit(solution)/shard_map/ppermute | solution.py:33
  45.6 1.5 %collective-permute-start.8 = (bf16[2,256,384]{2,1,0:T(8,128)(2,1)S(1)}, bf16[2,256,384]{2,1,0:T(8,128)(2,1)S(1)}, u32[]{:S(2)}, u32[]{:S(2)}) collective-permute-start(bf16[2,256,384]{2,1,0:T(8,128)(2,1)S(1)} %copy-done.12), channel_id=1, source_target_pairs={{9,0},{10,1},{11,2},{12,3},{13,4},{14,5},{15,6},{0,7},{1,8},{2,9},... | collective-permute-start | bytes 1179656 | tf_op jit(solution)/shard_map/ppermute | solution.py:42
  47.1 2.1 %collective-permute-start.9 = (bf16[2,256,384]{2,1,0:T(8,128)(2,1)S(1)}, bf16[2,256,384]{2,1,0:T(8,128)(2,1)S(1)}, u32[]{:S(2)}, u32[]{:S(2)}) collective-permute-start(bf16[2,256,384]{2,1,0:T(8,128)(2,1)S(1)} %copy-done.11), channel_id=1, source_target_pairs={{5,0},{6,1},{7,2},{8,3},{9,4},{10,5},{11,6},{12,7},{13,8},{14,9},{... | collective-permute-start | bytes 1179656 | tf_op jit(solution)/shard_map/ppermute | solution.py:42
  51.3 3.4 %attend.4.refs_0_ = bf16[512,256]{1,0:T(8,128)(2,1)S(1)} custom-call(s32[1]{0:T(128)S(6)} %copy.16.live_ref, s32[1]{0:T(128)S(6)} %copy.17.depth_ref, bf16[512,256]{1,0:T(8,128)(2,1)S(1)} %get-tuple-element.50.q_ref, bf16[512,256]{1,0:T(8,128)(2,1)S(1)} %get-tuple-element.55.k_ref, bf16[512,256]{1,0:T(8,128)(2,1)S(1)} %get-tuple-element.56.v_ref, ...), custom_call_target="tpu_custom_call" | custom-call | flops 1 | bytes 1 | tf_op jit(solution)/shard_map/attend/pallas_call | solution.py:311
  54.7 6.7 %collective-permute-done.6.refs_1_ = bf16[256,1280]{1,0:T(8,128)(2,1)S(1)} collective-permute-done((bf16[256,1280]{1,0:T(8,128)(2,1)}, bf16[256,1280]{1,0:T(8,128)(2,1)S(1)}, u32[]{:S(2)}, u32[]{:S(2)}) %collective-permute-start.6) | collective-permute-done | bytes 655392 | tf_op jit(solution)/shard_map/ppermute | solution.py:33
  61.3 1.8 %collective-permute-start.7 = (bf16[512,256]{1,0:T(8,128)(2,1)S(1)}, bf16[512,256]{1,0:T(8,128)(2,1)S(1)}, u32[]{:S(2)}, u32[]{:S(2)}) collective-permute-start(bf16[512,256]{1,0:T(8,128)(2,1)S(1)} %attend.4.refs_0_), channel_id=1, source_target_pairs={{16,0},{0,16},{17,1},{1,17},{18,2},{2,18},{19,3},{3,19},{20,4},{4,... | collective-permute-start | bytes 786440 | tf_op jit(solution)/shard_map/ppermute | solution.py:33
  63.2 5.1 %relay_project.1 = (bf16[2,256,640]{2,1,0:T(8,128)(2,1)}, bf16[2,256,640]{2,1,0:T(8,128)(2,1)}) custom-call(s32[1]{0:T(128)} %bitcast.kv_ref, s32[1]{0:T(128)} %bitcast.1.here_ref, s32[32]{0:T(128)S(1)} %copy-done.6, bf16[256,1280]{1,0:T(8,128)(2,1)} %collective-permute-done.1.refs_0_, bf16[256,1280]{1,0:T(8,128)(2,1)S(1)} %collective-permute-done.6.refs_1_, ...), custom_call_target="tpu_custom_call" | custom-call | flops 1 | bytes 1 | tf_op jit(solution)/shard_map/relay_project/pallas_call | solution.py:228
  74.1 5.4 %collective-permute-done.10.refs_1_ = bf16[2,256,384]{2,1,0:T(8,128)(2,1)S(1)} collective-permute-done((bf16[2,256,384]{2,1,0:T(8,128)(2,1)S(1)}, bf16[2,256,384]{2,1,0:T(8,128)(2,1)S(1)}, u32[]{:S(2)}, u32[]{:S(2)}) %collective-permute-start.10) | collective-permute-done | bytes 393248 | tf_op jit(solution)/shard_map/ppermute | solution.py:42
  80.7 2.0 %collective-permute-start.12 = (bf16[512,128]{1,0:T(8,128)(2,1)S(1)}, bf16[512,128]{1,0:T(8,128)(2,1)S(1)}, u32[]{:S(2)}, u32[]{:S(2)}) collective-permute-start(bf16[512,128]{1,0:T(8,128)(2,1)S(1)} %attend_rest.3.refs_0_), channel_id=1, source_target_pairs={{16,0},{0,16},{17,1},{1,17},{18,2},{2,18},{19,3},{3,19},{20,4},{4,... | collective-permute-start | bytes 393224 | tf_op jit(solution)/shard_map/ppermute | solution.py:33
  85.4 2.0 %collective-permute-start.14 = (bf16[512,128]{1,0:T(8,128)(2,1)S(1)}, bf16[512,128]{1,0:T(8,128)(2,1)S(1)}, u32[]{:S(2)}, u32[]{:S(2)}) collective-permute-start(bf16[512,128]{1,0:T(8,128)(2,1)S(1)} %attend_rest.5.refs_0_), channel_id=1, source_target_pairs={{16,0},{0,16},{17,1},{1,17},{18,2},{2,18},{19,3},{3,19},{20,4},{4,... | collective-permute-start | bytes 393224 | tf_op jit(solution)/shard_map/ppermute | solution.py:33
  87.4 3.2 %collective-permute-done.13.refs_3_ = bf16[512,128]{1,0:T(8,128)(2,1)S(1)} collective-permute-done((bf16[512,128]{1,0:T(8,128)(2,1)S(1)}, bf16[512,128]{1,0:T(8,128)(2,1)S(1)}, u32[]{:S(2)}, u32[]{:S(2)}) %collective-permute-start.13) | collective-permute-done | bytes 131104 | tf_op jit(solution)/shard_map/ppermute | solution.py:33
  90.6 1.6 %add_branch.1.begun = f32[512,1280]{1,0:T(8,128)S(1)} custom-call(f32[512,1280]{1,0:T(8,128)S(1)} %get-tuple-element.58.begun, bf16[640,1280]{1,0:T(8,128)(2,1)S(1)} %copy-done, bf16[640,1280]{1,0:T(8,128)(2,1)S(1)} %collective-permute-done.w_theirs, bf16[512,128]{1,0:T(8,128)(2,1)S(1)} %attend_rest.3.refs_0_, bf16[512,128]{1,0:T(8,128)(2,1)S(1)} %attend_rest.4.refs_1_, ...), custom_call_target="tpu_custom_call" | custom-call | flops 1 | bytes 1 | tf_op jit(solution)/shard_map/add_branch/pallas_call | solution.py:400
  92.8 2.4 %finish.1 = bf16[512,1280]{1,0:T(8,128)(2,1)} custom-call(f32[512,1280]{1,0:T(8,128)S(1)} %get-tuple-element.57.base, bf16[640,1280]{1,0:T(8,128)(2,1)S(1)} %copy-done, bf16[640,1280]{1,0:T(8,128)(2,1)S(1)} %collective-permute-done.w_theirs, f32[1,1280]{1,0:T(1,128)S(1)} %reshape.18.rate, f32[512,1280]{1,0:T(8,128)S(1)} %add_branch.1.begun, ...), custom_call_target="tpu_custom_call" | custom-call | flops 1 | bytes 1 | tf_op jit(solution)/shard_map/finish/pallas_call | solution.py:439
  (50 shorter events, 12.9 us)
Async XLA Ops:
  0.6 41.4 %collective-permute-start = (bf16[640,1280]{1,0:T(8,128)(2,1)}, bf16[640,1280]{1,0:T(8,128)(2,1)S(1)}, u32[]{:S(2)}, u32[]{:S(2)}) collective-permute-start(bf16[640,1280]{1,0:T(8,128)(2,1)} %w_mine.5), channel_id=1, source_target_pairs={{16,0},{0,16},{17,1},{1,17},{18,2},{2,18},{19,3},{3,19},{20,4},{4,... | collective-permute-start | bytes 4915208 | tf_op jit(solution)/shard_map/ppermute | solution.py:33
  4.2 21.1 %collective-permute-start.1 = (bf16[256,1280]{1,0:T(8,128)(2,1)}, bf16[256,1280]{1,0:T(8,128)(2,1)}, u32[]{:S(2)}, u32[]{:S(2)}) collective-permute-start(bf16[256,1280]{1,0:T(8,128)(2,1)} %split_rows.1._), channel_id=1, source_target_pairs={{12,0},{13,1},{14,2},{15,3},{0,4},{1,5},{2,6},{3,7},{4,8},{5,9},{6... | collective-permute-start | bytes 1966088 | tf_op jit(solution)/shard_map/ppermute | solution.py:42
  5.9 7.8 %copy-start.2 = (bf16[1280,640]{1,0:T(8,128)(2,1)S(1)}, bf16[1280,640]{1,0:T(8,128)(2,1)}, u32[]{:S(2)}) copy-start(bf16[1280,640]{1,0:T(8,128)(2,1)} %refs_2_.1) | copy-start | bytes 4915204
  10.1 20.7 %collective-permute-start.2 = (bf16[2,256,256]{2,1,0:T(8,128)(2,1)}, bf16[2,256,256]{2,1,0:T(8,128)(2,1)S(1)}, u32[]{:S(2)}, u32[]{:S(2)}) collective-permute-start(bf16[2,256,256]{2,1,0:T(8,128)(2,1)} %get-tuple-element.46), channel_id=1, source_target_pairs={{9,0},{10,1},{11,2},{12,3},{13,4},{14,5},{15,6},{0,7},{1,8},{2,9},... | collective-permute-start | bytes 786440 | tf_op jit(solution)/shard_map/ppermute | solution.py:42
  10.2 26.5 %collective-permute-start.3 = (bf16[2,256,256]{2,1,0:T(8,128)(2,1)}, bf16[2,256,256]{2,1,0:T(8,128)(2,1)S(1)}, u32[]{:S(2)}, u32[]{:S(2)}) collective-permute-start(bf16[2,256,256]{2,1,0:T(8,128)(2,1)} %get-tuple-element.47), channel_id=1, source_target_pairs={{5,0},{6,1},{7,2},{8,3},{9,4},{10,5},{11,6},{12,7},{13,8},{14,9},{... | collective-permute-start | bytes 786440 | tf_op jit(solution)/shard_map/ppermute | solution.py:42
  13.7 28.0 %collective-permute-start.4 = (bf16[2,256,256]{2,1,0:T(8,128)(2,1)}, bf16[2,256,256]{2,1,0:T(8,128)(2,1)S(1)}, u32[]{:S(2)}, u32[]{:S(2)}) collective-permute-start(bf16[2,256,256]{2,1,0:T(8,128)(2,1)} %get-tuple-element.48), channel_id=1, source_target_pairs={{13,0},{14,1},{15,2},{0,3},{1,4},{2,5},{3,6},{4,7},{5,8},{6,9},{7,... | collective-permute-start | bytes 786440 | tf_op jit(solution)/shard_map/ppermute | solution.py:42
  16.6 8.7 %copy-start.13 = (bf16[2,256,256]{2,1,0:T(8,128)(2,1)S(1)}, bf16[2,256,256]{2,1,0:T(8,128)(2,1)}, u32[]{:S(2)}) copy-start(bf16[2,256,256]{2,1,0:T(8,128)(2,1)} %get-tuple-element.51) | copy-start | bytes 786436
  16.6 29.0 %copy-start.12 = (bf16[2,256,384]{2,1,0:T(8,128)(2,1)S(1)}, bf16[2,256,384]{2,1,0:T(8,128)(2,1)}, u32[]{:S(2)}) copy-start(bf16[2,256,384]{2,1,0:T(8,128)(2,1)} %get-tuple-element.64) | copy-start | bytes 1179652
  16.6 30.5 %copy-start.11 = (bf16[2,256,384]{2,1,0:T(8,128)(2,1)S(1)}, bf16[2,256,384]{2,1,0:T(8,128)(2,1)}, u32[]{:S(2)}) copy-start(bf16[2,256,384]{2,1,0:T(8,128)(2,1)} %get-tuple-element.79) | copy-start | bytes 1179652
  16.6 32.6 %copy-start.10 = (bf16[2,256,384]{2,1,0:T(8,128)(2,1)S(1)}, bf16[2,256,384]{2,1,0:T(8,128)(2,1)}, u32[]{:S(2)}) copy-start(bf16[2,256,384]{2,1,0:T(8,128)(2,1)} %get-tuple-element.81) | copy-start | bytes 1179652
  16.6 32.6 %copy-start.9 = (bf16[2,256,384]{2,1,0:T(8,128)(2,1)S(1)}, bf16[2,256,384]{2,1,0:T(8,128)(2,1)}, u32[]{:S(2)}) copy-start(bf16[2,256,384]{2,1,0:T(8,128)(2,1)} %get-tuple-element.83) | copy-start | bytes 1179652
  23.6 39.6 %copy-start.7 = (f32[1280]{0:T(1024)S(1)}, f32[1280]{0:T(1024)}, u32[]{:S(2)}) copy-start(f32[1280]{0:T(1024)} %param.19) | copy-start | bytes 15364
  23.6 39.6 %copy-start.4 = (bf16[1280,640]{1,0:T(8,128)(2,1)S(1)}, bf16[1280,640]{1,0:T(8,128)(2,1)}, u32[]{:S(2)}) copy-start(bf16[1280,640]{1,0:T(8,128)(2,1)} %refs_3_.1) | copy-start | bytes 4915204
  23.6 39.6 %copy-start.6 = (s32[32]{0:T(128)S(1)}, s32[32]{0:T(128)}, u32[]{:S(2)}) copy-start(s32[32]{0:T(128)} %placement.1) | copy-start | bytes 388
  25.3 16.7 %collective-permute-start.5 = (bf16[2,256,256]{2,1,0:T(8,128)(2,1)S(1)}, bf16[2,256,256]{2,1,0:T(8,128)(2,1)S(1)}, u32[]{:S(2)}, u32[]{:S(2)}) collective-permute-start(bf16[2,256,256]{2,1,0:T(8,128)(2,1)S(1)} %copy-done.13), channel_id=1, source_target_pairs={{1,0},{2,1},{3,2},{4,3},{5,4},{6,5},{7,6},{8,7},{9,8},{10,9},{11,1... | collective-permute-start | bytes 786440 | tf_op jit(solution)/shard_map/ppermute | solution.py:42
  42.0 19.3 %collective-permute-start.6 = (bf16[256,1280]{1,0:T(8,128)(2,1)}, bf16[256,1280]{1,0:T(8,128)(2,1)S(1)}, u32[]{:S(2)}, u32[]{:S(2)}) collective-permute-start(bf16[256,1280]{1,0:T(8,128)(2,1)} %collective-permute-done.1.refs_0_), channel_id=1, source_target_pairs={{16,0},{0,16},{17,1},{1,17},{18,2},{2,18},{19,3},{3,19},{20,4},{4,... | collective-permute-start | bytes 1966088 | tf_op jit(solution)/shard_map/ppermute | solution.py:33
  45.6 25.3 %collective-permute-start.8 = (bf16[2,256,384]{2,1,0:T(8,128)(2,1)S(1)}, bf16[2,256,384]{2,1,0:T(8,128)(2,1)S(1)}, u32[]{:S(2)}, u32[]{:S(2)}) collective-permute-start(bf16[2,256,384]{2,1,0:T(8,128)(2,1)S(1)} %copy-done.12), channel_id=1, source_target_pairs={{9,0},{10,1},{11,2},{12,3},{13,4},{14,5},{15,6},{0,7},{1,8},{2,9},... | collective-permute-start | bytes 1179656 | tf_op jit(solution)/shard_map/ppermute | solution.py:42
  47.1 26.9 %collective-permute-start.9 = (bf16[2,256,384]{2,1,0:T(8,128)(2,1)S(1)}, bf16[2,256,384]{2,1,0:T(8,128)(2,1)S(1)}, u32[]{:S(2)}, u32[]{:S(2)}) collective-permute-start(bf16[2,256,384]{2,1,0:T(8,128)(2,1)S(1)} %copy-done.11), channel_id=1, source_target_pairs={{5,0},{6,1},{7,2},{8,3},{9,4},{10,5},{11,6},{12,7},{13,8},{14,9},{... | collective-permute-start | bytes 1179656 | tf_op jit(solution)/shard_map/ppermute | solution.py:42
  49.2 30.3 %collective-permute-start.10 = (bf16[2,256,384]{2,1,0:T(8,128)(2,1)S(1)}, bf16[2,256,384]{2,1,0:T(8,128)(2,1)S(1)}, u32[]{:S(2)}, u32[]{:S(2)}) collective-permute-start(bf16[2,256,384]{2,1,0:T(8,128)(2,1)S(1)} %copy-done.10), channel_id=1, source_target_pairs={{13,0},{14,1},{15,2},{0,3},{1,4},{2,5},{3,6},{4,7},{5,8},{6,9},{7,... | collective-permute-start | bytes 1179656 | tf_op jit(solution)/shard_map/ppermute | solution.py:42
  49.2 30.3 %collective-permute-start.11 = (bf16[2,256,384]{2,1,0:T(8,128)(2,1)S(1)}, bf16[2,256,384]{2,1,0:T(8,128)(2,1)S(1)}, u32[]{:S(2)}, u32[]{:S(2)}) collective-permute-start(bf16[2,256,384]{2,1,0:T(8,128)(2,1)S(1)} %copy-done.9), channel_id=1, source_target_pairs={{1,0},{2,1},{3,2},{4,3},{5,4},{6,5},{7,6},{8,7},{9,8},{10,9},{11,1... | collective-permute-start | bytes 1179656 | tf_op jit(solution)/shard_map/ppermute | solution.py:42
  61.3 8.4 %collective-permute-start.7 = (bf16[512,256]{1,0:T(8,128)(2,1)S(1)}, bf16[512,256]{1,0:T(8,128)(2,1)S(1)}, u32[]{:S(2)}, u32[]{:S(2)}) collective-permute-start(bf16[512,256]{1,0:T(8,128)(2,1)S(1)} %attend.4.refs_0_), channel_id=1, source_target_pairs={{16,0},{0,16},{17,1},{1,17},{18,2},{2,18},{19,3},{3,19},{20,4},{4,... | collective-permute-start | bytes 786440 | tf_op jit(solution)/shard_map/ppermute | solution.py:33
  80.7 6.7 %collective-permute-start.12 = (bf16[512,128]{1,0:T(8,128)(2,1)S(1)}, bf16[512,128]{1,0:T(8,128)(2,1)S(1)}, u32[]{:S(2)}, u32[]{:S(2)}) collective-permute-start(bf16[512,128]{1,0:T(8,128)(2,1)S(1)} %attend_rest.3.refs_0_), channel_id=1, source_target_pairs={{16,0},{0,16},{17,1},{1,17},{18,2},{2,18},{19,3},{3,19},{20,4},{4,... | collective-permute-start | bytes 393224 | tf_op jit(solution)/shard_map/ppermute | solution.py:33
  84.1 6.5 %collective-permute-start.13 = (bf16[512,128]{1,0:T(8,128)(2,1)S(1)}, bf16[512,128]{1,0:T(8,128)(2,1)S(1)}, u32[]{:S(2)}, u32[]{:S(2)}) collective-permute-start(bf16[512,128]{1,0:T(8,128)(2,1)S(1)} %attend_rest.4.refs_1_), channel_id=1, source_target_pairs={{16,0},{0,16},{17,1},{1,17},{18,2},{2,18},{19,3},{3,19},{20,4},{4,... | collective-permute-start | bytes 393224 | tf_op jit(solution)/shard_map/ppermute | solution.py:33
  85.4 7.3 %collective-permute-start.14 = (bf16[512,128]{1,0:T(8,128)(2,1)S(1)}, bf16[512,128]{1,0:T(8,128)(2,1)S(1)}, u32[]{:S(2)}, u32[]{:S(2)}) collective-permute-start(bf16[512,128]{1,0:T(8,128)(2,1)S(1)} %attend_rest.5.refs_0_), channel_id=1, source_target_pairs={{16,0},{0,16},{17,1},{1,17},{18,2},{2,18},{19,3},{3,19},{20,4},{4,... | collective-permute-start | bytes 393224 | tf_op jit(solution)/shard_map/ppermute | solution.py:33
  (5 other events, 25.0 us)
